TPU v7x, 32 devices: a whole 2x2x4 slice. The times are simulated.
32 devices in a mesh: tensor: 2 (over y), context: 16 (over z, x, core).
Axes of the slice: x: 2, y: 2, z: 4, core: 2. Of those that a mesh axis runs over, the one named last changes fastest.
Arguments:
- inputs: bfloat16 [2, 1024, 2560], P(None, 'context'), may hold values from -6 to 6
- valid: int32 [2, 1024], P(None, 'context'), may hold values from 0 to 1, as said below
- out_grad: bfloat16 [2, 1024, 2560], P(None, 'context'), may hold values from -6 to 6
- teacher: bfloat16 [2, 1024, 2560], P(None, 'context'), may hold values from -6 to 6
- norm_attn: bfloat16 [2560], P('context'), may hold values from 0.5 to 1.5
- w_query: bfloat16 [2560, 2560], P('context', 'tensor'), may hold values from -0.125 to 0.125
- key_matrix: bfloat16 [2560, 640], P('context', 'tensor'), may hold values from -0.125 to 0.125
- value_matrix: bfloat16 [2560, 640], P('context', 'tensor'), may hold values from -0.125 to 0.125
- w_out: bfloat16 [2560, 2560], P('tensor', 'context'), may hold values from -2 to 2
- norm_mlp: bfloat16 [2560], P('context'), may hold values from 0.5 to 1.5
- w_gate: bfloat16 [2560, 6912], P('context', 'tensor'), may hold values from -0.125 to 0.125
- w_up: bfloat16 [2560, 6912], P('context', 'tensor'), may hold values from -0.125 to 0.125
- w_down: bfloat16 [6912, 2560], P('tensor', 'context'), may hold values from -0.078125 to 0.078125
Outputs:
- output: bfloat16 [2, 1024, 2560], P(None, 'context')
- loss: float32 [], replicated
- input_grad: float32 [2, 1024, 2560], P(None, 'context')
- grad_norm_attn: float32 [2560], P('context')
- grad_norm_mlp: float32 [2560], P('context')
- grad_query: float32 [2560, 2560], P('context', 'tensor')
- grad_key: float32 [2560, 640], P('context', 'tensor')
- grad_value: float32 [2560, 640], P('context', 'tensor')
- grad_out: float32 [2560, 2560], P('tensor', 'context')
- grad_gate: float32 [2560, 6912], P('context', 'tensor')
- grad_up: float32 [2560, 6912], P('context', 'tensor')
- grad_down: float32 [6912, 2560], P('tensor', 'context')
Inputs may be any that keep to these rules, and one draw needn't show every extreme that they name: `valid`: each row is a run of ones followed by zeros, with 256 ones or more; some row is all ones.
All inputs are finite; a program needn't handle non-finite values.
Results may differ from a plain program's by a relative error of at most 0.012.
The roundings to bfloat16 on the way count: a program that leaves them out, or rounds other values in their place, can miss the bound.
Values may be sent and summed in bfloat16 or wider, within the bound.
No kernel may reach another device: no remote copies, remote signals or barrier semaphores. Data moves between devices by JAX's collectives and lax.ppermute only.
A program may use at most 256 MiB of HBM per device.

v0:
```python
import math

import jax
import jax.numpy as jnp
from jax import lax
from jax.sharding import PartitionSpec as P

HEAD_SIZE = 80
BLOCK = 256


eps = 1e-05
theta = 10000.0


def rms_forward(value_rows, gain):
    inverse = lax.rsqrt(jnp.mean(value_rows * value_rows, axis=-1, keepdims=True) + eps)
    normed = value_rows * inverse
    return (normed, inverse, normed * gain)


def rms_backward(grad, normed, inverse, gain):
    scaled = grad * gain
    return inverse * (scaled - normed * jnp.mean(scaled * normed, axis=-1, keepdims=True))


def rotate(value_rows, cosine, sine):
    half = value_rows.shape[-1] // 2
    first, second = (value_rows[..., :half], value_rows[..., half:])
    return jnp.concatenate(
        [first * cosine - second * sine, second * cosine + first * sine], axis=-1
    )


def rotate_back(grad, cosine, sine):
    half = grad.shape[-1] // 2
    first, second = (grad[..., :half], grad[..., half:])
    return jnp.concatenate(
        [first * cosine + second * sine, second * cosine - first * sine], axis=-1
    )


def allowed_pairs(key_ok, qpos, seq_len):
    kpos = jnp.arange(seq_len, dtype=jnp.int32)
    return (kpos[None, :] // BLOCK <= qpos[:, None] // BLOCK) & (key_ok[None, :] > 0)


def masked_scores(query_rows, key_rows, key_ok, qpos, scale):
    raw = (
        jnp.einsum("qkgd,jkd->kgqj", query_rows, key_rows, preferred_element_type=jnp.float32)
        * scale
    )
    allowed = allowed_pairs(key_ok, qpos, key_rows.shape[0])
    return jnp.where(allowed, raw, jnp.float32(-1e30))


def dot_left(left, right):
    return lax.dot_general(
        left, right, (((0,), (0,)), ((), ())), preferred_element_type=jnp.float32
    )


def dot_right(left, right):
    return lax.dot_general(
        left, right, (((1,), (1,)), ((), ())), preferred_element_type=jnp.float32
    )


def shards(
    inputs,
    valid,
    out_grad,
    teacher,
    norm_attn,
    w_query,
    key_matrix,
    value_matrix,
    w_out,
    norm_mlp,
    w_gate,
    w_up,
    w_down,
):
    seqs, seg, width = inputs.shape
    ctx_size = lax.axis_size("context")
    index = lax.axis_index("context")
    scale = HEAD_SIZE ** (-0.5)
    half = HEAD_SIZE // 2
    gathered = (
        lax.all_gather(norm_attn, "context", axis=0, tiled=True),
        lax.all_gather(w_query, "context", axis=0, tiled=True),
        lax.all_gather(key_matrix, "context", axis=0, tiled=True),
        lax.all_gather(value_matrix, "context", axis=0, tiled=True),
        lax.all_gather(w_out, "context", axis=1, tiled=True),
        lax.all_gather(norm_mlp, "context", axis=0, tiled=True),
        lax.all_gather(w_gate, "context", axis=0, tiled=True),
        lax.all_gather(w_up, "context", axis=0, tiled=True),
        lax.all_gather(w_down, "context", axis=1, tiled=True),
    )
    gain_first, wq, wk, wv, wo, gain_second, wg, wu, wd = gathered
    gain1 = gain_first.astype(jnp.float32)
    gain2 = gain_second.astype(jnp.float32)
    heads_q = wq.shape[1] // HEAD_SIZE
    heads_kv = wk.shape[1] // HEAD_SIZE
    head_group = heads_q // heads_kv
    row_count = seqs * seg
    positions = index * seg + jnp.arange(seg, dtype=jnp.int32)
    freqs = jnp.exp(-math.log(theta) * jnp.arange(half, dtype=jnp.float32) / half)
    angles = positions.astype(jnp.float32)[:, None] * freqs[None, :]
    cosine = jnp.cos(angles)[:, None, :]
    sine = jnp.sin(angles)[:, None, :]
    x = inputs.astype(jnp.float32)
    normed1, inverse1, pre1 = rms_forward(x, gain1)
    h1 = pre1.astype(jnp.bfloat16).reshape(row_count, width)
    query_before_rotary = jnp.dot(h1, wq, preferred_element_type=jnp.float32).reshape(
        seqs, seg, heads_q, HEAD_SIZE
    )
    key_before_rotary = jnp.dot(h1, wk, preferred_element_type=jnp.float32).reshape(
        seqs, seg, heads_kv, HEAD_SIZE
    )
    value_own = (
        jnp.dot(h1, wv, preferred_element_type=jnp.float32)
        .astype(jnp.bfloat16)
        .reshape(seqs, seg, heads_kv * HEAD_SIZE)
    )
    query_rows = (
        rotate(query_before_rotary, cosine, sine)
        .astype(jnp.bfloat16)
        .reshape(seqs, seg, heads_kv, head_group, HEAD_SIZE)
    )
    key_own = (
        rotate(key_before_rotary, cosine, sine)
        .astype(jnp.bfloat16)
        .reshape(seqs, seg, heads_kv * HEAD_SIZE)
    )
    keys_all, values_all, valid_all = (
        lax.all_gather(key_own, "context", axis=1, tiled=True),
        lax.all_gather(value_own, "context", axis=1, tiled=True),
        lax.all_gather(valid.astype(jnp.bfloat16), "context", axis=1, tiled=True),
    )
    seq_len = keys_all.shape[1]

    def attend(carry, items):
        qseq, kseq, vseq, okseq = items
        key_rows = kseq.reshape(seq_len, heads_kv, HEAD_SIZE)
        value_rows = vseq.reshape(seq_len, heads_kv, HEAD_SIZE)
        scores = masked_scores(qseq, key_rows, okseq, positions, scale)
        top = jnp.max(scores, axis=-1, keepdims=True)
        expo = jnp.exp(scores - top)
        total = jnp.sum(expo, axis=-1, keepdims=True)
        probr = (expo / total).astype(jnp.bfloat16)
        ctx = jnp.einsum("kgqj,jkd->qkgd", probr, value_rows, preferred_element_type=jnp.float32)
        lse = (top + jnp.log(total))[..., 0]
        return (carry, (ctx.astype(jnp.bfloat16).reshape(seg, heads_q * HEAD_SIZE), lse))

    carry, (context, lse_all) = lax.scan(
        attend, jnp.float32(0.0), (query_rows, keys_all, values_all, valid_all)
    )
    ctx_flat = context.reshape(row_count, heads_q * HEAD_SIZE)
    attn = lax.psum(
        jnp.dot(ctx_flat, wo, preferred_element_type=jnp.float32).astype(jnp.bfloat16), "tensor"
    ).astype(jnp.float32)
    resid = x + attn.reshape(seqs, seg, width)
    normed2, inverse2, pre2 = rms_forward(resid, gain2)
    h2 = pre2.astype(jnp.bfloat16).reshape(row_count, width)
    gate = jnp.dot(h2, wg, preferred_element_type=jnp.float32)
    up = jnp.dot(h2, wu, preferred_element_type=jnp.float32)
    sigma = jax.nn.sigmoid(gate)
    silu = gate * sigma
    act = (silu * up).astype(jnp.bfloat16)
    mixed = lax.psum(
        jnp.dot(act, wd, preferred_element_type=jnp.float32).astype(jnp.bfloat16), "tensor"
    ).astype(jnp.float32)
    out = resid + mixed.reshape(seqs, seg, width)
    output = out.astype(jnp.bfloat16)
    validf = valid.astype(jnp.float32)[..., None]
    diff = out - teacher.astype(jnp.float32)
    count, squares = lax.psum(
        (jnp.sum(valid.astype(jnp.float32)), jnp.sum(validf * diff * diff)), "context"
    )
    loss = squares / (count * width)
    dout = validf * (
        out_grad.astype(jnp.float32) + jnp.float32(seqs * seg * ctx_size) / count * diff
    )
    dm = dout.astype(jnp.bfloat16).reshape(row_count, width)
    grad_down = dot_left(act, dm)
    dact = dot_right(dm, wd)
    dgate = (dact * up * sigma * (1.0 + gate * (1.0 - sigma))).astype(jnp.bfloat16)
    dup = (dact * silu).astype(jnp.bfloat16)
    grad_gate = dot_left(h2, dgate)
    grad_up = dot_left(h2, dup)
    dh2 = (
        lax.psum((dot_right(dgate, wg) + dot_right(dup, wu)).astype(jnp.bfloat16), "tensor")
        .astype(jnp.float32)
        .reshape(seqs, seg, width)
    )
    grad_gain2 = jnp.sum(dh2 * normed2, axis=(0, 1))
    dresid = dout + rms_backward(dh2, normed2, inverse2, gain2)
    dattn = dresid.astype(jnp.bfloat16).reshape(row_count, width)
    grad_out = dot_left(ctx_flat, dattn)
    dctx = (
        dot_right(dattn, wo)
        .astype(jnp.bfloat16)
        .reshape(seqs, seg, heads_kv, head_group, HEAD_SIZE)
    )

    def attend_back(carry, items):
        qseq, kseq, vseq, okseq, lseq, dseq = items
        allowed = allowed_pairs(okseq, positions, seq_len)

        def head_back(parts):
            qhead, khead, vhead, dhead, lhead = parts
            raw = (
                jnp.einsum("qgd,jd->gqj", qhead, khead, preferred_element_type=jnp.float32) * scale
            )
            scores = jnp.where(allowed[None], raw, jnp.float32(-1e30))
            prob = jnp.exp(scores - lhead[..., None])
            probr = prob.astype(jnp.bfloat16)
            dprob = jnp.einsum("qgd,jd->gqj", dhead, vhead, preferred_element_type=jnp.float32)
            delta = jnp.sum(prob * dprob, axis=-1, keepdims=True)
            dscore = (prob * (dprob - delta)).astype(jnp.bfloat16)
            dq = (
                jnp.einsum("gqj,jd->qgd", dscore, khead, preferred_element_type=jnp.float32) * scale
            )
            dk = (
                jnp.einsum("gqj,qgd->jd", dscore, qhead, preferred_element_type=jnp.float32) * scale
            )
            dv = jnp.einsum("gqj,qgd->jd", probr, dhead, preferred_element_type=jnp.float32)
            return (dq, dk, dv)

        heads_in = (
            jnp.moveaxis(qseq, 1, 0),
            jnp.moveaxis(kseq.reshape(seq_len, heads_kv, HEAD_SIZE), 1, 0),
            jnp.moveaxis(vseq.reshape(seq_len, heads_kv, HEAD_SIZE), 1, 0),
            jnp.moveaxis(dseq, 1, 0),
            lseq,
        )
        dq_heads, dk_heads, dv_heads = lax.map(head_back, heads_in)
        dq = jnp.moveaxis(dq_heads, 0, 1)
        dk = jnp.moveaxis(dk_heads, 0, 1).reshape(seq_len, heads_kv * HEAD_SIZE)
        dv = jnp.moveaxis(dv_heads, 0, 1).reshape(seq_len, heads_kv * HEAD_SIZE)
        dk_own, dv_own = (
            lax.psum_scatter(dk, "context", scatter_dimension=0, tiled=True),
            lax.psum_scatter(dv, "context", scatter_dimension=0, tiled=True),
        )
        return (carry, (dq, dk_own, dv_own))

    carry, (dq_all, dk_all, dv_all) = lax.scan(
        attend_back, jnp.float32(0.0), (query_rows, keys_all, values_all, valid_all, lse_all, dctx)
    )
    dqpre = (
        rotate_back(dq_all.reshape(seqs, seg, heads_q, HEAD_SIZE), cosine, sine)
        .astype(jnp.bfloat16)
        .reshape(row_count, heads_q * HEAD_SIZE)
    )
    dkpre = (
        rotate_back(dk_all.reshape(seqs, seg, heads_kv, HEAD_SIZE), cosine, sine)
        .astype(jnp.bfloat16)
        .reshape(row_count, heads_kv * HEAD_SIZE)
    )
    dvr = dv_all.astype(jnp.bfloat16).reshape(row_count, heads_kv * HEAD_SIZE)
    grad_query = dot_left(h1, dqpre)
    grad_key = dot_left(h1, dkpre)
    grad_value = dot_left(h1, dvr)
    dh1 = (
        lax.psum(
            (dot_right(dqpre, wq) + dot_right(dkpre, wk) + dot_right(dvr, wv)).astype(jnp.bfloat16),
            "tensor",
        )
        .astype(jnp.float32)
        .reshape(seqs, seg, width)
    )
    grad_gain1 = jnp.sum(dh1 * normed1, axis=(0, 1))
    input_grad = dresid + rms_backward(dh1, normed1, inverse1, gain1)
    summed = (
        lax.psum_scatter(grad_gain1, "context", scatter_dimension=0, tiled=True),
        lax.psum_scatter(grad_query, "context", scatter_dimension=0, tiled=True),
        lax.psum_scatter(grad_key, "context", scatter_dimension=0, tiled=True),
        lax.psum_scatter(grad_value, "context", scatter_dimension=0, tiled=True),
        lax.psum_scatter(grad_out, "context", scatter_dimension=1, tiled=True),
        lax.psum_scatter(grad_gain2, "context", scatter_dimension=0, tiled=True),
        lax.psum_scatter(grad_gate, "context", scatter_dimension=0, tiled=True),
        lax.psum_scatter(grad_up, "context", scatter_dimension=0, tiled=True),
        lax.psum_scatter(grad_down, "context", scatter_dimension=1, tiled=True),
    )
    (
        grad_gain1,
        grad_query,
        grad_key,
        grad_value,
        grad_out,
        grad_gain2,
        grad_gate,
        grad_up,
        grad_down,
    ) = summed
    return (
        output,
        loss,
        input_grad,
        grad_gain1,
        grad_gain2,
        grad_query,
        grad_key,
        grad_value,
        grad_out,
        grad_gate,
        grad_up,
        grad_down,
    )


def solution(mesh):
    in_specs = (
        P(None, "context", None),
        P(None, "context"),
        P(None, "context", None),
        P(None, "context", None),
        P("context"),
        P("context", "tensor"),
        P("context", "tensor"),
        P("context", "tensor"),
        P("tensor", "context"),
        P("context"),
        P("context", "tensor"),
        P("context", "tensor"),
        P("tensor", "context"),
    )
    out_specs = (
        P(None, "context", None),
        P(),
        P(None, "context", None),
        P("context"),
        P("context"),
        P("context", "tensor"),
        P("context", "tensor"),
        P("context", "tensor"),
        P("tensor", "context"),
        P("context", "tensor"),
        P("context", "tensor"),
        P("tensor", "context"),
    )
    return jax.shard_map(shards, mesh=mesh, in_specs=in_specs, out_specs=out_specs, check_vma=False)
```

profile of v0, /device:TPU:11, one launch (start us, length us, event | category | flops | bytes accessed | tf_op | source)
XLA Modules:
  0.0 2595.1 jit_solution(12958237391377139610)
XLA Ops:
  12.4 45.0 %all-reduce.5 = (bf16[2560]{0:T(1024)(128)(2,1)S(1)}, bf16[2560]{0:T(1024)(128)(2,1)S(1)}) all-reduce(bf16[2560]{0:T(1024)(128)(2,1)S(1)} %dynamic-update-slice, bf16[2560]{0:T(1024)(128)(2,1)S(1)} %dynamic-update-slice.1), channel_id=1, replica_groups=mesh['tensor'=2,'context'=16] {'context'}, use_global_device_ids=true, to_apply=%add | all-reduce | flops 5120 | bytes 20480
  63.3 29.7 %all-gather.15.cloned.1.call-done = bf16[2560,320]{1,0:T(8,128)(2,1)} async-done(((bf16[160,320]{1,0:T(8,128)(2,1)}), bf16[2560,320]{1,0:T(8,128)(2,1)}) %all-gather.15.cloned.1.call-update) | async-done | bytes 1638416 | tf_op jit(solution)/shard_map/all_gather | solution.py:92
  99.1 16.8 all-gather
  116.0 18.6 all-gather.13.cloned.1.call-done
  136.2 39.7 %all-gather.17.cloned.1.call-done = bf16[2,1024,320]{2,1,0:T(8,128)(2,1)} async-done(((bf16[2,64,320]{2,1,0:T(8,128)(2,1)}), bf16[2,1024,320]{2,1,0:T(8,128)(2,1)}) %all-gather.17.cloned.1.call-update) | async-done | bytes 1310736 | tf_op jit(solution)/shard_map/all_gather | solution.py:137
  177.6 63.7 %all-gather.19.cloned.1.call-done = bf16[2560,1280]{1,0:T(8,128)(2,1)} async-done(((bf16[160,1280]{1,0:T(8,128)(2,1)}), bf16[2560,1280]{1,0:T(8,128)(2,1)}) %all-gather.19.cloned.1.call-update) | async-done | bytes 6553616 | tf_op jit(solution)/shard_map/all_gather | solution.py:91
  241.3 9.5 copy.53
  250.7 5.3 fusion.86
  257.6 16.1 while.73
  273.8 31.6 %all-gather.21.cloned.1.call-done = bf16[1280,2560]{0,1:T(8,128)(2,1)} async-done(((bf16[1280,160]{0,1:T(8,128)(2,1)}), bf16[1280,2560]{0,1:T(8,128)(2,1)}) %all-gather.21.cloned.1.call-update) | async-done | bytes 6553616 | tf_op jit(solution)/shard_map/all_gather | solution.py:94
  305.4 6.1 convolution_convert_fusion.1
  314.1 28.1 %all-reduce.11.cloned.1.call-done = bf16[2,64,2560]{2,1,0:T(8,128)(2,1)} async-done(((bf16[2,64,2560]{2,1,0:T(8,128)(2,1)}), bf16[2,64,2560]{2,1,0:T(8,128)(2,1)}) %all-reduce.11.cloned.1.call-update) | async-done | bytes 655376 | tf_op jit(solution)/shard_map/psum | solution.py:160
  344.8 92.8 %all-gather.23.cloned.1.call-done = bf16[2560,3456]{1,0:T(8,128)(2,1)} async-done(((bf16[160,3456]{1,0:T(8,128)(2,1)}), bf16[2560,3456]{1,0:T(8,128)(2,1)}) %all-gather.23.cloned.1.call-update) | async-done | bytes 17694736 | tf_op jit(solution)/shard_map/all_gather | solution.py:96
  437.6 10.0 fusion.96
  447.6 85.1 %all-gather.25.cloned.1.call-done = bf16[2560,3456]{1,0:T(8,128)(2,1)} async-done(((bf16[160,3456]{1,0:T(8,128)(2,1)}), bf16[2560,3456]{1,0:T(8,128)(2,1)}) %all-gather.25.cloned.1.call-update) | async-done | bytes 17694736 | tf_op jit(solution)/shard_map/all_gather | solution.py:97
  532.7 11.1 multiply_convert_fusion.3
  543.8 83.8 %all-gather.27.cloned.1.call-done = bf16[3456,2560]{0,1:T(8,128)(2,1)} async-done(((bf16[3456,160]{0,1:T(8,128)(2,1)}), bf16[3456,2560]{0,1:T(8,128)(2,1)}) %all-gather.27.cloned.1.call-update) | async-done | bytes 17694736 | tf_op jit(solution)/shard_map/all_gather | solution.py:98
  627.6 12.8 convolution_convert_fusion
  641.2 22.4 psum.45
  664.3 7.6 all-reduce.13.cloned.1.call-done
  674.7 10.3 multiply_convert_fusion.1
  684.9 13.1 fusion.97
  698.0 13.1 fusion.64
  711.2 31.9 %all-reduce.15.cloned.1.call-done = bf16[2,64,2560]{2,1,0:T(8,128)(2,1)} async-done(((bf16[2,64,2560]{2,1,0:T(8,128)(2,1)}), bf16[2,64,2560]{2,1,0:T(8,128)(2,1)}) %all-reduce.15.cloned.1.call-update) | async-done | bytes 655376 | tf_op jit(solution)/shard_map/psum | solution.py:193
  743.1 3.3 fusion.79
  748.2 3.9 convolution_convert_fusion.2
  753.9 291.5 %while.75 = (s32[]{:T(128)}, f32[2,64,4,4,80]{4,1,3,2,0:T(8,128)}, f32[2,64,320]{1,2,0:T(8,128)}, bf16[2,64,320]{1,2,0:T(8,128)(2,1)S(1)}, bf16[2,64,4,4,80]{4,1...) while((s32[]{:T(128)}, f32[2,64,4,4,80]{4,1,3,2,0:T(8,128)}, ...), condition=%wide.region_20.21_spmd.clone.clone, body=%wide.region_14.20_spmd.clone.clone.sunk | while | flops 212320064 | bytes 45916264 | solution.py:248
  758.1 16.2 while.76
  774.3 2.9 copy.91
  782.0 52.9 %reduce-scatter.34.cloned.1.call-done = f32[64,320]{1,0:T(8,128)} async-done(((f32[1024,320]{1,0:T(8,128)}), f32[64,320]{1,0:T(8,128)}) %reduce-scatter.34.cloned.1.call-update) | async-done | bytes 81936 | tf_op jit(solution)/shard_map/while
  835.9 61.5 %reduce-scatter.32.cloned.1.call-done = f32[64,320]{1,0:T(8,128)} async-done(((f32[1024,320]{1,0:T(8,128)}), f32[64,320]{1,0:T(8,128)}) %reduce-scatter.32.cloned.1.call-update) | async-done | bytes 81936 | tf_op jit(solution)/shard_map/while
  903.3 16.2 while.76
  927.2 53.9 %reduce-scatter.34.cloned.1.call-done = f32[64,320]{1,0:T(8,128)} async-done(((f32[1024,320]{1,0:T(8,128)}), f32[64,320]{1,0:T(8,128)}) %reduce-scatter.34.cloned.1.call-update) | async-done | bytes 81936 | tf_op jit(solution)/shard_map/while
  982.1 61.6 %reduce-scatter.32.cloned.1.call-done = f32[64,320]{1,0:T(8,128)} async-done(((f32[1024,320]{1,0:T(8,128)}), f32[64,320]{1,0:T(8,128)}) %reduce-scatter.32.cloned.1.call-update) | async-done | bytes 81936 | tf_op jit(solution)/shard_map/while
  1050.5 5.2 fusion.98
  1064.6 6.6 fusion.99
  1072.3 6.6 convolution_bitcast_fusion.3
  1080.3 13.9 fusion.103
  1095.5 15.0 fusion.102
  1111.8 14.4 fusion.101
  1129.7 46.3 %all-reduce.4 = (f32[]{:T(128)}, f32[2560]{0:T(1024)S(1)}, f32[2560]{0:T(1024)S(1)}) all-reduce(f32[]{:T(128)} %get-tuple-element.613, f32[2560]{0:T(1024)S(1)} %get-tuple-element.611, f32[2560]{0:T(1024)S(1)} %copy-done.39), channel_id=1, replica_groups=mesh['tensor'=2,'context'=16] {'context'}, use_global_device_ids=true, to_apply=%region_9.10 | all-reduce | flops 5121 | bytes 40968 | tf_op jit(solution)/shard_map/psum | solution.py:178
  1178.0 3.8 fusion.75
  1181.9 57.1 %reduce-scatter.20.cloned.1.call-done = f32[160,320]{1,0:T(8,128)} async-done(((f32[2560,320]{1,0:T(8,128)}), f32[160,320]{1,0:T(8,128)}) %reduce-scatter.20.cloned.1.call-update) | async-done | bytes 204816 | tf_op jit(solution)/shard_map/reduce_scatter | solution.py:278
  1239.0 142.7 %reduce-scatter.18.cloned.1.call-done = f32[160,1280]{1,0:T(8,128)} async-done(((f32[2560,1280]{1,0:T(8,128)}), f32[160,1280]{1,0:T(8,128)}) %reduce-scatter.18.cloned.1.call-update) | async-done | bytes 819216 | tf_op jit(solution)/shard_map/reduce_scatter | solution.py:277
  1381.6 142.7 %reduce-scatter.24.cloned.1.call-done = f32[1280,160]{0,1:T(8,128)} async-done(((f32[1280,2560]{0,1:T(8,128)}), f32[1280,160]{0,1:T(8,128)}) %reduce-scatter.24.cloned.1.call-update) | async-done | bytes 819216 | tf_op jit(solution)/shard_map/reduce_scatter | solution.py:280
  1524.4 353.6 %reduce-scatter.30.cloned.1.call-done = f32[3456,160]{0,1:T(8,128)} async-done(((f32[3456,2560]{0,1:T(8,128)}), f32[3456,160]{0,1:T(8,128)}) %reduce-scatter.30.cloned.1.call-update) | async-done | bytes 2211856 | tf_op jit(solution)/shard_map/reduce_scatter | solution.py:284
  1878.0 354.7 %reduce-scatter.28.cloned.1.call-done = f32[160,3456]{1,0:T(8,128)} async-done(((f32[2560,3456]{1,0:T(8,128)}), f32[160,3456]{1,0:T(8,128)}) %reduce-scatter.28.cloned.1.call-update) | async-done | bytes 2211856 | tf_op jit(solution)/shard_map/reduce_scatter | solution.py:283
  2232.7 354.0 %reduce-scatter.26.cloned.1.call-done = f32[160,3456]{1,0:T(8,128)} async-done(((f32[2560,3456]{1,0:T(8,128)}), f32[160,3456]{1,0:T(8,128)}) %reduce-scatter.26.cloned.1.call-update) | async-done | bytes 2211856 | tf_op jit(solution)/shard_map/reduce_scatter | solution.py:282
  (345 shorter events, 129.5 us)
Async XLA Ops:
  7.2 52.2 %copy-start = (bf16[2,64,2560]{2,1,0:T(8,128)(2,1)S(1)}, bf16[2,64,2560]{2,1,0:T(8,128)(2,1)}, u32[]{:S(2)}) copy-start(bf16[2,64,2560]{2,1,0:T(8,128)(2,1)} %param.19) | copy-start | bytes 1966084
  7.2 52.4 %all-gather.11.cloned.1.call-start = ((), (), s32[]{:S(2)}) async-start(), calls=%async_computation.9 | async-start | bytes 2088960 | tf_op jit(solution)/shard_map/all_gather | solution.py:93
  7.9 85.1 %all-gather.15.cloned.1.call-start = ((), (), s32[]{:S(2)}) async-start(), calls=%async_computation.11 | async-start | bytes 2088960 | tf_op jit(solution)/shard_map/all_gather | solution.py:92
  8.7 125.9 %all-gather.13.cloned.1.call-start = ((), (), s32[]{:S(2)}) async-start(), calls=%async_computation.10 | async-start | bytes 1671168 | tf_op jit(solution)/shard_map/all_gather | solution.py:138
  59.6 36.2 %copy-start.5 = (bf16[2,64,2560]{2,1,0:T(8,128)(2,1)}, bf16[2,64,2560]{2,1,0:T(8,128)(2,1)S(1)}, u32[]{:S(2)}) copy-start(bf16[2,64,2560]{2,1,0:T(8,128)(2,1)S(1)} %fusion.80) | copy-start | bytes 1966084
  63.0 112.9 %all-gather.17.cloned.1.call-start = ((), (), s32[]{:S(2)}) async-start(), calls=%async_computation.12 | async-start | bytes 1671168 | tf_op jit(solution)/shard_map/all_gather | solution.py:137
  63.3 192.8 %copy-start.31 = (f32[64,40]{1,0:T(8,128)}, f32[64,40]{1,0:T(8,128)S(1)}, u32[]{:S(2)}) copy-start(f32[64,40]{1,0:T(8,128)S(1)} %get-tuple-element.707) | copy-start | bytes 30724
  63.3 192.8 %copy-start.33 = (f32[64,40]{1,0:T(8,128)}, f32[64,40]{1,0:T(8,128)S(1)}, u32[]{:S(2)}) copy-start(f32[64,40]{1,0:T(8,128)S(1)} %get-tuple-element.708) | copy-start | bytes 30724
  97.8 143.4 %all-gather.19.cloned.1.call-start = ((), (), s32[]{:S(2)}) async-start(), calls=%async_computation.13 | async-start | bytes 6963200 | tf_op jit(solution)/shard_map/all_gather | solution.py:91
  98.4 207.0 %all-gather.21.cloned.1.call-start = ((), (), s32[]{:S(2)}) async-start(), calls=%async_computation.14 | async-start | bytes 6963200 | tf_op jit(solution)/shard_map/all_gather | solution.py:94
  99.0 243.2 %all-reduce.11.cloned.1.call-start = ((), (), s32[]{:S(2)}) async-start(), calls=%async_computation.15 | async-start | bytes 1310720 | tf_op jit(solution)/shard_map/psum | solution.py:160
  99.1 647.4 %copy-start.42 = (f32[2,64]{1,0:T(2,128)}, f32[2,64]{1,0:T(2,128)S(1)}, u32[]{:S(2)}) copy-start(f32[2,64]{1,0:T(2,128)S(1)} %get-tuple-element.705) | copy-start | bytes 1540
  311.5 126.1 %all-gather.23.cloned.1.call-start = ((), (), s32[]{:S(2)}) async-start(), calls=%async_computation.16 | async-start | bytes 18800640 | tf_op jit(solution)/shard_map/all_gather | solution.py:96
  312.2 220.4 %all-gather.25.cloned.1.call-start = ((), (), s32[]{:S(2)}) async-start(), calls=%async_computation.17 | async-start | bytes 18800640 | tf_op jit(solution)/shard_map/all_gather | solution.py:97
  313.0 314.7 %all-gather.27.cloned.1.call-start = ((), (), s32[]{:S(2)}) async-start(), calls=%async_computation.18 | async-start | bytes 18800640 | tf_op jit(solution)/shard_map/all_gather | solution.py:98
  313.5 358.3 %all-reduce.13.cloned.1.call-start = ((), (), s32[]{:S(2)}) async-start(), calls=%async_computation.19 | async-start | bytes 1310720 | tf_op jit(solution)/shard_map/psum | solution.py:171
  314.1 432.4 %copy-start.35 = (f32[2560]{0:T(1024)}, f32[2560]{0:T(1024)S(1)}, u32[]{:S(2)}) copy-start(f32[2560]{0:T(1024)S(1)} %convert_element_type.144) | copy-start | bytes 30724
  343.7 402.8 %copy-start.40 = (f32[2,64]{1,0:T(2,128)}, f32[2,64]{1,0:T(2,128)S(1)}, u32[]{:S(2)}) copy-start(f32[2,64]{1,0:T(2,128)S(1)} %add_rsqrt_fusion) | copy-start | bytes 1540
  627.6 12.9 copy-start.49
  640.5 102.6 %all-reduce.15.cloned.1.call-start = ((), (), s32[]{:S(2)}) async-start(), calls=%async_computation.20 | async-start | bytes 1310720 | tf_op jit(solution)/shard_map/psum | solution.py:193
  674.2 10.8 copy-start.27
  743.1 3.4 copy-start.23
  753.9 292.5 %copy-start.32 = (f32[64,40]{1,0:T(8,128)S(1)}, f32[64,40]{1,0:T(8,128)}, u32[]{:S(2)}) copy-start(f32[64,40]{1,0:T(8,128)} %copy-done.31) | copy-start | bytes 30724
  753.9 292.5 %copy-start.34 = (f32[64,40]{1,0:T(8,128)S(1)}, f32[64,40]{1,0:T(8,128)}, u32[]{:S(2)}) copy-start(f32[64,40]{1,0:T(8,128)} %copy-done.33) | copy-start | bytes 30724
  753.9 81.0 %reduce-scatter.34.cloned.1.call-start = ((), (), s32[]{:S(2)}) async-start(), calls=%async_computation.30 | async-start | bytes 1671168 | tf_op jit(solution)/shard_map/while
  777.2 120.2 %reduce-scatter.32.cloned.1.call-start = ((), (), s32[]{:S(2)}) async-start(), calls=%async_computation.29 | async-start | bytes 1671168 | tf_op jit(solution)/shard_map/while
  780.2 118.9 %copy-start.3 = (bf16[2,1024,320]{1,2,0:T(8,128)(2,1)S(1)}, bf16[2,1024,320]{1,2,0:T(8,128)(2,1)}, u32[]{:S(2)}) copy-start(bf16[2,1024,320]{1,2,0:T(8,128)(2,1)} %copy-done.2) | copy-start | bytes 3932164 | tf_op jit(solution)/shard_map/while
  899.1 82.0 %reduce-scatter.34.cloned.1.call-start = ((), (), s32[]{:S(2)}) async-start(), calls=%async_computation.30 | async-start | bytes 1671168 | tf_op jit(solution)/shard_map/while
  922.4 121.3 %reduce-scatter.32.cloned.1.call-start = ((), (), s32[]{:S(2)}) async-start(), calls=%async_computation.29 | async-start | bytes 1671168 | tf_op jit(solution)/shard_map/while
  925.4 120.0 %copy-start.3 = (bf16[2,1024,320]{1,2,0:T(8,128)(2,1)S(1)}, bf16[2,1024,320]{1,2,0:T(8,128)(2,1)}, u32[]{:S(2)}) copy-start(bf16[2,1024,320]{1,2,0:T(8,128)(2,1)} %copy-done.2) | copy-start | bytes 3932164 | tf_op jit(solution)/shard_map/while
  1045.4 82.5 %all-reduce.17.cloned.1.call-start = ((), (), s32[]{:S(2)}) async-start(), calls=%async_computation.21 | async-start | bytes 1310720 | tf_op jit(solution)/shard_map/psum | solution.py:266
  1050.5 5.2 copy-start.17
  1058.9 123.0 %reduce-scatter.22.cloned.1.call-start = ((), (), s32[]{:S(2)}) async-start(), calls=%async_computation.24 | async-start | bytes 4177920 | tf_op jit(solution)/shard_map/reduce_scatter | solution.py:279
  1061.8 177.1 %reduce-scatter.20.cloned.1.call-start = ((), (), s32[]{:S(2)}) async-start(), calls=%async_computation.23 | async-start | bytes 4177920 | tf_op jit(solution)/shard_map/reduce_scatter | solution.py:278
  1064.5 317.1 %reduce-scatter.18.cloned.1.call-start = ((), (), s32[]{:S(2)}) async-start(), calls=%async_computation.22 | async-start | bytes 13926400 | tf_op jit(solution)/shard_map/reduce_scatter | solution.py:277
  1071.2 453.2 %reduce-scatter.24.cloned.1.call-start = ((), (), s32[]{:S(2)}) async-start(), calls=%async_computation.25 | async-start | bytes 13926400 | tf_op jit(solution)/shard_map/reduce_scatter | solution.py:280
  1079.0 799.0 %reduce-scatter.30.cloned.1.call-start = ((), (), s32[]{:S(2)}) async-start(), calls=%async_computation.28 | async-start | bytes 37601280 | tf_op jit(solution)/shard_map/reduce_scatter | solution.py:284
  1094.2 1138.5 %reduce-scatter.28.cloned.1.call-start = ((), (), s32[]{:S(2)}) async-start(), calls=%async_computation.27 | async-start | bytes 37601280 | tf_op jit(solution)/shard_map/reduce_scatter | solution.py:283
  1110.6 1476.1 %reduce-scatter.26.cloned.1.call-start = ((), (), s32[]{:S(2)}) async-start(), calls=%async_computation.26 | async-start | bytes 37601280 | tf_op jit(solution)/shard_map/reduce_scatter | solution.py:282
  1126.2 51.7 %copy-start.16 = (bf16[2,64,2560]{2,1,0:T(8,128)(2,1)S(1)}, bf16[2,64,2560]{2,1,0:T(8,128)(2,1)}, u32[]{:S(2)}) copy-start(bf16[2,64,2560]{2,1,0:T(8,128)(2,1)} %all-reduce.13.cloned.1.call-done) | copy-start | bytes 1966084
  1126.2 51.7 %copy-start.22 = (bf16[2,64,2560]{2,1,0:T(8,128)(2,1)S(1)}, bf16[2,64,2560]{2,1,0:T(8,128)(2,1)}, u32[]{:S(2)}) copy-start(bf16[2,64,2560]{2,1,0:T(8,128)(2,1)} %param.21) | copy-start | bytes 1966084
  1126.3 3.4 copy-start.39
  1126.3 51.7 %copy-start.9 = (bf16[2,64,2560]{2,1,0:T(8,128)(2,1)S(1)}, bf16[2,64,2560]{2,1,0:T(8,128)(2,1)}, u32[]{:S(2)}) copy-start(bf16[2,64,2560]{2,1,0:T(8,128)(2,1)} %all-reduce.11.cloned.1.call-done) | copy-start | bytes 1966084
  1126.3 51.7 %copy-start.14 = (bf16[2,64,2560]{2,1,0:T(8,128)(2,1)S(1)}, bf16[2,64,2560]{2,1,0:T(8,128)(2,1)}, u32[]{:S(2)}) copy-start(bf16[2,64,2560]{2,1,0:T(8,128)(2,1)} %param.22) | copy-start | bytes 1966084
  1126.3 51.7 %copy-start.36 = (f32[2560]{0:T(1024)S(1)}, f32[2560]{0:T(1024)}, u32[]{:S(2)}) copy-start(f32[2560]{0:T(1024)} %copy-done.35) | copy-start | bytes 30724
  1126.3 51.7 %copy-start.41 = (f32[2,64]{1,0:T(2,128)S(1)}, f32[2,64]{1,0:T(2,128)}, u32[]{:S(2)}) copy-start(f32[2,64]{1,0:T(2,128)} %copy-done.40) | copy-start | bytes 1540
  1126.3 51.7 %copy-start.43 = (f32[2,64]{1,0:T(2,128)S(1)}, f32[2,64]{1,0:T(2,128)}, u32[]{:S(2)}) copy-start(f32[2,64]{1,0:T(2,128)} %copy-done.42) | copy-start | bytes 1540
  1126.3 51.7 %copy-start.47 = (f32[2,64]{1,0:T(2,128)S(1)}, f32[2,64]{1,0:T(2,128)}, u32[]{:S(2)}) copy-start(f32[2,64]{1,0:T(2,128)} %copy-done.46) | copy-start | bytes 1540
  (32 other events, 55.8 us)
Sparse Core Ops, SparseCore 0:
  10.3 40.6 all-gather.10
  53.3 39.7 all-gather.14
  95.9 38.6 all-gather.12
  137.3 38.5 all-gather.16
  178.0 63.1 all-gather.18
  243.4 61.9 all-gather.20
  311.6 30.5 all-reduce.10
  343.9 93.6 all-gather.22
  439.2 93.3 all-gather.24
  534.2 93.3 all-gather.26
  640.6 31.2 all-reduce.12
  711.3 31.7 all-reduce.14
  777.4 57.4 reduce-scatter.33
  839.0 58.4 reduce-scatter.31
  922.5 58.4 reduce-scatter.33
  985.2 58.4 reduce-scatter.31
  1059.0 32.5 all-reduce.16
  1095.9 68.7 reduce-scatter.21
  1169.7 69.2 reduce-scatter.19
  1243.5 138.1 reduce-scatter.17
  1386.9 137.4 reduce-scatter.23
  1529.3 348.6 reduce-scatter.29
  1883.5 349.1 reduce-scatter.27
  2237.5 349.1 reduce-scatter.25
where the time goes:
time: 2610 us; the launch traced here: 2600 us
  waiting for transfers between devices  2150 us (82%)
  matrix products  193 us (7%)
  blocking collectives  131 us (5%)
  local copies, waits for them, and re-layouts  69.5 us (3%)
  other arithmetic  27.3 us (1%)
    reduce_scatter x1, waiting for transfers between devices, shards(): lax.psum_scatter(grad_up, 'context', scatter_dimension=0, tiled=True)  355 us
    reduce_scatter x1, waiting for transfers between devices, shards(): lax.psum_scatter(grad_gate, 'context', scatter_dimension=0, tiled=True)  354 us
    reduce_scatter x1, waiting for transfers between devices, shards(): lax.psum_scatter(grad_down, 'context', scatter_dimension=1, tiled=True)  354 us
    while x8, waiting for transfers between devices  230 us
    reduce_scatter x1, waiting for transfers between devices, shards(): lax.psum_scatter(grad_out, 'context', scatter_dimension=1, tiled=True)  143 us
    reduce_scatter x1, waiting for transfers between devices, shards(): lax.psum_scatter(grad_query, 'context', scatter_dimension=0, tiled=True)  143 us
    all_gather x1, waiting for transfers between devices, shards(): lax.all_gather(w_gate, 'context', axis=0, tiled=True)  92.8 us
    all_gather x1, waiting for transfers between devices, shards(): lax.all_gather(w_up, 'context', axis=0, tiled=True)  85.1 us
  transfers between devices with their start and end apart: 24, of which 21 were waited for; matrix products, arithmetic and copies ran while one was open for 6% of the time, Pallas kernels for 0%

commit v1 on v0

--- a/solution.py
+++ b/solution.py
@@ -1,16 +1,470 @@
+import functools
 import math
 
 import jax
 import jax.numpy as jnp
 from jax import lax
+from jax.experimental import pallas as pl
+from jax.experimental.pallas import tpu as pltpu
 from jax.sharding import PartitionSpec as P
 
 HEAD_SIZE = 80
 BLOCK = 256
-
+LANES = 128
+VMEM_BYTES = 56 * 1024 * 1024
 
 eps = 1e-05
 theta = 10000.0
+BF = jnp.bfloat16
+F32 = jnp.float32
+
+
+def whole(shape, dtype):
+    return jax.ShapeDtypeStruct(shape, dtype)
+
+
+def vmem():
+    return pl.BlockSpec(memory_space=pltpu.VMEM)
+
+
+def smem():
+    return pl.BlockSpec(memory_space=pltpu.SMEM)
+
+
+def kernel_call(body, outs, ins_smem, ins, flops=0, nbytes=0, scratch=()):
+    single = not isinstance(outs, (list, tuple))
+    return pl.pallas_call(
+        body,
+        out_shape=outs,
+        in_specs=[smem()] * ins_smem + [vmem()] * (len(ins) - ins_smem),
+        out_specs=vmem() if single else [vmem()] * len(outs),
+        scratch_shapes=list(scratch),
+        compiler_params=pltpu.CompilerParams(vmem_limit_bytes=VMEM_BYTES),
+        cost_estimate=pl.CostEstimate(flops=flops, bytes_accessed=nbytes, transcendentals=0),
+    )(*ins)
+
+
+def dot_nn(a, b):
+    return lax.dot_general(a, b, (((1,), (0,)), ((), ())), preferred_element_type=F32)
+
+
+def dot_nt(a, b):
+    return lax.dot_general(a, b, (((1,), (1,)), ((), ())), preferred_element_type=F32)
+
+
+def dot_tn(a, b):
+    return lax.dot_general(a, b, (((0,), (0,)), ((), ())), preferred_element_type=F32)
+
+
+def move_c(a):
+    return lax.ppermute(a, "context", [(k, k ^ 1) for k in range(16)])
+
+
+def move_x(a):
+    return lax.ppermute(a, "context", [(k, k ^ 2) for k in range(16)])
+
+
+def move_z(a, step):
+    return lax.ppermute(a, "context", [(k, (k + 4 * step) % 16) for k in range(16)])
+
+
+def move_zx(a, bit):
+    return lax.ppermute(a, "context", [(k, k ^ (4 * bit)) for k in range(16)])
+
+
+def move_y(a):
+    return lax.ppermute(a, "tensor", [(0, 1), (1, 0)])
+
+
+def sum_context(a):
+    a = a + move_c(a)
+    a = a + move_x(a)
+    a = a + move_zx(a, 1)
+    return a + move_zx(a, 2)
+
+
+def gather_rows(own):
+    near = [own, move_z(own, 1), move_z(own, 2), move_z(own, 3)]
+    far = [move_x(p) for p in near]
+    near_c = move_c(jnp.stack(near))
+    far_c = move_c(jnp.stack(far))
+    pieces = []
+    for m in range(4):
+        pieces += [near[m], near_c[m], far[m], far_c[m]]
+    return jnp.concatenate(pieces, axis=0)
+
+
+def scatter_rows(part):
+    n = part.shape[0] // 16
+    p = part.reshape(4, 2, 2, n, part.shape[1])
+    q = p[:, :, 0] + move_c(p[:, :, 1].astype(BF)).astype(F32)
+    s = [None] * 4
+    for m in (2, 1, 3, 0):
+        s[m] = q[m, 0] + move_x(q[m, 1].astype(BF)).astype(F32)
+    total = s[0]
+    for m in (2, 1, 3):
+        total = total + move_z(s[m].astype(BF), 4 - m).astype(F32)
+    return total
+
+
+def pack_weights(place, wq, wk, wv, wot, wg, wu, wdt):
+    rows = wq.shape[0]
+    cq, ck, cf = wq.shape[1] // 8, wk.shape[1] // 4, wg.shape[1] // 8
+
+    def body(place_ref, wq_ref, wk_ref, wv_ref, wo_ref, wg_ref, wu_ref, wd_ref, a_ref, g_ref, d_ref):
+        z, x = place_ref[0], place_ref[1]
+        for zd in range(4):
+            for xd in range(2):
+                j = zd * 2 + xd
+                mz, mx = lax.rem(zd - z + 4, 4), lax.rem(xd + x, 2)
+                a_ref[mz, mx] = jnp.concatenate(
+                    [
+                        wq_ref[:, j * cq : (j + 1) * cq],
+                        wk_ref[:, zd * ck : (zd + 1) * ck],
+                        wv_ref[:, zd * ck : (zd + 1) * ck],
+                        wo_ref[:, j * cq : (j + 1) * cq],
+                    ],
+                    axis=1,
+                )
+                g_ref[mz, mx] = jnp.concatenate(
+                    [wg_ref[:, j * cf : (j + 1) * cf], wu_ref[:, j * cf : (j + 1) * cf]], axis=1
+                )
+                d_ref[mz, mx] = wd_ref[:, j * cf : (j + 1) * cf]
+
+    outs = [whole((4, 2, rows, w), BF) for w in (2 * cq + 2 * ck, 2 * cf, cf)]
+    return kernel_call(body, outs, 1, (place, wq, wk, wv, wot, wg, wu, wdt))
+
+
+def spread(place, blocks):
+    y, c = place[3], place[2]
+    rows, cols = blocks.shape[2:]
+    got = [blocks[0]] + [move_z(blocks[m], m) for m in (1, 2, 3)]
+    far = move_x(jnp.stack([g[1] for g in got]))
+    own = jnp.concatenate([jnp.stack([g[0] for g in got]), far])
+    other = move_y(own)
+    mine = y == c
+    come = move_c(jnp.where(mine, other, own))
+
+    def body(place_ref, own_ref, other_ref, come_ref, out_ref):
+        z, x, c, y = place_ref[0], place_ref[1], place_ref[2], place_ref[3]
+
+        def put(keep_ref):
+            for zs in range(4):
+                for xs in range(2):
+                    at = lax.rem(xs + x, 2) * 4 + lax.rem(z - zs + 4, 4)
+                    out_ref[zs, xs, c] = keep_ref[at]
+                    out_ref[zs, xs, 1 - c] = come_ref[at]
+
+        @pl.when(y == c)
+        def _():
+            put(own_ref)
+
+        @pl.when(y != c)
+        def _():
+            put(other_ref)
+
+    out = kernel_call(body, whole((4, 2, 2, rows, cols), BF), 1, (place, own, other, come))
+    return out.reshape(16 * rows, cols)
+
+
+def collect(place, part):
+    z, x, c, y = place[0], place[1], place[2], place[3]
+    rows, cols = part.shape[0] // 16, part.shape[1]
+    p = part.reshape(8, 2, rows, cols)
+    keep = lax.dynamic_index_in_dim(p, c, 1, keepdims=False)
+    come = move_c(lax.dynamic_index_in_dim(p, 1 - c, 1, keepdims=False).astype(BF))
+    mine = y == c
+    give = move_y(jnp.where(mine, come, keep.astype(BF)))
+    total = (jnp.where(mine, keep, come.astype(F32)) + give.astype(F32)).astype(BF)
+    total = total.reshape(4, 2, rows, cols)
+    to_near = [lax.dynamic_slice(total, (lax.rem(z + m, 4), x, 0, 0), (1, 1, rows, cols))[0] for m in range(4)]
+    to_far = [lax.dynamic_slice(total, (lax.rem(z + m, 4), 1 - x, 0, 0), (1, 1, rows, cols))[0] for m in range(4)]
+    far = move_x(jnp.stack(to_far))
+    pairs = [jnp.concatenate([to_near[m], far[m]]) for m in range(4)]
+    return jnp.stack([pairs[0]] + [move_z(pairs[m], m) for m in (1, 2, 3)])
+
+
+def unpack(place, got, widths, shared):
+    rows = got.shape[2]
+
+    def body(place_ref, got_ref, *outs):
+        z, x = place_ref[0], place_ref[1]
+        for zs in range(4):
+            blocks = [
+                got_ref[lax.rem(z - zs + 4, 4), lax.rem(xs + x, 2)].astype(F32) for xs in range(2)
+            ]
+            at = 0
+            for out, width, both in zip(outs, widths, shared):
+                a, b = blocks[0][:, at : at + width], blocks[1][:, at : at + width]
+                if both:
+                    out[:, zs * width : (zs + 1) * width] = a + b
+                else:
+                    out[:, 2 * zs * width : (2 * zs + 1) * width] = a
+                    out[:, (2 * zs + 1) * width : (2 * zs + 2) * width] = b
+                at += width
+
+    outs = [whole((rows, (4 if both else 8) * width), F32) for width, both in zip(widths, shared)]
+    return kernel_call(body, outs, 1, (place, got))
+
+
+def turn(a, cosine, sine):
+    half = HEAD_SIZE // 2
+    lane = lax.broadcasted_iota(jnp.int32, a.shape, 1)
+    swapped = jnp.where(lane < half, pltpu.roll(a, LANES - half, 1), pltpu.roll(a, half, 1))
+    return a * cosine + swapped * sine
+
+
+def attention(place, lens, qkv, cosine, sine):
+    rows = qkv.shape[0]
+    blocks = rows // BLOCK
+    scale = HEAD_SIZE ** (-0.5)
+
+    def body(place_ref, len_ref, qkv_ref, cos_ref, sin_ref, q_ref, k_ref, v_ref, ctx_ref, lse_ref):
+        z = place_ref[0]
+        length = len_ref[0]
+        for m in range(blocks):
+            to = pl.multiple_of(lax.rem(z - m + blocks, blocks) * BLOCK, BLOCK)
+            rs = slice(m * BLOCK, (m + 1) * BLOCK)
+            cosine, sine = cos_ref[pl.ds(to, BLOCK), :], sin_ref[pl.ds(to, BLOCK), :]
+            for h in range(2):
+                q_ref[h, pl.ds(to, BLOCK), :] = turn(
+                    qkv_ref[rs, h * LANES : (h + 1) * LANES], cosine, sine
+                ).astype(BF)
+            k_ref[pl.ds(to, BLOCK), :] = turn(
+                qkv_ref[rs, 2 * LANES : 3 * LANES], cosine, sine
+            ).astype(BF)
+            v_ref[pl.ds(to, BLOCK), :] = qkv_ref[rs, 3 * LANES : 4 * LANES].astype(BF)
+        return z, length
+
+    def kernel(place_ref, len_ref, kpos_ref, qkv_ref, cos_ref, sin_ref, q_ref, k_ref, v_ref, ctx_ref, lse_ref):
+        z, length = body(place_ref, len_ref, qkv_ref, cos_ref, sin_ref, q_ref, k_ref, v_ref, ctx_ref, lse_ref)
+        for i in range(blocks):
+            back = pl.multiple_of(lax.rem(z - i + blocks, blocks) * BLOCK, BLOCK)
+            n = (i + 1) * BLOCK
+            ok = kpos_ref[:, :n] < length
+            for h in range(2):
+                s = dot_nt(q_ref[h, i * BLOCK : n, :], k_ref[:n, :]) * scale
+                s = jnp.where(ok, s, F32(-1e30))
+                top = jnp.max(s, axis=1, keepdims=True)
+                e = jnp.exp(s - top)
+                total = jnp.sum(e, axis=1, keepdims=True)
+                pr = (e / total).astype(BF)
+                ctx_ref[pl.ds(back, BLOCK), h * LANES : (h + 1) * LANES] = dot_nn(
+                    pr, v_ref[:n, :]
+                ).astype(BF)
+                lse_ref[h, i * BLOCK : n, :] = top + jnp.log(total)
+
+    outs = [
+        whole((2, rows, LANES), BF),
+        whole((rows, LANES), BF),
+        whole((rows, LANES), BF),
+        whole((rows, 2 * LANES), BF),
+        whole((2, rows, 1), F32),
+    ]
+    flops = 2 * rows * rows * LANES * 2 * 2
+    return kernel_call(kernel, outs, 2, (place, *lens, qkv, cosine, sine), flops, 8 << 20)
+
+
+def attention_back(place, lens, q, k, v, lse, dctx, cosine, sine):
+    rows = k.shape[0]
+    blocks = rows // BLOCK
+    scale = HEAD_SIZE ** (-0.5)
+
+    def kernel(place_ref, len_ref, kpos_ref, q_ref, k_ref, v_ref, lse_ref, dctx_ref, cos_ref, sin_ref, out_ref, dk_ref, dv_ref):
+        z, length = place_ref[0], len_ref[0]
+        dk_ref[...] = jnp.zeros_like(dk_ref)
+        dv_ref[...] = jnp.zeros_like(dv_ref)
+        for i in range(blocks):
+            back = pl.multiple_of(lax.rem(z - i + blocks, blocks) * BLOCK, BLOCK)
+            n = (i + 1) * BLOCK
+            ok = kpos_ref[:, :n] < length
+            cosine, sine = cos_ref[i * BLOCK : n, :], sin_ref[i * BLOCK : n, :]
+            for h in range(2):
+                qi = q_ref[h, i * BLOCK : n, :]
+                di = dctx_ref[pl.ds(back, BLOCK), h * LANES : (h + 1) * LANES]
+                s = dot_nt(qi, k_ref[:n, :]) * scale
+                p = jnp.where(ok, jnp.exp(s - lse_ref[h, i * BLOCK : n, :]), F32(0.0))
+                dp = dot_nt(di, v_ref[:n, :])
+                delta = jnp.sum(p * dp, axis=1, keepdims=True)
+                ds = (p * (dp - delta)).astype(BF)
+                dq = dot_nn(ds, k_ref[:n, :]) * scale
+                out_ref[pl.ds(back, BLOCK), h * LANES : (h + 1) * LANES] = turn(
+                    dq, cosine, -sine
+                ).astype(BF)
+                dk_ref[:n, :] += dot_tn(ds, qi)
+                dv_ref[:n, :] += dot_tn(p.astype(BF), di)
+        for i in range(blocks):
+            back = pl.multiple_of(lax.rem(z - i + blocks, blocks) * BLOCK, BLOCK)
+            rs = slice(i * BLOCK, (i + 1) * BLOCK)
+            out_ref[pl.ds(back, BLOCK), 2 * LANES : 3 * LANES] = turn(
+                dk_ref[rs, :] * scale, cos_ref[rs, :], -sin_ref[rs, :]
+            ).astype(BF)
+            out_ref[pl.ds(back, BLOCK), 3 * LANES : 4 * LANES] = dv_ref[rs, :].astype(BF)
+
+    flops = 2 * rows * rows * LANES * 2 * 5
+    return kernel_call(
+        kernel,
+        whole((rows, 4 * LANES), BF),
+        2,
+        (place, *lens, q, k, v, lse, dctx, cosine, sine),
+        flops,
+        8 << 20,
+        scratch=[pltpu.VMEM((rows, LANES), F32), pltpu.VMEM((rows, LANES), F32)],
+    )
+
+
+def pad_head(a):
+    return jnp.pad(a, ((0, 0), (0, LANES - HEAD_SIZE)))
+
+
+def rms_of(rows):
+    return lax.rsqrt(jnp.mean(rows * rows, axis=-1, keepdims=True) + eps)
+
+
+def layer(
+    inputs,
+    valid,
+    out_grad,
+    teacher,
+    norm_attn,
+    w_query,
+    key_matrix,
+    value_matrix,
+    w_out,
+    norm_mlp,
+    w_gate,
+    w_up,
+    w_down,
+):
+    seqs, seg, width = inputs.shape
+    y = lax.axis_index("tensor")
+    k = lax.axis_index("context")
+    z, x, c = k // 4, (k // 2) % 2, k % 2
+    place = jnp.stack([z, x, c, y]).astype(jnp.int32)
+    seq_len = 16 * seg
+    depth = norm_attn.shape[0]
+
+    def mine(a):
+        return lax.dynamic_index_in_dim(a, y, 0, keepdims=False)
+
+    own = mine(inputs)
+    a_blocks, g_blocks, d_blocks = pack_weights(
+        place, w_query, key_matrix, value_matrix, w_out.T, w_gate, w_up, w_down.T
+    )
+    rows_all = gather_rows(own)
+    small = jnp.zeros((8, width), F32)
+    small = lax.dynamic_update_slice(small, norm_attn.astype(F32)[None], (0, k * depth))
+    small = lax.dynamic_update_slice(small, norm_mlp.astype(F32)[None], (1, k * depth))
+    counts = jnp.sum(valid.astype(F32), axis=1)
+    small = small.at[2, 0].set(counts[0]).at[2, 1].set(counts[1])
+    small = sum_context(small)
+    gain1, gain2 = small[0:1], small[1:2]
+    count = small[2, 0] + small[2, 1]
+    length = jnp.where(y == 0, small[2, 0], small[2, 1]).astype(jnp.int32)[None]
+
+    w_attn = spread(place, a_blocks)
+    w_qkv = jnp.concatenate([pad_head(w_attn[:, HEAD_SIZE * i : HEAD_SIZE * (i + 1)]) for i in range(4)], axis=1)
+    w_ot = jnp.concatenate([pad_head(w_attn[:, HEAD_SIZE * i : HEAD_SIZE * (i + 1)]) for i in (4, 5)], axis=1)
+    w_gu = spread(place, g_blocks)
+    w_dt = spread(place, d_blocks)
+    hidden = w_dt.shape[1]
+
+    far = jnp.arange(2, dtype=jnp.int32)
+    pos = (
+        jnp.arange(4, dtype=jnp.int32)[:, None, None, None] * (4 * seg)
+        + (far ^ x)[None, :, None, None] * (2 * seg)
+        + (far ^ c)[None, None, :, None] * seg
+        + jnp.arange(seg, dtype=jnp.int32)[None, None, None, :]
+    ).reshape(seq_len)
+    half = HEAD_SIZE // 2
+    freqs = jnp.exp(-math.log(theta) * jnp.arange(half, dtype=F32) / half)
+    angles = pos.astype(F32)[:, None] * freqs[None, :]
+    cos_half, sin_half = jnp.cos(angles), jnp.sin(angles)
+    pad = jnp.zeros((seq_len, LANES - HEAD_SIZE), F32)
+    cosine = jnp.concatenate([cos_half, cos_half, pad], axis=1)
+    sine = jnp.concatenate([-sin_half, sin_half, pad], axis=1)
+    lens = (length, pos[None, :])
+
+    x_all = rows_all.astype(F32)
+    h1 = (x_all * rms_of(x_all) * gain1).astype(BF)
+    qkv = dot_nn(h1, w_qkv)
+    q, keys, values, ctx, lse = attention(place, lens, qkv, cosine, sine)
+    attn = scatter_rows(dot_nt(ctx, w_ot))
+    x_own = own.astype(F32)
+    resid = x_own + attn
+    inverse2 = rms_of(resid)
+    normed2 = resid * inverse2
+    h2 = gather_rows((normed2 * gain2).astype(BF))
+    gu = dot_nn(h2, w_gu)
+    gate, up = gu[:, :hidden], gu[:, hidden:]
+    sigma = jax.nn.sigmoid(gate)
+    silu = gate * sigma
+    act = (silu * up).astype(BF)
+    out = resid + scatter_rows(dot_nt(act, w_dt))
+    out_own = out.astype(BF)
+    okf = mine(valid).astype(F32)[:, None]
+    diff = out - mine(teacher).astype(F32)
+    squares = jnp.sum(okf * diff * diff)
+    dout = okf * (mine(out_grad).astype(F32) + F32(seqs * seq_len) / count * diff)
+    dm = gather_rows(dout.astype(BF))
+    dact = dot_nn(dm, w_dt)
+    g_down = collect(place, dot_tn(dm, act))
+    dgate = (dact * up * sigma * (1.0 + gate * (1.0 - sigma))).astype(BF)
+    dup = (dact * silu).astype(BF)
+    dgu = jnp.concatenate([dgate, dup], axis=1)
+    dh2 = scatter_rows(dot_nt(dgu, w_gu))
+    part_gu = dot_tn(h2, dgu)
+    tail2 = jnp.sum(part_gu * w_gu.astype(F32), axis=1, keepdims=True)
+    g_gu = collect(place, jnp.concatenate([part_gu, tail2], axis=1))
+    scaled = dh2 * gain2
+    dresid = dout + inverse2 * (scaled - normed2 * jnp.mean(scaled * normed2, axis=-1, keepdims=True))
+    da = gather_rows(dresid.astype(BF))
+    dctx = dot_nn(da, w_ot).astype(BF)
+    part_ot = dot_tn(da, ctx)
+    dqkv = attention_back(place, lens, q, keys, values, lse, dctx, cosine, sine)
+    dh1 = scatter_rows(dot_nt(dqkv, w_qkv))
+    part_qkv = dot_tn(h1, dqkv)
+    tail1 = jnp.sum(part_qkv * w_qkv.astype(F32), axis=1, keepdims=True)
+    cut = [part_qkv[:, LANES * i : LANES * i + HEAD_SIZE] for i in range(4)]
+    cut += [part_ot[:, LANES * i : LANES * i + HEAD_SIZE] for i in range(2)]
+    g_attn = collect(place, jnp.concatenate(cut + [tail1], axis=1))
+    inverse1 = rms_of(x_own)
+    normed1 = x_own * inverse1
+    scaled1 = dh1 * gain1
+    dx = dresid + inverse1 * (scaled1 - normed1 * jnp.mean(scaled1 * normed1, axis=-1, keepdims=True))
+
+    both_out = move_y(out_own)
+    both_dx = move_y(dx)
+    first = y == 0
+    output = jnp.stack([jnp.where(first, out_own, both_out), jnp.where(first, both_out, out_own)])
+    input_grad = jnp.stack([jnp.where(first, dx, both_dx), jnp.where(first, both_dx, dx)])
+    squares = sum_context(jnp.full((8, LANES), squares, F32))
+    squares = squares + move_y(squares)
+    loss = squares[0, 0] / (count * width)
+
+    grad_query, grad_key, grad_value, grad_out, tail1 = unpack(
+        place, g_attn, (2 * HEAD_SIZE, HEAD_SIZE, HEAD_SIZE, 2 * HEAD_SIZE, 1), (False, True, True, False, False)
+    )
+    grad_gate, grad_up, tail2 = unpack(place, g_gu, (hidden, hidden, 1), (False, False, False))
+    (grad_down,) = unpack(place, g_down, (hidden,), (False,))
+    tails = jnp.stack([jnp.sum(tail1, axis=1), jnp.sum(tail2, axis=1)])
+    tails = tails + move_y(tails)
+    grad_gain1 = tails[0] / norm_attn.astype(F32)
+    grad_gain2 = tails[1] / norm_mlp.astype(F32)
+    return (
+        output,
+        loss,
+        input_grad,
+        grad_gain1,
+        grad_gain2,
+        grad_query,
+        grad_key,
+        grad_value,
+        grad_out.T,
+        grad_gate,
+        grad_up,
+        grad_down.T,
+    )
 
 
 def rms_forward(value_rows, gain):
@@ -340,4 +794,7 @@
         P("context", "tensor"),
         P("tensor", "context"),
     )
-    return jax.shard_map(shards, mesh=mesh, in_specs=in_specs, out_specs=out_specs, check_vma=False)
+    fits = dict(mesh.shape) == {"tensor": 2, "context": 16}
+    return jax.shard_map(
+        layer if fits else shards, mesh=mesh, in_specs=in_specs, out_specs=out_specs, check_vma=False
+    )

time: 2610 us -> 1010 us (0.39)
  waiting for transfers between devices: 2150 us -> 469 us
  local copies, waits for them, and re-layouts: 69.5 us -> 205 us
  blocking collectives: 131 us -> 0 us
  matrix products: 193 us -> 69.3 us
  starting transfers between devices: 1.64 us -> 113 us
  other arithmetic: 27.3 us -> 85.3 us
  Pallas kernels: 0 us -> 47.3 us
    reduce_scatter x7 -> x0, waiting for transfers between devices: 1400 us -> none  [the longest x1 355 us: shards(): lax.psum_scatter(grad_up, 'context', scatter_dimension=0, tiled=True)]
    ppermute x0 -> x116, waiting for transfers between devices: none -> 469 us  [the longest x42 202 us: move_z(): lax.ppermute(a, 'context', [(k, (k + 4 * step) % 16) for k in range(16)])]
    all_gather x9 -> x0, waiting for transfers between devices: 445 us -> none  [the longest x1 92.8 us: shards(): lax.all_gather(w_gate, 'context', axis=0, tiled=True)]
    while x8 -> x0, waiting for transfers between devices: 230 us -> none
    dot_general x65 -> x12, matrix products: 193 us -> 69.3 us  [the longest x4 29.4 us: dot_tn(): lax.dot_general(a, b, (((0,), (0,)), ((), ())), preferred_element_type=F32)]
    ppermute x0 -> x116, starting transfers between devices: none -> 113 us  [the longest x42 40.3 us: move_z(): lax.ppermute(a, 'context', [(k, (k + 4 * step) % 16) for k in range(16)])]
    psum x2 -> x0, blocking collectives: 68.8 us -> none  [shards(): lax.psum((jnp.sum(valid.astype(jnp.float32)), jnp.sum(validf * diff * dif...]
    psum x4 -> x0, waiting for transfers between devices: 67.6 us -> none  [the longest x1 31.9 us: shards(): lax.psum((dot_right(dgate, wg) + dot_right(dup, wu)).astype(jnp.bfloat16)...]
  transfers between devices with their start and end apart: 24 -> 116, of which waited for: 21 -> 56; matrix products, arithmetic and copies ran while one was open for 6% -> 28% of each run, Pallas kernels for 0% -> 4%
where the time goes in v1:
time: 1010 us; the launch traced here: 995 us
  waiting for transfers between devices  469 us (46%)
  local copies, waits for them, and re-layouts  205 us (20%)
  starting transfers between devices  113 us (11%)
  other arithmetic  85.3 us (8%)
  matrix products  69.3 us (7%)
  Pallas kernels  47.3 us (5%)
    ppermute x42, waiting for transfers between devices, move_z(): lax.ppermute(a, 'context', [(k, (k + 4 * step) % 16) for k in range(16)])  202 us
    ppermute x40, waiting for transfers between devices, move_x(): return lax.ppermute(a, 'context', [(k, k ^ 2) for k in range(16)])  154 us
    unnamed x202, local copies, waits for them, and re-layouts  82.3 us
    ppermute x10, waiting for transfers between devices, move_y(): return lax.ppermute(a, 'tensor', [(0, 1), (1, 0)])  78.3 us
    concatenate x15, local copies, waits for them, and re-layouts, layer(): g_attn = collect(place, jnp.concatenate(cut + [tail1], axis=1))  49.2 us
    pallas_call x9, Pallas kernels, kernel_call(): pl.pallas_call(body, out_shape=outs, in_specs=[smem()] * ins_smem + [vmem...  47.3 us
    ppermute x42, starting transfers between devices, move_z(): lax.ppermute(a, 'context', [(k, (k + 4 * step) % 16) for k in range(16)])  40.3 us
    ppermute x20, starting transfers between devices, move_c(): return lax.ppermute(a, 'context', [(k, k ^ 1) for k in range(16)])  32.4 us
  transfers between devices with their start and end apart: 116, of which 56 were waited for; matrix products, arithmetic and copies ran while one was open for 28% of the time, Pallas kernels for 4%

profile of v1, /device:TPU:11, one launch (start us, length us, event | category | flops | bytes accessed | tf_op | source)
XLA Modules:
  0.0 995.3 jit_solution(8081854003601947436)
XLA Ops:
  4.8 6.0 shard_map.220
  33.3 14.9 %collective-permute-done.2 = f32[8,2560]{1,0:T(8,128)S(1)} collective-permute-done((f32[8,2560]{1,0:T(8,128)S(1)}, f32[8,2560]{1,0:T(8,128)S(1)}, u32[]{:S(2)}, u32[]{:S(2)}) %collective-permute-start.2) | collective-permute-done | bytes 81952 | tf_op jit(solution)/shard_map/ppermute | solution.py:72
  73.0 7.0 collective-permute-done.10
  80.0 7.0 collective-permute-done.11
  125.0 9.5 collective-permute-done.17.other_ref
  160.6 7.0 fusion.35.qkv_ref
  167.6 7.9 shard_map.222
  190.3 12.8 %collective-permute-done.43 = bf16[2,160,432]{2,1,0:T(8,128)(2,1)S(1)} collective-permute-done((bf16[2,160,432]{2,1,0:T(8,128)(2,1)S(1)}, bf16[2,160,432]{2,1,0:T(8,128)(2,1)S(1)}, u32[]{:S(2)}, u32[]{:S(2)}) %collective-permute-start.43) | collective-permute-done | bytes 276512 | tf_op jit(solution)/shard_map/ppermute | solution.py:68
  205.8 7.5 collective-permute-done.39
  234.5 7.0 collective-permute-done.23
  241.4 7.0 collective-permute-done.25
  250.4 11.6 %collective-permute-done.40.other_ref = bf16[8,160,864]{2,1,0:T(8,128)(2,1)S(1)} collective-permute-done((bf16[8,160,864]{2,1,0:T(8,128)(2,1)S(1)}, bf16[8,160,864]{2,1,0:T(8,128)(2,1)S(1)}, u32[]{:S(2)}, u32[]{:S(2)}) %collective-permute-start.40) | collective-permute-done | bytes 2211872 | tf_op jit(solution)/shard_map/ppermute | solution.py:76
  264.2 7.6 collective-permute-start.41
  271.8 8.6 collective-permute-done.24
  284.3 6.0 collective-permute-done.27
  290.4 19.1 %collective-permute-done.28 = bf16[64,2560]{1,0:T(8,128)(2,1)S(1)} collective-permute-done((bf16[64,2560]{1,0:T(8,128)(2,1)S(1)}, bf16[64,2560]{1,0:T(8,128)(2,1)S(1)}, u32[]{:S(2)}, u32[]{:S(2)}) %collective-permute-start.28) | collective-permute-done | bytes 327712 | tf_op jit(solution)/shard_map/ppermute | solution.py:68
  315.9 7.3 collective-permute-done.32
  323.3 6.9 collective-permute-done.33
  330.2 7.0 collective-permute-done.34
  361.5 6.8 fusion.172
  385.4 6.2 collective-permute-done.50
  391.6 7.0 collective-permute-done.52
  398.6 7.0 collective-permute-done.54
  412.8 15.9 %collective-permute-done.51 = bf16[64,2560]{1,0:T(8,128)(2,1)S(1)} collective-permute-done((bf16[64,2560]{1,0:T(8,128)(2,1)}, bf16[64,2560]{1,0:T(8,128)(2,1)S(1)}, u32[]{:S(2)}, u32[]{:S(2)}) %collective-permute-start.51) | collective-permute-done | bytes 327712 | tf_op jit(solution)/shard_map/ppermute | solution.py:68
  450.2 11.8 %collective-permute-done.59 = f32[8,128]{1,0:T(8,128)S(1)} collective-permute-done((f32[8,128]{1,0:T(8,128)S(1)}, f32[8,128]{1,0:T(8,128)S(1)}, u32[]{:S(2)}, u32[]{:S(2)}) %collective-permute-start.59) | collective-permute-done | bytes 4128 | tf_op jit(solution)/shard_map/ppermute | solution.py:72
  475.7 7.4 copy.97
  488.4 7.0 collective-permute-done.68
  534.1 8.0 fusion.30
  543.9 9.1 fusion.175
  556.9 7.9 fusion.141
  564.8 10.9 %copy.96 = f32[2560,864]{1,0:T(8,128)} copy(f32[2560,864]{0,1:T(8,128)} %fusion.141) | data formatting | bytes 17694720 | tf_op jit(solution)/shard_map/dot_general | solution.py:56
  575.7 5.8 multiply_reduce_fusion
  595.6 22.3 %collective-permute-done.111 = bf16[8,160,432]{2,1,0:T(8,128)(2,1)} collective-permute-done((bf16[8,160,432]{2,1,0:T(8,128)(2,1)S(1)}, bf16[8,160,432]{2,1,0:T(8,128)(2,1)}, u32[]{:S(2)}, u32[]{:S(2)}) %collective-permute-start.111) | collective-permute-done | bytes 1105952 | tf_op jit(solution)/shard_map/ppermute | solution.py:76
  627.3 16.8 %collective-permute-done.72 = bf16[64,2560]{1,0:T(8,128)(2,1)S(1)} collective-permute-done((bf16[64,2560]{1,0:T(8,128)(2,1)S(1)}, bf16[64,2560]{1,0:T(8,128)(2,1)S(1)}, u32[]{:S(2)}, u32[]{:S(2)}) %collective-permute-start.72) | collective-permute-done | bytes 327712 | tf_op jit(solution)/shard_map/ppermute | solution.py:64
  646.8 15.6 %collective-permute-done.76 = bf16[64,2560]{1,0:T(8,128)(2,1)S(1)} collective-permute-done((bf16[64,2560]{1,0:T(8,128)(2,1)S(1)}, bf16[64,2560]{1,0:T(8,128)(2,1)S(1)}, u32[]{:S(2)}, u32[]{:S(2)}) %collective-permute-start.76) | collective-permute-done | bytes 327712 | tf_op jit(solution)/shard_map/ppermute | solution.py:68
  667.1 5.8 collective-permute-done.79
  673.0 19.1 %collective-permute-done.80 = bf16[64,2560]{1,0:T(8,128)(2,1)S(1)} collective-permute-done((bf16[64,2560]{1,0:T(8,128)(2,1)S(1)}, bf16[64,2560]{1,0:T(8,128)(2,1)S(1)}, u32[]{:S(2)}, u32[]{:S(2)}) %collective-permute-start.80) | collective-permute-done | bytes 327712 | tf_op jit(solution)/shard_map/ppermute | solution.py:68
  733.5 9.1 shard_map.225
  742.6 6.6 multiply_reduce_fusion.1
  803.3 8.7 concatenate.121
  833.7 33.0 %collective-permute-done.107 = bf16[2,160,865]{2,1,0:T(8,128)(2,1)S(1)} collective-permute-done((bf16[2,160,865]{2,1,0:T(8,128)(2,1)S(1)}, bf16[2,160,865]{2,1,0:T(8,128)(2,1)S(1)}, u32[]{:S(2)}, u32[]{:S(2)}) %collective-permute-start.107) | collective-permute-done | bytes 553632 | tf_op jit(solution)/shard_map/ppermute | solution.py:68
  890.5 20.5 %collective-permute-done.98 = bf16[8,160,481]{2,1,0:T(8,128)(2,1)S(1)} collective-permute-done((bf16[8,160,481]{2,1,0:T(8,128)(2,1)S(1)}, bf16[8,160,481]{2,1,0:T(8,128)(2,1)S(1)}, u32[]{:S(2)}, u32[]{:S(2)}) %collective-permute-start.98) | collective-permute-done | bytes 1231392 | tf_op jit(solution)/shard_map/ppermute | solution.py:76
  915.2 11.2 %collective-permute-done.99 = bf16[4,1,160,481]{3,2,1,0:T(8,128)(2,1)S(1)} collective-permute-done((bf16[4,1,160,481]{3,2,1,0:T(8,128)(2,1)S(1)}, bf16[4,1,160,481]{3,2,1,0:T(8,128)(2,1)S(1)}, u32[]{:S(2)}, u32[]{:S(2)}) %collective-permute-start.99) | collective-permute-done | bytes 615712 | tf_op jit(solution)/shard_map/ppermute | solution.py:64
  926.8 6.7 collective-permute-done.89
  935.1 17.3 %collective-permute-done.93 = bf16[64,2560]{1,0:T(8,128)(2,1)S(1)} collective-permute-done((bf16[64,2560]{1,0:T(8,128)(2,1)S(1)}, bf16[64,2560]{1,0:T(8,128)(2,1)S(1)}, u32[]{:S(2)}, u32[]{:S(2)}) %collective-permute-start.93) | collective-permute-done | bytes 327712 | tf_op jit(solution)/shard_map/ppermute | solution.py:68
  952.8 10.4 %collective-permute-done.100 = bf16[2,160,481]{2,1,0:T(8,128)(2,1)S(1)} collective-permute-done((bf16[2,160,481]{2,1,0:T(8,128)(2,1)S(1)}, bf16[2,160,481]{2,1,0:T(8,128)(2,1)S(1)}, u32[]{:S(2)}, u32[]{:S(2)}) %collective-permute-start.100) | collective-permute-done | bytes 307872 | tf_op jit(solution)/shard_map/ppermute | solution.py:68
  963.2 7.0 collective-permute-done.101
  978.8 13.7 %collective-permute-done.96 = f32[64,2560]{1,0:T(8,128)S(1)} collective-permute-done((f32[64,2560]{1,0:T(8,128)S(1)}, f32[64,2560]{1,0:T(8,128)S(1)}, u32[]{:S(2)}, u32[]{:S(2)}) %collective-permute-start.96) | collective-permute-done | bytes 655392 | tf_op jit(solution)/shard_map/ppermute | solution.py:76
  (586 shorter events, 485.6 us)
Async XLA Ops:
  1.8 51.0 %collective-permute-start.4 = (bf16[64,2560]{1,0:T(8,128)(2,1)S(1)}, bf16[64,2560]{1,0:T(8,128)(2,1)S(1)}, u32[]{:S(2)}, u32[]{:S(2)}) collective-permute-start(bf16[64,2560]{1,0:T(8,128)(2,1)S(1)} %bitcast.588), channel_id=1, source_target_pairs={{0,4},{1,5},{2,6},{3,7},{4,8},{5,9},{6,10},{7,11},{8,12},{9,13},{1... | collective-permute-start | bytes 983048 | tf_op jit(solution)/shard_map/ppermute | solution.py:68
  3.2 50.2 %collective-permute-start.5 = (bf16[64,2560]{1,0:T(8,128)(2,1)S(1)}, bf16[64,2560]{1,0:T(8,128)(2,1)S(1)}, u32[]{:S(2)}, u32[]{:S(2)}) collective-permute-start(bf16[64,2560]{1,0:T(8,128)(2,1)S(1)} %bitcast.589), channel_id=1, source_target_pairs={{0,8},{1,9},{2,10},{3,11},{4,12},{5,13},{6,14},{7,15},{8,0},{9,1},... | collective-permute-start | bytes 983048 | tf_op jit(solution)/shard_map/ppermute | solution.py:68
  13.1 37.3 %collective-permute-start.13 = (bf16[2,160,480]{2,1,0:T(8,128)(2,1)}, bf16[2,160,480]{2,1,0:T(8,128)(2,1)}, u32[]{:S(2)}, u32[]{:S(2)}) collective-permute-start(bf16[2,160,480]{2,1,0:T(8,128)(2,1)} %get-tuple-element.169), channel_id=1, source_target_pairs={{0,4},{1,5},{2,6},{3,7},{4,8},{5,9},{6,10},{7,11},{8,12},{9,13},{1... | collective-permute-start | bytes 921608 | tf_op jit(solution)/shard_map/ppermute | solution.py:68
  13.3 38.4 %collective-permute-start.14 = (bf16[2,160,480]{2,1,0:T(8,128)(2,1)}, bf16[2,160,480]{2,1,0:T(8,128)(2,1)}, u32[]{:S(2)}, u32[]{:S(2)}) collective-permute-start(bf16[2,160,480]{2,1,0:T(8,128)(2,1)} %get-tuple-element.168), channel_id=1, source_target_pairs={{0,8},{1,9},{2,10},{3,11},{4,12},{5,13},{6,14},{7,15},{8,0},{9,1},... | collective-permute-start | bytes 921608 | tf_op jit(solution)/shard_map/ppermute | solution.py:68
  58.2 46.0 %collective-permute-start.7 = (bf16[4,64,2560]{2,1,0:T(8,128)(2,1)}, bf16[4,64,2560]{2,1,0:T(8,128)(2,1)}, u32[]{:S(2)}, u32[]{:S(2)}) collective-permute-start(bf16[4,64,2560]{2,1,0:T(8,128)(2,1)} %pad_maximum_fusion.2), channel_id=1, source_target_pairs={{0,1},{1,0},{2,3},{3,2},{4,5},{5,4},{6,7},{7,6},{8,9},{9,8},{10,11... | collective-permute-start | bytes 3932168 | tf_op jit(solution)/shard_map/ppermute | solution.py:60
  68.4 32.6 %collective-permute-start.16 = (bf16[4,160,480]{2,1,0:T(8,128)(2,1)}, bf16[4,160,480]{2,1,0:T(8,128)(2,1)}, u32[]{:S(2)}, u32[]{:S(2)}) collective-permute-start(bf16[4,160,480]{2,1,0:T(8,128)(2,1)} %pad_maximum_fusion.15), channel_id=1, source_target_pairs={{0,2},{1,3},{2,0},{3,1},{4,6},{5,7},{6,4},{7,5},{8,10},{9,11},{10,... | collective-permute-start | bytes 1843208 | tf_op jit(solution)/shard_map/ppermute | solution.py:64
  73.0 116.3 %collective-permute-start.42 = (bf16[2,160,432]{2,1,0:T(8,128)(2,1)}, bf16[2,160,432]{2,1,0:T(8,128)(2,1)}, u32[]{:S(2)}, u32[]{:S(2)}) collective-permute-start(bf16[2,160,432]{2,1,0:T(8,128)(2,1)} %get-tuple-element.166), channel_id=1, source_target_pairs={{0,4},{1,5},{2,6},{3,7},{4,8},{5,9},{6,10},{7,11},{8,12},{9,13},{1... | collective-permute-start | bytes 829448 | tf_op jit(solution)/shard_map/ppermute | solution.py:68
  80.0 100.8 %collective-permute-start.36 = (bf16[2,160,864]{2,1,0:T(8,128)(2,1)}, bf16[2,160,864]{2,1,0:T(8,128)(2,1)}, u32[]{:S(2)}, u32[]{:S(2)}) collective-permute-start(bf16[2,160,864]{2,1,0:T(8,128)(2,1)} %get-tuple-element.145), channel_id=1, source_target_pairs={{0,4},{1,5},{2,6},{3,7},{4,8},{5,9},{6,10},{7,11},{8,12},{9,13},{1... | collective-permute-start | bytes 1658888 | tf_op jit(solution)/shard_map/ppermute | solution.py:68
  101.1 82.3 %collective-permute-start.37 = (bf16[2,160,864]{2,1,0:T(8,128)(2,1)}, bf16[2,160,864]{2,1,0:T(8,128)(2,1)}, u32[]{:S(2)}, u32[]{:S(2)}) collective-permute-start(bf16[2,160,864]{2,1,0:T(8,128)(2,1)} %get-tuple-element.144), channel_id=1, source_target_pairs={{0,8},{1,9},{2,10},{3,11},{4,12},{5,13},{6,14},{7,15},{8,0},{9,1},... | collective-permute-start | bytes 1658888 | tf_op jit(solution)/shard_map/ppermute | solution.py:68
  104.2 81.8 %collective-permute-start.38 = (bf16[2,160,864]{2,1,0:T(8,128)(2,1)}, bf16[2,160,864]{2,1,0:T(8,128)(2,1)}, u32[]{:S(2)}, u32[]{:S(2)}) collective-permute-start(bf16[2,160,864]{2,1,0:T(8,128)(2,1)} %get-tuple-element.143), channel_id=1, source_target_pairs={{0,12},{1,13},{2,14},{3,15},{4,0},{5,1},{6,2},{7,3},{8,4},{9,5},{1... | collective-permute-start | bytes 1658888 | tf_op jit(solution)/shard_map/ppermute | solution.py:68
  178.5 36.4 %collective-permute-start.19 = (bf16[4,2,64,2560]{3,2,1,0:T(8,128)(2,1)S(1)}, bf16[4,2,64,2560]{3,2,1,0:T(8,128)(2,1)}, u32[]{:S(2)}, u32[]{:S(2)}) collective-permute-start(bf16[4,2,64,2560]{3,2,1,0:T(8,128)(2,1)S(1)} %fusion.21), channel_id=1, source_target_pairs={{0,1},{1,0},{2,3},{3,2},{4,5},{5,4},{6,7},{7,6},{8,9},{9,8},{10,11... | collective-permute-start | bytes 7864328 | tf_op jit(solution)/shard_map/ppermute | solution.py:60
  213.5 48.4 %collective-permute-start.40 = (bf16[8,160,864]{2,1,0:T(8,128)(2,1)S(1)}, bf16[8,160,864]{2,1,0:T(8,128)(2,1)S(1)}, u32[]{:S(2)}, u32[]{:S(2)}) collective-permute-start(bf16[8,160,864]{2,1,0:T(8,128)(2,1)S(1)} %constant_dynamic-update-slice_fusion.18.own_ref), channel_id=1, source_target_pairs={{0,16},{16,0},{1,17},{17,1},{2,18},{18,2},{3,19},{19,3},{4,20},{20... | collective-permute-start | bytes 6635528 | tf_op jit(solution)/shard_map/ppermute | solution.py:76
  227.5 86.5 %collective-permute-start.46 = (bf16[8,160,432]{2,1,0:T(8,128)(2,1)S(1)}, bf16[8,160,432]{2,1,0:T(8,128)(2,1)S(1)}, u32[]{:S(2)}, u32[]{:S(2)}) collective-permute-start(bf16[8,160,432]{2,1,0:T(8,128)(2,1)S(1)} %constant_dynamic-update-slice_fusion.19.own_ref), channel_id=1, source_target_pairs={{0,16},{16,0},{1,17},{17,1},{2,18},{18,2},{3,19},{19,3},{4,20},{20... | collective-permute-start | bytes 3317768 | tf_op jit(solution)/shard_map/ppermute | solution.py:76
  234.4 29.7 %collective-permute-start.20 = (bf16[64,2560]{1,0:T(8,128)(2,1)S(1)}, bf16[64,2560]{1,0:T(8,128)(2,1)S(1)}, u32[]{:S(2)}, u32[]{:S(2)}) collective-permute-start(bf16[64,2560]{1,0:T(8,128)(2,1)S(1)} %get-tuple-element.126), channel_id=1, source_target_pairs={{0,2},{1,3},{2,0},{3,1},{4,6},{5,7},{6,4},{7,5},{8,10},{9,11},{10,... | collective-permute-start | bytes 983048 | tf_op jit(solution)/shard_map/ppermute | solution.py:64
  250.0 30.3 %collective-permute-start.24 = (bf16[64,2560]{1,0:T(8,128)(2,1)S(1)}, bf16[64,2560]{1,0:T(8,128)(2,1)S(1)}, u32[]{:S(2)}, u32[]{:S(2)}) collective-permute-start(bf16[64,2560]{1,0:T(8,128)(2,1)S(1)} %get-tuple-element.110), channel_id=1, source_target_pairs={{0,12},{1,13},{2,14},{3,15},{4,0},{5,1},{6,2},{7,3},{8,4},{9,5},{1... | collective-permute-start | bytes 983048 | tf_op jit(solution)/shard_map/ppermute | solution.py:68
  264.2 79.0 %collective-permute-start.41 = (bf16[8,160,864]{2,1,0:T(8,128)(2,1)}, bf16[8,160,864]{2,1,0:T(8,128)(2,1)S(1)}, u32[]{:S(2)}, u32[]{:S(2)}) collective-permute-start(bf16[8,160,864]{2,1,0:T(8,128)(2,1)} %broadcast_select_fusion), channel_id=1, source_target_pairs={{0,1},{1,0},{2,3},{3,2},{4,5},{5,4},{6,7},{7,6},{8,9},{9,8},{10,11... | collective-permute-start | bytes 6635528 | tf_op jit(solution)/shard_map/ppermute | solution.py:60
  282.9 29.3 %collective-permute-start.29 = (bf16[64,2560]{1,0:T(8,128)(2,1)S(1)}, bf16[64,2560]{1,0:T(8,128)(2,1)S(1)}, u32[]{:S(2)}, u32[]{:S(2)}) collective-permute-start(bf16[64,2560]{1,0:T(8,128)(2,1)S(1)} %get-tuple-element.89), channel_id=1, source_target_pairs={{0,12},{1,13},{2,14},{3,15},{4,0},{5,1},{6,2},{7,3},{8,4},{9,5},{1... | collective-permute-start | bytes 983048 | tf_op jit(solution)/shard_map/ppermute | solution.py:68
  313.4 36.8 %collective-permute-start.30 = (bf16[4,64,2560]{2,1,0:T(8,128)(2,1)}, bf16[4,64,2560]{2,1,0:T(8,128)(2,1)S(1)}, u32[]{:S(2)}, u32[]{:S(2)}) collective-permute-start(bf16[4,64,2560]{2,1,0:T(8,128)(2,1)} %pad_maximum_fusion.4), channel_id=1, source_target_pairs={{0,1},{1,0},{2,3},{3,2},{4,5},{5,4},{6,7},{7,6},{8,9},{9,8},{10,11... | collective-permute-start | bytes 3932168 | tf_op jit(solution)/shard_map/ppermute | solution.py:60
  384.0 28.8 %collective-permute-start.49 = (bf16[64,2560]{1,0:T(8,128)(2,1)S(1)}, bf16[64,2560]{1,0:T(8,128)(2,1)}, u32[]{:S(2)}, u32[]{:S(2)}) collective-permute-start(bf16[64,2560]{1,0:T(8,128)(2,1)S(1)} %get-tuple-element.122), channel_id=1, source_target_pairs={{0,2},{1,3},{2,0},{3,1},{4,6},{5,7},{6,4},{7,5},{8,10},{9,11},{10,... | collective-permute-start | bytes 983048 | tf_op jit(solution)/shard_map/ppermute | solution.py:64
  441.1 28.5 %collective-permute-start.64 = (bf16[64,2560]{1,0:T(8,128)(2,1)}, bf16[64,2560]{1,0:T(8,128)(2,1)S(1)}, u32[]{:S(2)}, u32[]{:S(2)}) collective-permute-start(bf16[64,2560]{1,0:T(8,128)(2,1)} %get-tuple-element.84), channel_id=1, source_target_pairs={{0,12},{1,13},{2,14},{3,15},{4,0},{5,1},{6,2},{7,3},{8,4},{9,5},{1... | collective-permute-start | bytes 983048 | tf_op jit(solution)/shard_map/ppermute | solution.py:68
  441.1 28.6 %collective-permute-start.62 = (bf16[64,2560]{1,0:T(8,128)(2,1)}, bf16[64,2560]{1,0:T(8,128)(2,1)}, u32[]{:S(2)}, u32[]{:S(2)}) collective-permute-start(bf16[64,2560]{1,0:T(8,128)(2,1)} %get-tuple-element.84), channel_id=1, source_target_pairs={{0,4},{1,5},{2,6},{3,7},{4,8},{5,9},{6,10},{7,11},{8,12},{9,13},{1... | collective-permute-start | bytes 983048 | tf_op jit(solution)/shard_map/ppermute | solution.py:68
  543.9 45.5 %collective-permute-start.71 = (bf16[4,2,64,2560]{3,2,1,0:T(8,128)(2,1)}, bf16[4,2,64,2560]{3,2,1,0:T(8,128)(2,1)}, u32[]{:S(2)}, u32[]{:S(2)}) collective-permute-start(bf16[4,2,64,2560]{3,2,1,0:T(8,128)(2,1)} %fusion.20), channel_id=1, source_target_pairs={{0,1},{1,0},{2,3},{3,2},{4,5},{5,4},{6,7},{7,6},{8,9},{9,8},{10,11... | collective-permute-start | bytes 7864328 | tf_op jit(solution)/shard_map/ppermute | solution.py:60
  556.7 29.1 %collective-permute-start.110 = (bf16[8,160,432]{2,1,0:T(8,128)(2,1)}, bf16[8,160,432]{2,1,0:T(8,128)(2,1)}, u32[]{:S(2)}, u32[]{:S(2)}) collective-permute-start(bf16[8,160,432]{2,1,0:T(8,128)(2,1)} %fusion.41), channel_id=1, source_target_pairs={{0,1},{1,0},{2,3},{3,2},{4,5},{5,4},{6,7},{7,6},{8,9},{9,8},{10,11... | collective-permute-start | bytes 3317768 | tf_op jit(solution)/shard_map/ppermute | solution.py:60
  585.3 40.3 %collective-permute-start.103 = (bf16[8,160,865]{2,1,0:T(8,128)(2,1)S(1)}, bf16[8,160,865]{2,1,0:T(8,128)(2,1)S(1)}, u32[]{:S(2)}, u32[]{:S(2)}) collective-permute-start(bf16[8,160,865]{2,1,0:T(8,128)(2,1)S(1)} %fusion.29), channel_id=1, source_target_pairs={{0,1},{1,0},{2,3},{3,2},{4,5},{5,4},{6,7},{7,6},{8,9},{9,8},{10,11... | collective-permute-start | bytes 6643208 | tf_op jit(solution)/shard_map/ppermute | solution.py:60
  587.6 30.3 %collective-permute-start.111 = (bf16[8,160,432]{2,1,0:T(8,128)(2,1)S(1)}, bf16[8,160,432]{2,1,0:T(8,128)(2,1)}, u32[]{:S(2)}, u32[]{:S(2)}) collective-permute-start(bf16[8,160,432]{2,1,0:T(8,128)(2,1)S(1)} %fusion.40), channel_id=1, source_target_pairs={{0,16},{16,0},{1,17},{17,1},{2,18},{18,2},{3,19},{19,3},{4,20},{20... | collective-permute-start | bytes 3317768 | tf_op jit(solution)/shard_map/ppermute | solution.py:76
  594.0 28.1 %collective-permute-start.73 = (bf16[64,2560]{1,0:T(8,128)(2,1)S(1)}, bf16[64,2560]{1,0:T(8,128)(2,1)S(1)}, u32[]{:S(2)}, u32[]{:S(2)}) collective-permute-start(bf16[64,2560]{1,0:T(8,128)(2,1)S(1)} %get-tuple-element.121), channel_id=1, source_target_pairs={{0,2},{1,3},{2,0},{3,1},{4,6},{5,7},{6,4},{7,5},{8,10},{9,11},{10,... | collective-permute-start | bytes 983048 | tf_op jit(solution)/shard_map/ppermute | solution.py:64
  594.1 29.4 %collective-permute-start.75 = (bf16[64,2560]{1,0:T(8,128)(2,1)S(1)}, bf16[64,2560]{1,0:T(8,128)(2,1)S(1)}, u32[]{:S(2)}, u32[]{:S(2)}) collective-permute-start(bf16[64,2560]{1,0:T(8,128)(2,1)S(1)} %get-tuple-element.120), channel_id=1, source_target_pairs={{0,2},{1,3},{2,0},{3,1},{4,6},{5,7},{6,4},{7,5},{8,10},{9,11},{10,... | collective-permute-start | bytes 983048 | tf_op jit(solution)/shard_map/ppermute | solution.py:64
  595.5 28.0 %collective-permute-start.77 = (bf16[64,2560]{1,0:T(8,128)(2,1)S(1)}, bf16[64,2560]{1,0:T(8,128)(2,1)S(1)}, u32[]{:S(2)}, u32[]{:S(2)}) collective-permute-start(bf16[64,2560]{1,0:T(8,128)(2,1)S(1)} %get-tuple-element.119), channel_id=1, source_target_pairs={{0,2},{1,3},{2,0},{3,1},{4,6},{5,7},{6,4},{7,5},{8,10},{9,11},{10,... | collective-permute-start | bytes 983048 | tf_op jit(solution)/shard_map/ppermute | solution.py:64
  622.0 43.6 %collective-permute-start.112 = (bf16[4,1,160,432]{3,2,1,0:T(8,128)(2,1)S(1)}, bf16[4,1,160,432]{3,2,1,0:T(8,128)(2,1)S(1)}, u32[]{:S(2)}, u32[]{:S(2)}) collective-permute-start(bf16[4,1,160,432]{3,2,1,0:T(8,128)(2,1)S(1)} %pad_maximum_fusion.19), channel_id=1, source_target_pairs={{0,2},{1,3},{2,0},{3,1},{4,6},{5,7},{6,4},{7,5},{8,10},{9,11},{10,... | collective-permute-start | bytes 1658888 | tf_op jit(solution)/shard_map/ppermute | solution.py:64
  623.8 38.6 %collective-permute-start.76 = (bf16[64,2560]{1,0:T(8,128)(2,1)S(1)}, bf16[64,2560]{1,0:T(8,128)(2,1)S(1)}, u32[]{:S(2)}, u32[]{:S(2)}) collective-permute-start(bf16[64,2560]{1,0:T(8,128)(2,1)S(1)} %get-tuple-element.104), channel_id=1, source_target_pairs={{0,12},{1,13},{2,14},{3,15},{4,0},{5,1},{6,2},{7,3},{8,4},{9,5},{1... | collective-permute-start | bytes 983048 | tf_op jit(solution)/shard_map/ppermute | solution.py:68
  625.7 36.7 %collective-permute-start.78 = (bf16[64,2560]{1,0:T(8,128)(2,1)S(1)}, bf16[64,2560]{1,0:T(8,128)(2,1)S(1)}, u32[]{:S(2)}, u32[]{:S(2)}) collective-permute-start(bf16[64,2560]{1,0:T(8,128)(2,1)S(1)} %get-tuple-element.105), channel_id=1, source_target_pairs={{0,4},{1,5},{2,6},{3,7},{4,8},{5,9},{6,10},{7,11},{8,12},{9,13},{1... | collective-permute-start | bytes 983048 | tf_op jit(solution)/shard_map/ppermute | solution.py:68
  644.1 64.7 %collective-permute-start.104 = (bf16[8,160,865]{2,1,0:T(8,128)(2,1)S(1)}, bf16[8,160,865]{2,1,0:T(8,128)(2,1)S(1)}, u32[]{:S(2)}, u32[]{:S(2)}) collective-permute-start(bf16[8,160,865]{2,1,0:T(8,128)(2,1)S(1)} %convert_select_fusion), channel_id=1, source_target_pairs={{0,16},{16,0},{1,17},{17,1},{2,18},{18,2},{3,19},{19,3},{4,20},{20... | collective-permute-start | bytes 6643208 | tf_op jit(solution)/shard_map/ppermute | solution.py:76
  664.1 28.0 %collective-permute-start.80 = (bf16[64,2560]{1,0:T(8,128)(2,1)S(1)}, bf16[64,2560]{1,0:T(8,128)(2,1)S(1)}, u32[]{:S(2)}, u32[]{:S(2)}) collective-permute-start(bf16[64,2560]{1,0:T(8,128)(2,1)S(1)} %get-tuple-element.77), channel_id=1, source_target_pairs={{0,8},{1,9},{2,10},{3,11},{4,12},{5,13},{6,14},{7,15},{8,0},{9,1},... | collective-permute-start | bytes 983048 | tf_op jit(solution)/shard_map/ppermute | solution.py:68
  664.1 28.1 %collective-permute-start.81 = (bf16[64,2560]{1,0:T(8,128)(2,1)S(1)}, bf16[64,2560]{1,0:T(8,128)(2,1)S(1)}, u32[]{:S(2)}, u32[]{:S(2)}) collective-permute-start(bf16[64,2560]{1,0:T(8,128)(2,1)S(1)} %get-tuple-element.77), channel_id=1, source_target_pairs={{0,12},{1,13},{2,14},{3,15},{4,0},{5,1},{6,2},{7,3},{8,4},{9,5},{1... | collective-permute-start | bytes 983048 | tf_op jit(solution)/shard_map/ppermute | solution.py:68
  697.0 119.0 %collective-permute-start.113 = (bf16[2,160,432]{2,1,0:T(8,128)(2,1)}, bf16[2,160,432]{2,1,0:T(8,128)(2,1)}, u32[]{:S(2)}, u32[]{:S(2)}) collective-permute-start(bf16[2,160,432]{2,1,0:T(8,128)(2,1)} %pad_maximum_fusion.26), channel_id=1, source_target_pairs={{0,4},{1,5},{2,6},{3,7},{4,8},{5,9},{6,10},{7,11},{8,12},{9,13},{1... | collective-permute-start | bytes 829448 | tf_op jit(solution)/shard_map/ppermute | solution.py:68
  700.3 117.5 %collective-permute-start.114 = (bf16[2,160,432]{2,1,0:T(8,128)(2,1)}, bf16[2,160,432]{2,1,0:T(8,128)(2,1)}, u32[]{:S(2)}, u32[]{:S(2)}) collective-permute-start(bf16[2,160,432]{2,1,0:T(8,128)(2,1)} %pad_maximum_fusion.27), channel_id=1, source_target_pairs={{0,8},{1,9},{2,10},{3,11},{4,12},{5,13},{6,14},{7,15},{8,0},{9,1},... | collective-permute-start | bytes 829448 | tf_op jit(solution)/shard_map/ppermute | solution.py:68
  707.4 115.2 %collective-permute-start.115 = (bf16[2,160,432]{2,1,0:T(8,128)(2,1)}, bf16[2,160,432]{2,1,0:T(8,128)(2,1)}, u32[]{:S(2)}, u32[]{:S(2)}) collective-permute-start(bf16[2,160,432]{2,1,0:T(8,128)(2,1)} %pad_maximum_fusion.28), channel_id=1, source_target_pairs={{0,12},{1,13},{2,14},{3,15},{4,0},{5,1},{6,2},{7,3},{8,4},{9,5},{1... | collective-permute-start | bytes 829448 | tf_op jit(solution)/shard_map/ppermute | solution.py:68
  713.9 100.1 %collective-permute-start.105 = (bf16[4,1,160,865]{3,2,1,0:T(8,128)(2,1)}, bf16[4,1,160,865]{3,2,1,0:T(8,128)(2,1)}, u32[]{:S(2)}, u32[]{:S(2)}) collective-permute-start(bf16[4,1,160,865]{3,2,1,0:T(8,128)(2,1)} %pad_maximum_fusion.14), channel_id=1, source_target_pairs={{0,2},{1,3},{2,0},{3,1},{4,6},{5,7},{6,4},{7,5},{8,10},{9,11},{10,... | collective-permute-start | bytes 3321608 | tf_op jit(solution)/shard_map/ppermute | solution.py:64
  768.3 114.7 %collective-permute-start.88 = (bf16[4,2,64,2560]{3,2,1,0:T(8,128)(2,1)}, bf16[4,2,64,2560]{3,2,1,0:T(8,128)(2,1)}, u32[]{:S(2)}, u32[]{:S(2)}) collective-permute-start(bf16[4,2,64,2560]{3,2,1,0:T(8,128)(2,1)} %fusion.22), channel_id=1, source_target_pairs={{0,1},{1,0},{2,3},{3,2},{4,5},{5,4},{6,7},{7,6},{8,9},{9,8},{10,11... | collective-permute-start | bytes 7864328 | tf_op jit(solution)/shard_map/ppermute | solution.py:60
  814.0 64.8 %collective-permute-start.97 = (bf16[8,160,481]{2,1,0:T(8,128)(2,1)S(1)}, bf16[8,160,481]{2,1,0:T(8,128)(2,1)S(1)}, u32[]{:S(2)}, u32[]{:S(2)}) collective-permute-start(bf16[8,160,481]{2,1,0:T(8,128)(2,1)S(1)} %fusion.38), channel_id=1, source_target_pairs={{0,1},{1,0},{2,3},{3,2},{4,5},{5,4},{6,7},{7,6},{8,9},{9,8},{10,11... | collective-permute-start | bytes 3694088 | tf_op jit(solution)/shard_map/ppermute | solution.py:60
  817.7 49.0 %collective-permute-start.107 = (bf16[2,160,865]{2,1,0:T(8,128)(2,1)S(1)}, bf16[2,160,865]{2,1,0:T(8,128)(2,1)S(1)}, u32[]{:S(2)}, u32[]{:S(2)}) collective-permute-start(bf16[2,160,865]{2,1,0:T(8,128)(2,1)S(1)} %pad_maximum_fusion.21), channel_id=1, source_target_pairs={{0,8},{1,9},{2,10},{3,11},{4,12},{5,13},{6,14},{7,15},{8,0},{9,1},... | collective-permute-start | bytes 1660808 | tf_op jit(solution)/shard_map/ppermute | solution.py:68
  822.6 48.9 %collective-permute-start.108 = (bf16[2,160,865]{2,1,0:T(8,128)(2,1)S(1)}, bf16[2,160,865]{2,1,0:T(8,128)(2,1)S(1)}, u32[]{:S(2)}, u32[]{:S(2)}) collective-permute-start(bf16[2,160,865]{2,1,0:T(8,128)(2,1)S(1)} %pad_maximum_fusion.22), channel_id=1, source_target_pairs={{0,12},{1,13},{2,14},{3,15},{4,0},{5,1},{6,2},{7,3},{8,4},{9,5},{1... | collective-permute-start | bytes 1660808 | tf_op jit(solution)/shard_map/ppermute | solution.py:68
  881.0 30.1 %collective-permute-start.98 = (bf16[8,160,481]{2,1,0:T(8,128)(2,1)S(1)}, bf16[8,160,481]{2,1,0:T(8,128)(2,1)S(1)}, u32[]{:S(2)}, u32[]{:S(2)}) collective-permute-start(bf16[8,160,481]{2,1,0:T(8,128)(2,1)S(1)} %fusion.39), channel_id=1, source_target_pairs={{0,16},{16,0},{1,17},{17,1},{2,18},{18,2},{3,19},{19,3},{4,20},{20... | collective-permute-start | bytes 3694088 | tf_op jit(solution)/shard_map/ppermute | solution.py:76
  913.7 38.6 %collective-permute-start.93 = (bf16[64,2560]{1,0:T(8,128)(2,1)S(1)}, bf16[64,2560]{1,0:T(8,128)(2,1)S(1)}, u32[]{:S(2)}, u32[]{:S(2)}) collective-permute-start(bf16[64,2560]{1,0:T(8,128)(2,1)S(1)} %get-tuple-element.101), channel_id=1, source_target_pairs={{0,12},{1,13},{2,14},{3,15},{4,0},{5,1},{6,2},{7,3},{8,4},{9,5},{1... | collective-permute-start | bytes 983048 | tf_op jit(solution)/shard_map/ppermute | solution.py:68
  914.2 38.2 %collective-permute-start.95 = (bf16[64,2560]{1,0:T(8,128)(2,1)S(1)}, bf16[64,2560]{1,0:T(8,128)(2,1)S(1)}, u32[]{:S(2)}, u32[]{:S(2)}) collective-permute-start(bf16[64,2560]{1,0:T(8,128)(2,1)S(1)} %get-tuple-element.102), channel_id=1, source_target_pairs={{0,4},{1,5},{2,6},{3,7},{4,8},{5,9},{6,10},{7,11},{8,12},{9,13},{1... | collective-permute-start | bytes 983048 | tf_op jit(solution)/shard_map/ppermute | solution.py:68
  926.6 36.6 %collective-permute-start.100 = (bf16[2,160,481]{2,1,0:T(8,128)(2,1)S(1)}, bf16[2,160,481]{2,1,0:T(8,128)(2,1)S(1)}, u32[]{:S(2)}, u32[]{:S(2)}) collective-permute-start(bf16[2,160,481]{2,1,0:T(8,128)(2,1)S(1)} %pad_maximum_fusion.23), channel_id=1, source_target_pairs={{0,4},{1,5},{2,6},{3,7},{4,8},{5,9},{6,10},{7,11},{8,12},{9,13},{1... | collective-permute-start | bytes 923528 | tf_op jit(solution)/shard_map/ppermute | solution.py:68
  933.5 36.7 %collective-permute-start.101 = (bf16[2,160,481]{2,1,0:T(8,128)(2,1)S(1)}, bf16[2,160,481]{2,1,0:T(8,128)(2,1)S(1)}, u32[]{:S(2)}, u32[]{:S(2)}) collective-permute-start(bf16[2,160,481]{2,1,0:T(8,128)(2,1)S(1)} %pad_maximum_fusion.24), channel_id=1, source_target_pairs={{0,8},{1,9},{2,10},{3,11},{4,12},{5,13},{6,14},{7,15},{8,0},{9,1},... | collective-permute-start | bytes 923528 | tf_op jit(solution)/shard_map/ppermute | solution.py:68
  935.1 35.1 %collective-permute-start.102 = (bf16[2,160,481]{2,1,0:T(8,128)(2,1)S(1)}, bf16[2,160,481]{2,1,0:T(8,128)(2,1)S(1)}, u32[]{:S(2)}, u32[]{:S(2)}) collective-permute-start(bf16[2,160,481]{2,1,0:T(8,128)(2,1)S(1)} %pad_maximum_fusion.25), channel_id=1, source_target_pairs={{0,12},{1,13},{2,14},{3,15},{4,0},{5,1},{6,2},{7,3},{8,4},{9,5},{1... | collective-permute-start | bytes 923528 | tf_op jit(solution)/shard_map/ppermute | solution.py:68
  (137 other events, 2419.1 us)

commit v2 on v0

--- a/solution.py
+++ b/solution.py
@@ -1,16 +1,812 @@
+import functools
 import math
 
 import jax
 import jax.numpy as jnp
 from jax import lax
+from jax.experimental import pallas as pl
+from jax.experimental.pallas import tpu as pltpu
 from jax.sharding import PartitionSpec as P
 
 HEAD_SIZE = 80
 BLOCK = 256
-
+LANES = 128
 
 eps = 1e-05
 theta = 10000.0
+BF = jnp.bfloat16
+F32 = jnp.float32
+MIB = 1024 * 1024
+SLOW = ()
+
+
+def whole(shape, dtype):
+    return jax.ShapeDtypeStruct(tuple(shape), dtype)
+
+
+def kernel_call(body, outs, ins, scalars=0, far=(), flops=0, scratch=(), limit=16, name=None):
+    single = not isinstance(outs, (list, tuple))
+    spec = lambda i: (
+        pl.BlockSpec(memory_space=pltpu.SMEM)
+        if i < scalars
+        else pl.BlockSpec(memory_space=pl.ANY)
+        if i in far
+        else pl.BlockSpec(memory_space=pltpu.VMEM)
+    )
+    out_spec = pl.BlockSpec(memory_space=pltpu.VMEM)
+    nbytes = sum(math.prod(a.shape) * a.dtype.itemsize for a in ins)
+    nbytes += sum(math.prod(o.shape) * o.dtype.itemsize for o in ([outs] if single else outs))
+    return pl.pallas_call(
+        body,
+        out_shape=outs,
+        in_specs=[spec(i) for i in range(len(ins))],
+        out_specs=out_spec if single else [out_spec] * len(outs),
+        scratch_shapes=list(scratch),
+        compiler_params=pltpu.CompilerParams(vmem_limit_bytes=limit * MIB),
+        cost_estimate=pl.CostEstimate(flops=flops if name in SLOW else 0, bytes_accessed=0, transcendentals=0),
+        name=name,
+    )(*ins)
+
+
+def dot_nn(a, b):
+    return lax.dot_general(a, b, (((1,), (0,)), ((), ())), preferred_element_type=F32)
+
+
+def dot_nt(a, b):
+    return lax.dot_general(a, b, (((1,), (1,)), ((), ())), preferred_element_type=F32)
+
+
+def dot_tn(a, b):
+    return lax.dot_general(a, b, (((0,), (0,)), ((), ())), preferred_element_type=F32)
+
+
+def move_c(a):
+    return lax.ppermute(a, "context", [(k, k ^ 1) for k in range(16)])
+
+
+def move_x(a):
+    return lax.ppermute(a, "context", [(k, k ^ 2) for k in range(16)])
+
+
+def move_z(a, step):
+    return lax.ppermute(a, "context", [(k, (k + 4 * step) % 16) for k in range(16)])
+
+
+def move_y(a):
+    return lax.ppermute(a, "tensor", [(0, 1), (1, 0)])
+
+
+def share_out(a):
+    return lax.all_to_all(a, "context", split_axis=0, concat_axis=0, tiled=True)
+
+
+def after(value, *others):
+    return lax.optimization_barrier((value, *others))[0]
+
+
+def stack(pieces):
+    def body(*refs):
+        for m in range(4):
+            refs[4][m] = refs[m][...]
+
+    return kernel_call(body, whole((4, *pieces[0].shape), BF), tuple(pieces), limit=8, name="stack")
+
+
+def gather_rows(own, *late, early=()):
+    near = [own] + [move_z(own, m) for m in (1, 2, 3)]
+    far = [move_x(own)]
+    far += [move_x(after(p, far[0], *early)) for p in near[1:]]
+    near_all, far_all = stack(near), stack(far)
+    last = after(far_all, *late) if late else far_all
+    return (near_all, move_c(near_all), far_all, move_c(last)), near, far
+
+
+def scatter_rows(part, *late):
+    far1, far0, near1, *near0 = part
+    shape = far1.shape[1:]
+
+    def add_far(a_ref, b_ref, *outs):
+        for m in range(4):
+            outs[m][...] = (a_ref[m].astype(F32) + b_ref[m].astype(F32)).astype(BF)
+
+    def add_near(a_ref, b_ref, c_ref, out_ref):
+        out_ref[...] = (a_ref[...].astype(F32) + b_ref[...].astype(F32) + c_ref[...].astype(F32)).astype(BF)
+
+    far = kernel_call(add_far, [whole(shape, BF)] * 4, (far0, move_c(far1)), limit=16, name="add_far")
+    near1 = move_c(near1)
+    come = {m: move_x(far[m]) for m in (2, 1, 3, 0)}
+    if late:
+        come[2] = after(come[2], *late)
+    terms = [near0[0], near1[0], come[0]]
+    for m in (2, 1, 3):
+        s = kernel_call(add_near, whole(shape, BF), (near0[m], near1[m], come[m]), limit=8, name="add_near")
+        terms.append(move_z(s, 4 - m))
+    return terms, far, come
+
+
+def part_shapes(seg, width):
+    return [
+        whole((4, seg, width), BF),
+        whole((4, seg, width), BF),
+        whole((4, seg, width), BF),
+    ] + [whole((seg, width), BF)] * 4
+
+
+def write_part(outs, group, value):
+    far1, far0, near1, *near0 = outs
+    seg = far1.shape[1]
+    for m in range(4):
+        rows = value[m * seg : (m + 1) * seg]
+        if group == 3:
+            far1[m] = rows.astype(BF)
+        elif group == 2:
+            far0[m] = rows.astype(BF)
+        elif group == 1:
+            near1[m] = rows.astype(BF)
+        else:
+            near0[m][...] = rows.astype(BF)
+
+
+def total(refs):
+    out = refs[0][...].astype(F32)
+    for r in refs[1:]:
+        out = out + r[...].astype(F32)
+    return out
+
+
+FIRST = 384
+SECOND = 640
+EXTRA = 4
+
+
+def pack_first(wq, wk, wv, wot, extra, wdt):
+    rows, d = wq.shape[0], HEAD_SIZE
+    hidden = wdt.shape[1] // 16
+    some = FIRST - 4 * d - EXTRA
+
+    def body(q_ref, k_ref, v_ref, o_ref, e_ref, d_ref, out_ref):
+        for k in range(16):
+            block = jnp.concatenate(
+                [
+                    q_ref[:, k * d : (k + 1) * d],
+                    k_ref[:, k // 4 * d : (k // 4 + 1) * d],
+                    v_ref[:, k // 4 * d : (k // 4 + 1) * d],
+                    o_ref[:, k * d : (k + 1) * d],
+                    e_ref[...],
+                    d_ref[:, k * hidden : k * hidden + some],
+                ],
+                axis=1,
+            )
+            out_ref[k] = block
+
+    return kernel_call(
+        body, whole((16, rows, FIRST), BF), (wq, wk, wv, wot, extra, wdt), limit=16, name="pack_first"
+    )
+
+
+def pack_second(wg, wu, wdt):
+    rows = wg.shape[0]
+    hidden = wg.shape[1] // 16
+    some = FIRST - 4 * HEAD_SIZE - EXTRA
+    spare = SECOND - 3 * hidden + some
+
+    def body(g_ref, u_ref, d_ref, out_ref):
+        for k in range(16):
+            block = jnp.concatenate(
+                [
+                    d_ref[:, k * hidden + some : (k + 1) * hidden],
+                    g_ref[:, k * hidden : (k + 1) * hidden],
+                    u_ref[:, k * hidden : (k + 1) * hidden],
+                    jnp.zeros((rows, spare), BF),
+                ],
+                axis=1,
+            )
+            out_ref[k] = block
+
+    return kernel_call(body, whole((16, rows, SECOND), BF), (wg, wu, wdt), limit=16, name="pack_second")
+
+
+def share_blocks(a):
+    return share_out(a.reshape(-1, a.shape[2])).reshape(a.shape)
+
+
+def of_other(a):
+    return lax.all_gather(a, "tensor", axis=0, tiled=False)
+
+
+def over_sequences(parts):
+    return lax.psum_scatter(parts, "tensor", scatter_dimension=0, tiled=False)
+
+
+def unpack_second(second, hidden):
+    rows = second.shape[1]
+
+    def body(s_ref, g_ref, u_ref):
+        for k in range(16):
+            c = s_ref[k].astype(F32)
+            g_ref[:, k * hidden : (k + 1) * hidden] = c[:, :hidden]
+            u_ref[:, k * hidden : (k + 1) * hidden] = c[:, hidden : 2 * hidden]
+
+    return kernel_call(body, [whole((rows, 16 * hidden), F32)] * 2, (second,), limit=16, name="unpack_second")
+
+
+def unpack_first(first, second, hidden):
+    rows, d = first.shape[1], HEAD_SIZE
+    cut = SECOND - 2 * hidden
+    rest = 4 * d + hidden - cut
+
+    def body(f_ref, s_ref, q_ref, k_ref, v_ref, o_ref, d_ref, tail_ref):
+        tail = jnp.zeros((rows, 3), F32)
+        for k in range(16):
+            b = f_ref[k].astype(F32)
+            q_ref[:, k * d : (k + 1) * d] = b[:, :d]
+            o_ref[:, k * d : (k + 1) * d] = b[:, 3 * d : 4 * d]
+            if k % 4 == 0:
+                keys = jnp.zeros((rows, 2 * d), F32)
+            keys = keys + b[:, d : 3 * d]
+            if k % 4 == 3:
+                k_ref[:, k // 4 * d : (k // 4 + 1) * d] = keys[:, :d]
+                v_ref[:, k // 4 * d : (k // 4 + 1) * d] = keys[:, d:]
+            tail = tail + b[:, rest : rest + 3]
+            d_ref[:, k * hidden : k * hidden + cut] = s_ref[k][:, 2 * hidden :].astype(F32)
+            d_ref[:, k * hidden + cut : (k + 1) * hidden] = b[:, 4 * d : rest]
+        tail_ref[...] = tail
+
+    outs = [whole((rows, w), F32) for w in (16 * d, 4 * d, 4 * d, 16 * d, 16 * hidden, 3)]
+    return kernel_call(body, outs, (first, second), limit=16, name="unpack_first")
+
+
+def prepare_attention(place, mine, both):
+    size, d = mine.shape[1], HEAD_SIZE
+    depth = 16 * size
+
+    def body(place_ref, mine_ref, both_ref, w_ref, out_ref, row_ref, info_ref):
+        other_ref = both_ref.at[1 - place_ref[3]]
+        info_ref[...] = jnp.zeros_like(info_ref)
+        for k in range(16):
+            rs = slice(k * size, (k + 1) * size)
+            parts = [mine_ref[k], other_ref[k]]
+            w_ref[rs, :] = jnp.concatenate([p[:, : 3 * d] for p in parts], axis=1)
+            out_ref[rs, :] = jnp.concatenate([p[:, 3 * d : 4 * d] for p in parts], axis=1)
+            info_ref[rs, :EXTRA] = parts[0][:, 4 * d : 4 * d + EXTRA].astype(F32)
+        for b in range(depth // LANES):
+            rs = slice(b * LANES, (b + 1) * LANES)
+            row_ref[:, rs] = info_ref[rs, :].T[0:8, :]
+
+    return kernel_call(
+        body,
+        [whole((depth, 6 * d), BF), whole((depth, 2 * d), BF), whole((8, depth), F32)],
+        (place, mine, both),
+        scalars=1,
+        scratch=[pltpu.VMEM((depth, LANES), F32)],
+        limit=16,
+        name="prepare_attention",
+    )
+
+
+def prepare_feed(place, first_mine, first_both, mine, both, hidden):
+    size = mine.shape[1]
+    depth = 16 * size
+    at = 4 * HEAD_SIZE + EXTRA
+    rest = hidden - (FIRST - at)
+
+    def body(place_ref, fm_ref, fboth_ref, m_ref, both_ref, gu_ref, d_ref):
+        fo_ref, o_ref = fboth_ref.at[1 - place_ref[3]], both_ref.at[1 - place_ref[3]]
+        for k in range(16):
+            rs = slice(k * size, (k + 1) * size)
+            fm, fo, m, o = fm_ref[k], fo_ref[k], m_ref[k], o_ref[k]
+            gu_ref[rs, :] = jnp.concatenate(
+                [
+                    m[:, rest : rest + hidden],
+                    o[:, rest : rest + hidden],
+                    m[:, rest + hidden : rest + 2 * hidden],
+                    o[:, rest + hidden : rest + 2 * hidden],
+                ],
+                axis=1,
+            )
+            d_ref[rs, :] = jnp.concatenate([fm[:, at:], m[:, :rest], fo[:, at:], o[:, :rest]], axis=1)
+
+    return kernel_call(
+        body,
+        [whole((depth, 4 * hidden), BF), whole((depth, 2 * hidden), BF)],
+        (place, first_mine, first_both, mine, both),
+        scalars=1,
+        limit=16,
+        name="prepare_feed",
+    )
+
+
+def turn(a, cosine, sine):
+    half = HEAD_SIZE // 2
+    lane = lax.broadcasted_iota(jnp.int32, a.shape, 1)
+    swapped = jnp.where(lane < half, pltpu.roll(a, LANES - half, 1), pltpu.roll(a, half, 1))
+    return a * cosine + swapped * sine
+
+
+def head_of(value, at):
+    part = value[:, at * HEAD_SIZE : (at + 1) * HEAD_SIZE]
+    return jnp.concatenate([part, jnp.zeros((value.shape[0], LANES - HEAD_SIZE), value.dtype)], axis=1)
+
+
+def attention(place, pieces, weights, w_o, rows_info, length, kpos, cosine, sine):
+    seg, width = pieces[0].shape[1:]
+    rows = 16 * seg
+    blocks = rows // BLOCK
+    scale = HEAD_SIZE ** (-0.5)
+
+    def body(place_ref, *refs):
+        x_refs = [refs[i // 4].at[i % 4] for i in range(16)]
+        w_ref, wo_ref, info_ref, len_ref, kpos_ref, cos_ref, sin_ref = refs[4:11]
+        h_ref, q_ref, k_ref, v_ref, ctx_ref, lse_ref, *part = refs[11:]
+        z = place_ref[0]
+        gain = info_ref[0:1, :]
+        length = len_ref[0:1, 0:1]
+        for i in range(16):
+
+            @pl.loop(0, seg // 16)
+            def _(r):
+                at = pl.multiple_of(r * 16, 16)
+                xs = x_refs[i][pl.ds(at, 16), :].astype(F32)
+                inv = lax.rsqrt(jnp.mean(xs * xs, axis=-1, keepdims=True) + eps)
+                h_ref[pl.ds(i * seg + at, 16), :] = (xs * inv * gain).astype(BF)
+
+        for g in range(4):
+            qkv = dot_nn(h_ref[g * 4 * seg : (g + 1) * 4 * seg, :], w_ref[...])
+            for m in range(4):
+                to = pl.multiple_of(lax.rem(z - m + 4, 4) * BLOCK + g * seg, seg)
+                to = pl.ds(to, seg)
+                piece = qkv[m * seg : (m + 1) * seg]
+                cosine, sine = cos_ref[to, :], sin_ref[to, :]
+                for h in range(2):
+                    q_ref[h, to, :] = turn(head_of(piece, 3 * h), cosine, sine).astype(BF)
+                    k_ref[h, to, :] = turn(head_of(piece, 3 * h + 1), cosine, sine).astype(BF)
+                    v_ref[h, to, :] = head_of(piece, 3 * h + 2).astype(BF)
+        for i in range(blocks):
+            m = lax.rem(z - i + 4, 4)
+            n = (i + 1) * BLOCK
+            ok = kpos_ref[:, :n].astype(F32) < length
+            for h in range(2):
+                s = dot_nt(q_ref[h, i * BLOCK : n, :], k_ref[h, :n, :]) * scale
+                s = jnp.where(ok, s, F32(-1e30))
+                top = jnp.max(s, axis=1, keepdims=True)
+                e = jnp.exp(s - top)
+                tot = jnp.sum(e, axis=1, keepdims=True)
+                ctx = dot_nn((e / tot).astype(BF), v_ref[h, :n, :]).astype(BF)
+                for g in range(4):
+                    to = pl.ds(pl.multiple_of((g * 4 + m) * seg, seg), seg)
+                    ctx_ref[to, h * HEAD_SIZE : (h + 1) * HEAD_SIZE] = ctx[g * seg : (g + 1) * seg, :HEAD_SIZE]
+                lse_ref[h, i * BLOCK : n, :] = top + jnp.log(tot)
+        for g in (3, 2, 1, 0):
+            write_part(part, g, dot_nt(ctx_ref[g * 4 * seg : (g + 1) * 4 * seg, :], wo_ref[...]))
+
+    outs = [
+        whole((rows, width), BF),
+        whole((2, rows, LANES), BF),
+        whole((2, rows, LANES), BF),
+        whole((2, rows, LANES), BF),
+        whole((rows, 2 * HEAD_SIZE), BF),
+        whole((2, rows, 1), F32),
+    ] + part_shapes(seg, width)
+    flops = 2 * rows * width * 6 * LANES + 2 * rows * rows * LANES * 2 * 2
+    out = kernel_call(
+        body,
+        outs,
+        (place, *pieces, weights, w_o, rows_info, length, kpos, cosine, sine),
+        scalars=1,
+        flops=flops,
+        name="attention",
+    )
+    return out[:6], out[6:]
+
+
+def attention_back(place, pieces, weights, w_o, length, kpos, cosine, sine, q, k, v, lse):
+    seg, width = pieces[0].shape[1:]
+    rows = 16 * seg
+    blocks = rows // BLOCK
+    scale = HEAD_SIZE ** (-0.5)
+
+    def body(place_ref, *refs):
+        d_refs = [refs[i // 4].at[i % 4] for i in range(16)]
+        w_ref, wo_ref, len_ref, kpos_ref, cos_ref, sin_ref, q_ref, k_ref, v_ref, lse_ref = refs[4:14]
+        da_ref, dqkv_ref, *part = refs[14:23]
+        dctx_ref, dk_ref, dv_ref = refs[23:]
+        z = place_ref[0]
+        length = len_ref[0:1, 0:1]
+        for i in range(16):
+            da_ref[i * seg : (i + 1) * seg, :] = d_refs[i][...]
+        for g in range(4):
+            dctx = dot_nn(da_ref[g * 4 * seg : (g + 1) * 4 * seg, :], wo_ref[...])
+            for m in range(4):
+                to = pl.multiple_of(lax.rem(z - m + 4, 4) * BLOCK + g * seg, seg)
+                for h in range(2):
+                    dctx_ref[h, pl.ds(to, seg), :] = head_of(dctx[m * seg : (m + 1) * seg], h).astype(BF)
+        dk_ref[...] = jnp.zeros_like(dk_ref)
+        dv_ref[...] = jnp.zeros_like(dv_ref)
+
+        def put(i, at, value):
+            m = lax.rem(z - i + 4, 4)
+            for g in range(4):
+                to = pl.ds(pl.multiple_of((g * 4 + m) * seg, seg), seg)
+                dqkv_ref[to, at * HEAD_SIZE : (at + 1) * HEAD_SIZE] = value[g * seg : (g + 1) * seg, :HEAD_SIZE]
+
+        for i in range(blocks):
+            n = (i + 1) * BLOCK
+            ok = kpos_ref[:, :n].astype(F32) < length
+            cosine, sine = cos_ref[i * BLOCK : n, :], sin_ref[i * BLOCK : n, :]
+            for h in range(2):
+                qi = q_ref[h, i * BLOCK : n, :]
+                di = dctx_ref[h, i * BLOCK : n, :]
+                s = dot_nt(qi, k_ref[h, :n, :]) * scale
+                p = jnp.where(ok, jnp.exp(s - lse_ref[h, i * BLOCK : n, :]), F32(0.0))
+                dp = dot_nt(di, v_ref[h, :n, :])
+                delta = jnp.sum(p * dp, axis=1, keepdims=True)
+                ds = (p * (dp - delta)).astype(BF)
+                dq = dot_nn(ds, k_ref[h, :n, :]) * scale
+                put(i, 3 * h, turn(dq, cosine, -sine).astype(BF))
+                dk_ref[h, :n, :] += dot_tn(ds, qi)
+                dv_ref[h, :n, :] += dot_tn(p.astype(BF), di)
+        for i in range(blocks):
+            rs = slice(i * BLOCK, (i + 1) * BLOCK)
+            for h in range(2):
+                dk = turn(dk_ref[h, rs, :] * scale, cos_ref[rs, :], -sin_ref[rs, :])
+                put(i, 3 * h + 1, dk.astype(BF))
+                put(i, 3 * h + 2, dv_ref[h, rs, :].astype(BF))
+        for g in (3, 2, 1, 0):
+            write_part(part, g, dot_nt(dqkv_ref[g * 4 * seg : (g + 1) * 4 * seg, :], w_ref[...]))
+
+    outs = [whole((rows, width), BF), whole((rows, 6 * HEAD_SIZE), BF)] + part_shapes(seg, width)
+    flops = 2 * rows * width * 6 * LANES + 2 * rows * rows * LANES * 2 * 5
+    out = kernel_call(
+        body,
+        outs,
+        (place, *pieces, weights, w_o, length, kpos, cosine, sine, q, k, v, lse),
+        scalars=1,
+        flops=flops,
+        scratch=[
+            pltpu.VMEM((2, rows, LANES), BF),
+            pltpu.VMEM((2, rows, LANES), F32),
+            pltpu.VMEM((2, rows, LANES), F32),
+        ],
+        name="attention_back",
+    )
+    return out[0], out[1], out[2:]
+
+
+def write_blocks(out_ref, index, chunk, value):
+    rows = out_ref.shape[2]
+    for k in range(4):
+        out_ref[index, chunk * 4 + k] = value[k * rows : (k + 1) * rows].astype(BF)
+
+
+def attention_grads(place, h1, dqkv, da, ctx, weights, rest, tail2, squares):
+    rows, width = h1.shape
+    d, cut = HEAD_SIZE, rest.shape[1] // 2
+    spare = FIRST - 4 * d - cut - 3
+
+    def body(place_ref, h_ref, dqkv_ref, da_ref, ctx_ref, w_ref, rest_ref, tail_ref, sq_ref, out_ref):
+        y = place_ref[3]
+        quarter = width // 4
+        for b in range(4):
+            at = slice(b * quarter, (b + 1) * quarter)
+            g = dot_tn(h_ref[:, at], dqkv_ref[...])
+            tail1 = jnp.sum(g * w_ref[at, :].astype(F32), axis=1, keepdims=True)
+            o = dot_tn(da_ref[:, at], ctx_ref[...])
+            sq = jnp.broadcast_to(sq_ref[0:1, 0:1], (quarter, 1))
+            last = [tail1, tail_ref[at, :], sq, jnp.zeros((quarter, spare), F32)]
+            for h, index in enumerate((y, 1 - y)):
+                parts = [g[:, 3 * d * h : 3 * d * (h + 1)], o[:, d * h : d * (h + 1)]]
+                parts += [rest_ref[at, cut * h : cut * (h + 1)].astype(F32)]
+                write_blocks(out_ref, index, b, jnp.concatenate(parts + last, axis=1))
+
+    return kernel_call(
+        body,
+        whole((2, 16, width // 16, FIRST), BF),
+        (place, h1, dqkv, da, ctx, weights, rest, tail2, squares),
+        scalars=1,
+        flops=2 * rows * width * 8 * d,
+        name="attention_grads",
+    )
+
+
+def feed(pieces, w_gu, w_d):
+    seg, width = pieces[0].shape[1:]
+    rows = 16 * seg
+    hidden = w_d.shape[1]
+
+    def body(*refs):
+        h_refs = [refs[i // 4].at[i % 4] for i in range(16)]
+        wg_ref, wd_ref, h_ref, gate_ref, act_ref, *part = refs[4:]
+        for i in range(16):
+            h_ref[i * seg : (i + 1) * seg, :] = h_refs[i][...]
+        for g in range(4):
+            rs = slice(g * 4 * seg, (g + 1) * 4 * seg)
+            both = dot_nn(h_ref[rs, :], wg_ref[...])
+            gate_ref[rs, :] = both
+            gate, up = both[:, :hidden], both[:, hidden:]
+            act_ref[rs, :] = (gate * jax.nn.sigmoid(gate) * up).astype(BF)
+        for g in (3, 2, 1, 0):
+            rs = slice(g * 4 * seg, (g + 1) * 4 * seg)
+            write_part(part, g, dot_nt(act_ref[rs, :], wd_ref[...]))
+
+    outs = [whole((rows, width), BF), whole((rows, 2 * hidden), F32), whole((rows, hidden), BF)]
+    out = kernel_call(
+        body,
+        outs + part_shapes(seg, width),
+        (*pieces, w_gu, w_d),
+        flops=2 * rows * width * hidden * 3,
+        limit=16,
+        name="feed",
+    )
+    return out[:3], out[3:]
+
+
+def feed_back(pieces, w_gu, w_d, gate_up):
+    seg, width = pieces[0].shape[1:]
+    rows = 16 * seg
+    hidden = w_d.shape[1]
+
+    def body(*refs):
+        d_refs = [refs[i // 4].at[i % 4] for i in range(16)]
+        wg_ref, wd_ref, gate_ref, dm_ref, dgu_ref, *part = refs[4:]
+        for i in range(16):
+            dm_ref[i * seg : (i + 1) * seg, :] = d_refs[i][...]
+        for g in (3, 2, 1, 0):
+            rs = slice(g * 4 * seg, (g + 1) * 4 * seg)
+            dact = dot_nn(dm_ref[rs, :], wd_ref[...])
+            gate, up = gate_ref[rs, :hidden], gate_ref[rs, hidden:]
+            sigma = jax.nn.sigmoid(gate)
+            dgate = dact * up * sigma * (1.0 + gate * (1.0 - sigma))
+            dgu_ref[rs, :] = jnp.concatenate([dgate, dact * (gate * sigma)], axis=1).astype(BF)
+        for g in (3, 2, 1, 0):
+            rs = slice(g * 4 * seg, (g + 1) * 4 * seg)
+            write_part(part, g, dot_nt(dgu_ref[rs, :], wg_ref[...]))
+
+    outs = [whole((rows, width), BF), whole((rows, 2 * hidden), BF)]
+    out = kernel_call(
+        body,
+        outs + part_shapes(seg, width),
+        (*pieces, w_gu, w_d, gate_up),
+        flops=2 * rows * width * hidden * 3,
+        limit=16,
+        name="feed_back",
+    )
+    return out[0], out[1], out[2:]
+
+
+def down_grads(dm, act):
+    rows, width = dm.shape
+    hidden = act.shape[1]
+
+    def body(dm_ref, act_ref, out_ref):
+        quarter = width // 4
+        for b in range(4):
+            at = slice(b * quarter, (b + 1) * quarter)
+            out_ref[at, :] = dot_tn(dm_ref[:, at], act_ref[...]).astype(BF)
+
+    return kernel_call(
+        body, whole((width, hidden), BF), (dm, act), flops=2 * rows * width * hidden, limit=16, name="down_grads"
+    )
+
+
+def feed_grads(place, down, h2, dgu, w_gu):
+    rows, width = h2.shape
+    hidden = down.shape[1] // 2
+    cut = SECOND - 2 * hidden
+    left = hidden - cut
+
+    def body(place_ref, down_ref, h_ref, dgu_ref, w_ref, out_ref, rest_ref, tail_ref):
+        y = place_ref[3]
+        quarter = width // 4
+        for b in range(4):
+            at = slice(b * quarter, (b + 1) * quarter)
+            g = dot_tn(h_ref[:, at], dgu_ref[...])
+            tail_ref[at, :] = jnp.sum(g * w_ref[at, :].astype(F32), axis=1, keepdims=True)
+            down = down_ref[at, :].astype(F32)
+            rest_ref[at, :] = jnp.concatenate([down[:, cut:hidden], down[:, hidden + cut :]], axis=1).astype(BF)
+            for h, index in enumerate((y, 1 - y)):
+                parts = [
+                    g[:, hidden * h : hidden * (h + 1)],
+                    g[:, hidden * (2 + h) : hidden * (3 + h)],
+                    down[:, hidden * h : hidden * h + cut],
+                ]
+                write_blocks(out_ref, index, b, jnp.concatenate(parts, axis=1))
+
+    outs = [whole((2, 16, width // 16, SECOND), BF)] + [whole((width, 2 * left), BF), whole((width, 1), F32)]
+    return kernel_call(
+        body,
+        outs,
+        (place, down, h2, dgu, w_gu),
+        scalars=1,
+        flops=2 * rows * width * hidden * 4,
+        limit=16,
+        name="feed_grads",
+    )
+
+
+def norm_back(grad, rows, inverse, gain):
+    normed = rows * inverse
+    scaled = grad * gain
+    return inverse * (scaled - normed * jnp.mean(scaled * normed, axis=-1, keepdims=True))
+
+
+def rms_of(rows):
+    return lax.rsqrt(jnp.mean(rows * rows, axis=-1, keepdims=True) + eps)
+
+
+def rows_after_attention(terms, own, info):
+    def body(*refs):
+        *term_refs, own_ref, info_ref, resid_ref, h_ref = refs
+        resid = own_ref[...].astype(F32) + total(term_refs)
+        resid_ref[...] = resid
+        h_ref[...] = (resid * rms_of(resid) * info_ref[1:2, :]).astype(BF)
+
+    return kernel_call(
+        body, [whole(own.shape, F32), whole(own.shape, BF)], (*terms, own, info), limit=16, name="after_attention"
+    )
+
+
+def rows_after_feed(terms, resid, valid, teacher, out_grad, factor):
+    def body(*refs):
+        *term_refs, resid_ref, ok_ref, teacher_ref, grad_ref, factor_ref = refs[:-4]
+        out_ref, dout_ref, dm_ref, squares_ref = refs[-4:]
+        out = resid_ref[...] + total(term_refs)
+        out_ref[...] = out.astype(BF)
+        ok = ok_ref[...]
+        diff = out - teacher_ref[...].astype(F32)
+        part = jnp.sum(ok * diff * diff, axis=0, keepdims=True)
+        squares_ref[...] = jnp.broadcast_to(jnp.sum(part, axis=1, keepdims=True), squares_ref.shape)
+        dout = ok * (grad_ref[...].astype(F32) + factor_ref[0:1, 0:1] * diff)
+        dout_ref[...] = dout
+        dm_ref[...] = dout.astype(BF)
+
+    shape = resid.shape
+    return kernel_call(
+        body,
+        [whole(shape, BF), whole(shape, F32), whole(shape, BF), whole((8, LANES), F32)],
+        (*terms, resid, valid, teacher, out_grad, factor),
+        limit=16,
+        name="after_feed",
+    )
+
+
+def rows_after_feed_back(terms, resid, dout, info):
+    def body(*refs):
+        *term_refs, resid_ref, dout_ref, info_ref, dresid_ref, da_ref = refs
+        resid = resid_ref[...]
+        dresid = dout_ref[...] + norm_back(total(term_refs), resid, rms_of(resid), info_ref[1:2, :])
+        dresid_ref[...] = dresid
+        da_ref[...] = dresid.astype(BF)
+
+    return kernel_call(
+        body,
+        [whole(resid.shape, F32), whole(resid.shape, BF)],
+        (*terms, resid, dout, info),
+        flops=10**11,
+        limit=16,
+        name="after_feed_back",
+    )
+
+
+def rows_at_end(terms, own, dresid, info):
+    def body(*refs):
+        *term_refs, own_ref, dresid_ref, info_ref, dx_ref = refs
+        rows = own_ref[...].astype(F32)
+        dx = dresid_ref[...] + norm_back(total(term_refs), rows, rms_of(rows), info_ref[0:1, :])
+        dx_ref[...] = dx.astype(BF)
+
+    return kernel_call(body, whole(own.shape, BF), (*terms, own, dresid, info), limit=16, name="at_end")
+
+
+def layer(
+    inputs,
+    valid,
+    out_grad,
+    teacher,
+    norm_attn,
+    w_query,
+    key_matrix,
+    value_matrix,
+    w_out,
+    norm_mlp,
+    w_gate,
+    w_up,
+    w_down,
+):
+    seqs, seg, width = inputs.shape
+    y = lax.axis_index("tensor")
+    k = lax.axis_index("context")
+    z, x, c = k // 4, (k // 2) % 2, k % 2
+    place = jnp.stack([z, x, c, y]).astype(jnp.int32)
+    seq_len = 16 * seg
+    first = y == 0
+
+    def mine(a):
+        return lax.dynamic_index_in_dim(a, y, 0, keepdims=False)
+
+    own = mine(inputs)
+    counts = jnp.sum(valid.astype(F32), axis=1).astype(BF)
+    ones = jnp.ones_like(norm_attn)
+    extra = jnp.stack([norm_attn, norm_mlp, ones * counts[0], ones * counts[1]], axis=1)
+    hidden = w_gate.shape[1] // 16
+    firsts = pack_first(w_query, key_matrix, value_matrix, w_out.T, extra, w_down.T)
+    seconds = pack_second(w_gate, w_up, w_down.T)
+    first_in = share_blocks(firsts)
+    pieces, near, far = gather_rows(own)
+    first_both = of_other(first_in)
+    second_in = share_blocks(after(seconds, first_both, *near, *far))
+    w_qkv, w_o, info = prepare_attention(place, first_in, first_both)
+    lengths = jnp.sum(info[2:4], axis=1) / F32(width // 16)
+    count = lengths[0] + lengths[1]
+    length = jnp.full((8, LANES), jnp.where(first, lengths[0], lengths[1]), F32)
+    factor = jnp.full((8, LANES), F32(seqs * seq_len) / count, F32)
+
+    bit = jnp.arange(2, dtype=jnp.int32)
+    pos = (
+        jnp.arange(4, dtype=jnp.int32)[:, None, None, None] * (4 * seg)
+        + (bit ^ x)[None, :, None, None] * (2 * seg)
+        + (bit ^ c)[None, None, :, None] * seg
+        + jnp.arange(seg, dtype=jnp.int32)[None, None, None, :]
+    ).reshape(seq_len)
+    half = HEAD_SIZE // 2
+    freqs = jnp.exp(-math.log(theta) * jnp.arange(half, dtype=F32) / half)
+    angles = pos.astype(F32)[:, None] * freqs[None, :]
+    cos_half, sin_half = jnp.cos(angles), jnp.sin(angles)
+    pad = jnp.zeros((seq_len, LANES - HEAD_SIZE), F32)
+    cosine = jnp.concatenate([cos_half, cos_half, pad], axis=1)
+    sine = jnp.concatenate([-sin_half, sin_half, pad], axis=1)
+    kpos = pos[None, :]
+
+    (h1, q, keys, values, ctx, lse), part = attention(
+        place, pieces, w_qkv, w_o, info, length, kpos, cosine, sine
+    )
+    terms, far, come = scatter_rows(part)
+    second_both = of_other(after(second_in, come[2]))
+    resid, h2_own = rows_after_attention(terms, own, info)
+    w_gu, w_d = prepare_feed(place, first_in, first_both, second_in, second_both, hidden)
+    pieces, _, _ = gather_rows(h2_own, w_gu)
+    (h2, gate_up, act), part = feed(pieces, w_gu, w_d)
+    okf = mine(valid).astype(F32)[:, None]
+    terms, _, _ = scatter_rows(part)
+    out_own, dout, dm_own, squares = rows_after_feed(
+        terms, resid, okf, mine(teacher), mine(out_grad), factor
+    )
+    pieces, _, _ = gather_rows(dm_own)
+    dm, dgu, part = feed_back(pieces, w_gu, w_d, gate_up)
+    terms, far, _ = scatter_rows(part)
+    down = down_grads(after(dm, part[0]), act)
+    shares, rest, tail2 = feed_grads(place, down, h2, after(dgu, *far), w_gu)
+    summed = over_sequences(shares)
+    dresid, da_own = rows_after_feed_back(terms, resid, dout, info)
+    pieces, near, far = gather_rows(da_own)
+    seconds = share_blocks(after(summed, *near))
+    da, dqkv, part = attention_back(
+        place, pieces, w_qkv, w_o, length, kpos, cosine, sine, q, keys, values, lse
+    )
+    terms, far, _ = scatter_rows(part)
+    shares = attention_grads(place, h1, after(dqkv, *far), da, ctx, w_qkv, rest, tail2, squares)
+    summed = over_sequences(after(shares, seconds))
+    dx = rows_at_end(terms, own, dresid, info)
+    firsts = share_blocks(after(summed, seconds, dx))
+    grad_gate, grad_up = unpack_second(after(seconds, dx), hidden)
+    both_out = move_y(out_own)
+    both_dx = move_y(dx)
+    output = jnp.stack([jnp.where(first, out_own, both_out), jnp.where(first, both_out, out_own)])
+    input_grad = jnp.stack([jnp.where(first, dx, both_dx), jnp.where(first, both_dx, dx)]).astype(F32)
+    grad_query, grad_key, grad_value, grad_out, grad_down, tails = unpack_first(firsts, seconds, hidden)
+    return (
+        output,
+        tails[0, 2] / (count * width),
+        input_grad,
+        tails[:, 0] / norm_attn.astype(F32),
+        tails[:, 1] / norm_mlp.astype(F32),
+        grad_query,
+        grad_key,
+        grad_value,
+        grad_out.T,
+        grad_gate,
+        grad_up,
+        grad_down.T,
+    )
 
 
 def rms_forward(value_rows, gain):
@@ -340,4 +1136,7 @@
         P("context", "tensor"),
         P("tensor", "context"),
     )
-    return jax.shard_map(shards, mesh=mesh, in_specs=in_specs, out_specs=out_specs, check_vma=False)
+    fits = dict(mesh.shape) == {"tensor": 2, "context": 16}
+    return jax.shard_map(
+        layer if fits else shards, mesh=mesh, in_specs=in_specs, out_specs=out_specs, check_vma=False
+    )

time: 2610 us -> 778 us (0.30)
  waiting for transfers between devices: 2150 us -> 407 us
  matrix products: 193 us -> 0 us
  Pallas kernels: 0 us -> 104 us
  starting transfers between devices: 1.64 us -> 105 us
  blocking collectives: 131 us -> 51 us
    reduce_scatter x7 -> x2, waiting for transfers between devices: 1400 us -> 0.27 us  [over_sequences(): return lax.psum_scatter(parts, 'tensor', scatter_dimension=0, tiled=False)]
    all_gather x9 -> x2, waiting for transfers between devices: 445 us -> 18.5 us  [of_other(): return lax.all_gather(a, 'tensor', axis=0, tiled=False)]
    ppermute x0 -> x74, waiting for transfers between devices: none -> 356 us  [the longest x32 178 us: move_x(): return lax.ppermute(a, 'context', [(k, k ^ 2) for k in range(16)])]
    while x8 -> x0, waiting for transfers between devices: 230 us -> none
    dot_general x65 -> x0, matrix products: 193 us -> none  [the longest x7 62 us: dot_left(): lax.dot_general(left, right, (((0,), (0,)), ((), ())), preferred_element_...]
    pallas_call x0 -> x41, Pallas kernels: none -> 104 us  [kernel_call(): pl.pallas_call(body, out_shape=outs, in_specs=[spec(i) for i in range(len...]
    ppermute x0 -> x74, starting transfers between devices: none -> 81 us  [the longest x24 42.8 us: move_z(): lax.ppermute(a, 'context', [(k, (k + 4 * step) % 16) for k in range(16)])]
    psum x2 -> x0, blocking collectives: 68.8 us -> none  [shards(): lax.psum((jnp.sum(valid.astype(jnp.float32)), jnp.sum(validf * diff * dif...]
  transfers between devices with their start and end apart: 24 -> 81, of which waited for: 21 -> 55; matrix products, arithmetic and copies ran while one was open for 6% -> 1% of each run, Pallas kernels for 0% -> 9%
where the time goes in v2:
time: 778 us; the launch traced here: 770 us
  waiting for transfers between devices  407 us (52%)
  starting transfers between devices  105 us (13%)
  Pallas kernels  104 us (13%)
  local copies, waits for them, and re-layouts  74.7 us (10%)
  blocking collectives  51 us (7%)
  between operations  19.4 us (2%)
  other arithmetic  8.96 us (1%)
    ppermute x32, waiting for transfers between devices, move_x(): return lax.ppermute(a, 'context', [(k, k ^ 2) for k in range(16)])  178 us
    ppermute x24, waiting for transfers between devices, move_z(): lax.ppermute(a, 'context', [(k, (k + 4 * step) % 16) for k in range(16)])  144 us
    pallas_call x41, Pallas kernels, kernel_call(): pl.pallas_call(body, out_shape=outs, in_specs=[spec(i) for i in range(len...  104 us
    unnamed x250, local copies, waits for them, and re-layouts  67.8 us
    all_to_all x1, blocking collectives, share_out(): return lax.all_to_all(a, 'context', split_axis=0, concat_axis=0, tiled=True)  51 us
    ppermute x24, starting transfers between devices, move_z(): lax.ppermute(a, 'context', [(k, (k + 4 * step) % 16) for k in range(16)])  42.8 us
    all_to_all x3, waiting for transfers between devices, share_out(): return lax.all_to_all(a, 'context', split_axis=0, concat_axis=0, tiled=True)  32.6 us
    all_to_all x3, starting transfers between devices, share_out(): return lax.all_to_all(a, 'context', split_axis=0, concat_axis=0, tiled=True)  23.5 us
  transfers between devices with their start and end apart: 81, of which 55 were waited for; matrix products, arithmetic and copies ran while one was open for 1% of the time, Pallas kernels for 9%

profile of v2, /device:TPU:11, one launch (start us, length us, event | category | flops | bytes accessed | tf_op | source)
XLA Modules:
  0.0 770.3 jit_solution(666254910584937164)
XLA Ops:
  18.0 51.0 %all_to_all.24.mine_ref.fm_ref = bf16[16,160,384]{2,1,0:T(8,128)(2,1)} all-to-all(bf16[16,160,384]{2,1,0:T(8,128)(2,1)S(1)} %pack_first.1), channel_id=1, replica_groups=mesh['tensor'=2,'context'=16] {'context'}, dimensions={0} | all-to-all | bytes 3932160 | tf_op jit(solution)/shard_map/all_to_all | solution.py:80
  73.2 5.1 collective-permute-done.4.refs_0_
  80.5 12.0 %collective-permute-done.1.refs_2_ = bf16[64,2560]{1,0:T(8,128)(2,1)S(1)} collective-permute-done((bf16[64,2560]{1,0:T(8,128)(2,1)S(1)}, bf16[64,2560]{1,0:T(8,128)(2,1)S(1)}, u32[]{:S(2)}, u32[]{:S(2)}) %collective-permute-start.1) | collective-permute-done | bytes 327712 | tf_op jit(solution)/shard_map/ppermute | solution.py:72
  92.5 7.0 collective-permute-done.refs_1_
  110.2 12.5 %all-gather.5.cloned.1.call-done = bf16[32,160,384]{2,1,0:T(8,128)(2,1)} async-done(((bf16[16,160,384]{2,1,0:T(8,128)(2,1)}), bf16[32,160,384]{2,1,0:T(8,128)(2,1)}) %all-gather.5.cloned.1.call-update) | async-done | bytes 3932176 | tf_op jit(solution)/shard_map/all_gather | solution.py:214
  122.6 6.5 all-to-all-start.1
  150.5 19.1 %attention.1 = (bf16[1024,2560]{1,0:T(8,128)(2,1)S(1)}, bf16[2,1024,128]{2,1,0:T(8,128)(2,1)S(1)}, bf16[2,1024,128]{2,1,0:T(8,128)(2,1)S(1)}, bf16[2,1024,128]{2...) custom-call(s32[4]{0:T(128)S(1)} %pad_add_fusion.place_ref, ...), custom_call_target="tpu_custom_call" | custom-call | tf_op jit(solution)/shard_map/attention/pallas_call | solution.py:39
  181.4 10.0 %collective-permute-done.12.c_ref = bf16[64,2560]{1,0:T(8,128)(2,1)S(1)} collective-permute-done((bf16[64,2560]{1,0:T(8,128)(2,1)S(1)}, bf16[64,2560]{1,0:T(8,128)(2,1)S(1)}, u32[]{:S(2)}, u32[]{:S(2)}) %collective-permute-start.12) | collective-permute-done | bytes 327712 | tf_op jit(solution)/shard_map/ppermute | solution.py:68
  191.4 10.5 %all-to-all-done.1.m_ref = bf16[16,160,640]{2,1,0:T(8,128)(2,1)} async-done(((bf16[16,160,640]{2,1,0:T(8,128)(2,1)}), bf16[16,160,640]{2,1,0:T(8,128)(2,1)}, u32[]{:S(2)}, u32[]{:S(2)}) %all-to-all-start.1) | async-done | bytes 3276832 | tf_op jit(solution)/shard_map/all_to_all | solution.py:80
  206.8 11.8 %collective-permute-done.14.c_ref = bf16[64,2560]{1,0:T(8,128)(2,1)S(1)} collective-permute-done((bf16[64,2560]{1,0:T(8,128)(2,1)}, bf16[64,2560]{1,0:T(8,128)(2,1)S(1)}, u32[]{:S(2)}, u32[]{:S(2)}) %collective-permute-start.14) | collective-permute-done | bytes 327712 | tf_op jit(solution)/shard_map/ppermute | solution.py:68
  218.9 6.8 collective-permute-done.16.c_ref
  226.7 9.0 %collective-permute-done.17.refs_5_ = bf16[64,2560]{1,0:T(8,128)(2,1)S(1)} collective-permute-done((bf16[64,2560]{1,0:T(8,128)(2,1)S(1)}, bf16[64,2560]{1,0:T(8,128)(2,1)S(1)}, u32[]{:S(2)}, u32[]{:S(2)}) %collective-permute-start.17) | collective-permute-done | bytes 327712 | tf_op jit(solution)/shard_map/ppermute | solution.py:72
  246.1 13.8 %collective-permute-done.19.refs_2_ = bf16[64,2560]{1,0:T(8,128)(2,1)S(1)} collective-permute-done((bf16[64,2560]{1,0:T(8,128)(2,1)S(1)}, bf16[64,2560]{1,0:T(8,128)(2,1)S(1)}, u32[]{:S(2)}, u32[]{:S(2)}) %collective-permute-start.19) | collective-permute-done | bytes 327712 | tf_op jit(solution)/shard_map/ppermute | solution.py:72
  261.4 5.6 collective-permute-done.18.refs_1_
  270.1 6.8 collective-permute-done.23.refs_1_
  278.0 6.0 all-gather.7.cloned.1.call-done
  297.3 10.2 %feed.1 = (bf16[1024,2560]{1,0:T(8,128)(2,1)S(1)}, f32[1024,864]{1,0:T(8,128)S(1)}, bf16[1024,432]{1,0:T(8,128)(2,1)S(1)}, bf16[4,64,2560]{2,1,0:T(8,128)(2,1)},...) custom-call(bf16[4,64,2560]{2,1,0:T(8,128)(2,1)S(1)} %stack.74.refs_, ...), custom_call_target="tpu_custom_call" | custom-call | tf_op jit(solution)/shard_map/feed/pallas_call | solution.py:39
  324.6 11.8 %collective-permute-done.30.c_ref = bf16[64,2560]{1,0:T(8,128)(2,1)S(1)} collective-permute-done((bf16[64,2560]{1,0:T(8,128)(2,1)S(1)}, bf16[64,2560]{1,0:T(8,128)(2,1)S(1)}, u32[]{:S(2)}, u32[]{:S(2)}) %collective-permute-start.30) | collective-permute-done | bytes 327712 | tf_op jit(solution)/shard_map/ppermute | solution.py:68
  345.1 5.5 collective-permute-done.34.c_ref
  354.8 6.4 collective-permute-done.31.refs_3_
  362.0 5.9 collective-permute-done.33.refs_4_
  383.4 13.6 %collective-permute-done.38.refs_2_ = bf16[64,2560]{1,0:T(8,128)(2,1)S(1)} collective-permute-done((bf16[64,2560]{1,0:T(8,128)(2,1)S(1)}, bf16[64,2560]{1,0:T(8,128)(2,1)S(1)}, u32[]{:S(2)}, u32[]{:S(2)}) %collective-permute-start.38) | collective-permute-done | bytes 327712 | tf_op jit(solution)/shard_map/ppermute | solution.py:72
  398.1 5.8 collective-permute-done.37.refs_1_
  406.8 7.0 collective-permute-done.42.refs_1_
  422.5 8.8 %feed_back.1 = (bf16[1024,2560]{1,0:T(8,128)(2,1)S(1)}, bf16[1024,864]{1,0:T(8,128)(2,1)S(1)}, bf16[4,64,2560]{2,1,0:T(8,128)(2,1)S(1)}, bf16[4,64,2560]{2,1,0:T...) custom-call(bf16[4,64,2560]{2,1,0:T(8,128)(2,1)S(1)} %stack.76.refs_, ...), custom_call_target="tpu_custom_call" | custom-call | tf_op jit(solution)/shard_map/feed_back/pallas_call | solution.py:39
  438.4 8.9 %feed_grads.1 = (bf16[2,16,160,640]{3,2,1,0:T(8,128)(2,1)S(1)}, bf16[2560,16]{1,0:T(8,128)(2,1)S(1)}, f32[2560,1]{1,0:T(8,128)S(1)}) custom-call(s32[4]{0:T(128)S(1)} %pad_add_fusion.place_ref, bf16[2560,432]{1,0:T(8,128)(2,1)S(1)} %down_grads.1.down_ref, bf16[1024,2560]{1,0:T(8,128)(2,1)S(1)} %bitcast.71, bf16[1024,864]{1,0:T(8,128)(2,1)S(1)} %get-tuple-element.195.dgu_ref, ...), custom_call_target="tpu_custom_call" | custom-call | tf_op jit(solution)/shard_map/feed_grads/pallas_call | solution.py:39
  455.4 13.0 %collective-permute-done.49.c_ref = bf16[64,2560]{1,0:T(8,128)(2,1)S(1)} collective-permute-done((bf16[64,2560]{1,0:T(8,128)(2,1)}, bf16[64,2560]{1,0:T(8,128)(2,1)S(1)}, u32[]{:S(2)}, u32[]{:S(2)}) %collective-permute-start.49) | collective-permute-done | bytes 327712 | tf_op jit(solution)/shard_map/ppermute | solution.py:68
  468.6 6.8 collective-permute-done.51.c_ref
  488.1 12.3 %collective-permute-done.52.refs_4_ = bf16[64,2560]{1,0:T(8,128)(2,1)S(1)} collective-permute-done((bf16[64,2560]{1,0:T(8,128)(2,1)S(1)}, bf16[64,2560]{1,0:T(8,128)(2,1)S(1)}, u32[]{:S(2)}, u32[]{:S(2)}) %collective-permute-start.52) | collective-permute-done | bytes 327712 | tf_op jit(solution)/shard_map/ppermute | solution.py:72
  504.9 20.9 %collective-permute-done.57.refs_3_ = bf16[64,2560]{1,0:T(8,128)(2,1)} collective-permute-done((bf16[64,2560]{1,0:T(8,128)(2,1)}, bf16[64,2560]{1,0:T(8,128)(2,1)}, u32[]{:S(2)}, u32[]{:S(2)}) %collective-permute-start.57) | collective-permute-done | bytes 327712 | tf_op jit(solution)/shard_map/ppermute | solution.py:72
  525.8 6.5 collective-permute-done.55.refs_1_
  532.5 7.1 all-to-all-start.2
  540.4 25.0 %collective-permute-done.59.refs_0_ = bf16[64,2560]{1,0:T(8,128)(2,1)S(1)} collective-permute-done((bf16[64,2560]{1,0:T(8,128)(2,1)}, bf16[64,2560]{1,0:T(8,128)(2,1)S(1)}, u32[]{:S(2)}, u32[]{:S(2)}) %collective-permute-start.59) | collective-permute-done | bytes 327712 | tf_op jit(solution)/shard_map/ppermute | solution.py:68
  570.0 9.2 %collective-permute-done.62.refs_3_ = bf16[64,2560]{1,0:T(8,128)(2,1)S(1)} collective-permute-done((bf16[64,2560]{1,0:T(8,128)(2,1)}, bf16[64,2560]{1,0:T(8,128)(2,1)S(1)}, u32[]{:S(2)}, u32[]{:S(2)}) %collective-permute-start.62) | collective-permute-done | bytes 327712 | tf_op jit(solution)/shard_map/ppermute | solution.py:68
  579.2 10.6 %collective-permute-done.61.refs_2_ = bf16[64,2560]{1,0:T(8,128)(2,1)S(1)} collective-permute-done((bf16[64,2560]{1,0:T(8,128)(2,1)}, bf16[64,2560]{1,0:T(8,128)(2,1)S(1)}, u32[]{:S(2)}, u32[]{:S(2)}) %collective-permute-start.61) | collective-permute-done | bytes 327712 | tf_op jit(solution)/shard_map/ppermute | solution.py:68
  589.8 11.4 %collective-permute-done.60.refs_1_ = bf16[64,2560]{1,0:T(8,128)(2,1)S(1)} collective-permute-done((bf16[64,2560]{1,0:T(8,128)(2,1)}, bf16[64,2560]{1,0:T(8,128)(2,1)S(1)}, u32[]{:S(2)}, u32[]{:S(2)}) %collective-permute-start.60) | collective-permute-done | bytes 327712 | tf_op jit(solution)/shard_map/ppermute | solution.py:68
  610.5 11.6 %attention_back.1 = (bf16[1024,2560]{1,0:T(8,128)(2,1)S(1)}, bf16[1024,480]{1,0:T(8,128)(2,1)S(1)}, bf16[4,64,2560]{2,1,0:T(8,128)(2,1)S(1)}, bf16[4,64,2560]{2,...) custom-call(s32[4]{0:T(128)S(1)} %pad_add_fusion.place_ref, ...), custom_call_target="tpu_custom_call" | custom-call | tf_op jit(solution)/shard_map/attention_back/pallas_call | solution.py:39
  629.6 7.2 attention_grads.1
  642.3 13.5 %collective-permute-done.69.c_ref = bf16[64,2560]{1,0:T(8,128)(2,1)S(1)} collective-permute-done((bf16[64,2560]{1,0:T(8,128)(2,1)}, bf16[64,2560]{1,0:T(8,128)(2,1)S(1)}, u32[]{:S(2)}, u32[]{:S(2)}) %collective-permute-start.69) | collective-permute-done | bytes 327712 | tf_op jit(solution)/shard_map/ppermute | solution.py:68
  655.9 6.4 collective-permute-start.70
  662.3 7.5 collective-permute-done.71.c_ref
  669.9 5.7 collective-permute-start.72
  683.7 12.1 %collective-permute-done.68.refs_3_ = bf16[64,2560]{1,0:T(8,128)(2,1)S(1)} collective-permute-done((bf16[64,2560]{1,0:T(8,128)(2,1)S(1)}, bf16[64,2560]{1,0:T(8,128)(2,1)S(1)}, u32[]{:S(2)}, u32[]{:S(2)}) %collective-permute-start.68) | collective-permute-done | bytes 327712 | tf_op jit(solution)/shard_map/ppermute | solution.py:72
  697.1 9.9 %all-to-all-start.3 = ((bf16[16,160,384]{2,1,0:T(8,128)(2,1)}), bf16[16,160,384]{2,1,0:T(8,128)(2,1)}, u32[]{:S(2)}, u32[]{:S(2)}) async-start(bf16[16,160,384]{2,1,0:T(8,128)(2,1)} %bitcast.78), calls=%async_computation.5 | async-start | bytes 3932160 | tf_op jit(solution)/shard_map/all_to_all | solution.py:80
  707.4 8.9 %collective-permute-done.36 = bf16[64,2560]{1,0:T(8,128)(2,1)} collective-permute-done((bf16[64,2560]{1,0:T(8,128)(2,1)}, bf16[64,2560]{1,0:T(8,128)(2,1)}, u32[]{:S(2)}, u32[]{:S(2)}) %collective-permute-start.36) | collective-permute-done | bytes 327712 | tf_op jit(solution)/shard_map/ppermute | solution.py:76
  718.8 6.9 collective-permute-done.73
  729.7 22.1 %all-to-all-done.3.f_ref = bf16[16,160,384]{2,1,0:T(8,128)(2,1)} async-done(((bf16[16,160,384]{2,1,0:T(8,128)(2,1)}), bf16[16,160,384]{2,1,0:T(8,128)(2,1)}, u32[]{:S(2)}, u32[]{:S(2)}) %all-to-all-start.3) | async-done | bytes 1966112 | tf_op jit(solution)/shard_map/all_to_all | solution.py:80
  753.7 6.1 unpack_first.1
  (456 shorter events, 232.8 us)
Async XLA Ops:
  7.2 115.5 %all-gather.5.cloned.1.call-start = ((), (), s32[]{:S(2)}) async-start(), calls=%async_computation.8 | async-start | bytes 5898240 | tf_op jit(solution)/shard_map/all_gather | solution.py:214
  70.4 22.1 %collective-permute-start.1 = (bf16[64,2560]{1,0:T(8,128)(2,1)S(1)}, bf16[64,2560]{1,0:T(8,128)(2,1)S(1)}, u32[]{:S(2)}, u32[]{:S(2)}) collective-permute-start(bf16[64,2560]{1,0:T(8,128)(2,1)S(1)} %dynamic-slice_bitcast_fusion.2.refs_0_.refs_6_), channel_id=1, source_target_pairs={{0,8},{1,9},{2,10},{3,11},{4,12},{5,13},{6,14},{7,15},{8,0},{9,1},... | collective-permute-start | bytes 983048 | tf_op jit(solution)/shard_map/ppermute | solution.py:72
  71.4 28.1 %collective-permute-start = (bf16[64,2560]{1,0:T(8,128)(2,1)S(1)}, bf16[64,2560]{1,0:T(8,128)(2,1)S(1)}, u32[]{:S(2)}, u32[]{:S(2)}) collective-permute-start(bf16[64,2560]{1,0:T(8,128)(2,1)S(1)} %dynamic-slice_bitcast_fusion.2.refs_0_.refs_6_), channel_id=1, source_target_pairs={{0,4},{1,5},{2,6},{3,7},{4,8},{5,9},{6,10},{7,11},{8,12},{9,13},{1... | collective-permute-start | bytes 983048 | tf_op jit(solution)/shard_map/ppermute | solution.py:72
  80.5 23.4 %collective-permute-start.7 = (bf16[64,2560]{1,0:T(8,128)(2,1)S(1)}, bf16[64,2560]{1,0:T(8,128)(2,1)S(1)}, u32[]{:S(2)}, u32[]{:S(2)}) collective-permute-start(bf16[64,2560]{1,0:T(8,128)(2,1)S(1)} %collective-permute-done.2.refs_3_), channel_id=1, source_target_pairs={{0,2},{1,3},{2,0},{3,1},{4,6},{5,7},{6,4},{7,5},{8,10},{9,11},{10,... | collective-permute-start | bytes 983048 | tf_op jit(solution)/shard_map/ppermute | solution.py:68
  122.6 79.3 %all-to-all-start.1 = ((bf16[16,160,640]{2,1,0:T(8,128)(2,1)}), bf16[16,160,640]{2,1,0:T(8,128)(2,1)}, u32[]{:S(2)}, u32[]{:S(2)}) async-start(bf16[16,160,640]{2,1,0:T(8,128)(2,1)} %pack_second.1), calls=%async_computation.1 | async-start | bytes 6553600 | tf_op jit(solution)/shard_map/all_to_all | solution.py:80
  129.2 154.9 %all-gather.7.cloned.1.call-start = ((), (), s32[]{:S(2)}) async-start(), calls=%async_computation.9 | async-start | bytes 9830400 | tf_op jit(solution)/shard_map/all_gather | solution.py:214
  129.6 15.7 %collective-permute-start.3 = (bf16[4,64,2560]{2,1,0:T(8,128)(2,1)S(1)}, bf16[4,64,2560]{2,1,0:T(8,128)(2,1)}, u32[]{:S(2)}, u32[]{:S(2)}) collective-permute-start(bf16[4,64,2560]{2,1,0:T(8,128)(2,1)S(1)} %stack.72.refs_0_), channel_id=1, source_target_pairs={{0,1},{1,0},{2,3},{3,2},{4,5},{5,4},{6,7},{7,6},{8,9},{9,8},{10,11... | collective-permute-start | bytes 3932168 | tf_op jit(solution)/shard_map/ppermute | solution.py:64
  202.0 330.6 %reduce-scatter.3.cloned.1.call-start = ((), (), s32[]{:S(2)}) async-start(), calls=%async_computation.6 | async-start | bytes 9830400 | tf_op jit(solution)/shard_map/reduce_scatter | solution.py:218
  202.3 24.4 %collective-permute-start.11 = (bf16[64,2560]{1,0:T(8,128)(2,1)}, bf16[64,2560]{1,0:T(8,128)(2,1)S(1)}, u32[]{:S(2)}, u32[]{:S(2)}) collective-permute-start(bf16[64,2560]{1,0:T(8,128)(2,1)} %get-tuple-element.125), channel_id=1, source_target_pairs={{0,2},{1,3},{2,0},{3,1},{4,6},{5,7},{6,4},{7,5},{8,10},{9,11},{10,... | collective-permute-start | bytes 983048 | tf_op jit(solution)/shard_map/ppermute | solution.py:68
  202.3 16.3 %collective-permute-start.14 = (bf16[64,2560]{1,0:T(8,128)(2,1)}, bf16[64,2560]{1,0:T(8,128)(2,1)S(1)}, u32[]{:S(2)}, u32[]{:S(2)}) collective-permute-start(bf16[64,2560]{1,0:T(8,128)(2,1)} %get-tuple-element.129), channel_id=1, source_target_pairs={{0,2},{1,3},{2,0},{3,1},{4,6},{5,7},{6,4},{7,5},{8,10},{9,11},{10,... | collective-permute-start | bytes 983048 | tf_op jit(solution)/shard_map/ppermute | solution.py:68
  203.8 21.9 %collective-permute-start.16 = (bf16[64,2560]{1,0:T(8,128)(2,1)}, bf16[64,2560]{1,0:T(8,128)(2,1)S(1)}, u32[]{:S(2)}, u32[]{:S(2)}) collective-permute-start(bf16[64,2560]{1,0:T(8,128)(2,1)} %get-tuple-element.131), channel_id=1, source_target_pairs={{0,2},{1,3},{2,0},{3,1},{4,6},{5,7},{6,4},{7,5},{8,10},{9,11},{10,... | collective-permute-start | bytes 983048 | tf_op jit(solution)/shard_map/ppermute | solution.py:68
  205.6 21.1 %collective-permute-start.13 = (bf16[64,2560]{1,0:T(8,128)(2,1)S(1)}, bf16[64,2560]{1,0:T(8,128)(2,1)S(1)}, u32[]{:S(2)}, u32[]{:S(2)}) collective-permute-start(bf16[64,2560]{1,0:T(8,128)(2,1)S(1)} %add_near.12), channel_id=1, source_target_pairs={{0,8},{1,9},{2,10},{3,11},{4,12},{5,13},{6,14},{7,15},{8,0},{9,1},... | collective-permute-start | bytes 983048 | tf_op jit(solution)/shard_map/ppermute | solution.py:72
  237.4 22.5 %collective-permute-start.19 = (bf16[64,2560]{1,0:T(8,128)(2,1)S(1)}, bf16[64,2560]{1,0:T(8,128)(2,1)S(1)}, u32[]{:S(2)}, u32[]{:S(2)}) collective-permute-start(bf16[64,2560]{1,0:T(8,128)(2,1)S(1)} %get-tuple-element.132.refs_0_), channel_id=1, source_target_pairs={{0,8},{1,9},{2,10},{3,11},{4,12},{5,13},{6,14},{7,15},{8,0},{9,1},... | collective-permute-start | bytes 983048 | tf_op jit(solution)/shard_map/ppermute | solution.py:72
  239.4 27.6 %collective-permute-start.18 = (bf16[64,2560]{1,0:T(8,128)(2,1)S(1)}, bf16[64,2560]{1,0:T(8,128)(2,1)S(1)}, u32[]{:S(2)}, u32[]{:S(2)}) collective-permute-start(bf16[64,2560]{1,0:T(8,128)(2,1)S(1)} %get-tuple-element.132.refs_0_), channel_id=1, source_target_pairs={{0,4},{1,5},{2,6},{3,7},{4,8},{5,9},{6,10},{7,11},{8,12},{9,13},{1... | collective-permute-start | bytes 983048 | tf_op jit(solution)/shard_map/ppermute | solution.py:72
  244.8 25.3 %collective-permute-start.25 = (bf16[64,2560]{1,0:T(8,128)(2,1)S(1)}, bf16[64,2560]{1,0:T(8,128)(2,1)S(1)}, u32[]{:S(2)}, u32[]{:S(2)}) collective-permute-start(bf16[64,2560]{1,0:T(8,128)(2,1)S(1)} %collective-permute-done.20.refs_3_), channel_id=1, source_target_pairs={{0,2},{1,3},{2,0},{3,1},{4,6},{5,7},{6,4},{7,5},{8,10},{9,11},{10,... | collective-permute-start | bytes 983048 | tf_op jit(solution)/shard_map/ppermute | solution.py:68
  268.5 26.1 %collective-permute-start.21 = (bf16[4,64,2560]{2,1,0:T(8,128)(2,1)S(1)}, bf16[4,64,2560]{2,1,0:T(8,128)(2,1)}, u32[]{:S(2)}, u32[]{:S(2)}) collective-permute-start(bf16[4,64,2560]{2,1,0:T(8,128)(2,1)S(1)} %stack.74.refs_0_), channel_id=1, source_target_pairs={{0,1},{1,0},{2,3},{3,2},{4,5},{5,4},{6,7},{7,6},{8,9},{9,8},{10,11... | collective-permute-start | bytes 3932168 | tf_op jit(solution)/shard_map/ppermute | solution.py:64
  320.3 33.8 %collective-permute-start.29 = (bf16[64,2560]{1,0:T(8,128)(2,1)}, bf16[64,2560]{1,0:T(8,128)(2,1)S(1)}, u32[]{:S(2)}, u32[]{:S(2)}) collective-permute-start(bf16[64,2560]{1,0:T(8,128)(2,1)} %get-tuple-element.145), channel_id=1, source_target_pairs={{0,2},{1,3},{2,0},{3,1},{4,6},{5,7},{6,4},{7,5},{8,10},{9,11},{10,... | collective-permute-start | bytes 983048 | tf_op jit(solution)/shard_map/ppermute | solution.py:68
  320.7 15.8 %collective-permute-start.30 = (bf16[64,2560]{1,0:T(8,128)(2,1)S(1)}, bf16[64,2560]{1,0:T(8,128)(2,1)S(1)}, u32[]{:S(2)}, u32[]{:S(2)}) collective-permute-start(bf16[64,2560]{1,0:T(8,128)(2,1)S(1)} %get-tuple-element.147), channel_id=1, source_target_pairs={{0,2},{1,3},{2,0},{3,1},{4,6},{5,7},{6,4},{7,5},{8,10},{9,11},{10,... | collective-permute-start | bytes 983048 | tf_op jit(solution)/shard_map/ppermute | solution.py:68
  321.8 21.7 %collective-permute-start.32 = (bf16[64,2560]{1,0:T(8,128)(2,1)S(1)}, bf16[64,2560]{1,0:T(8,128)(2,1)S(1)}, u32[]{:S(2)}, u32[]{:S(2)}) collective-permute-start(bf16[64,2560]{1,0:T(8,128)(2,1)S(1)} %get-tuple-element.149), channel_id=1, source_target_pairs={{0,2},{1,3},{2,0},{3,1},{4,6},{5,7},{6,4},{7,5},{8,10},{9,11},{10,... | collective-permute-start | bytes 983048 | tf_op jit(solution)/shard_map/ppermute | solution.py:68
  322.2 28.3 %collective-permute-start.34 = (bf16[64,2560]{1,0:T(8,128)(2,1)S(1)}, bf16[64,2560]{1,0:T(8,128)(2,1)S(1)}, u32[]{:S(2)}, u32[]{:S(2)}) collective-permute-start(bf16[64,2560]{1,0:T(8,128)(2,1)S(1)} %get-tuple-element.151), channel_id=1, source_target_pairs={{0,2},{1,3},{2,0},{3,1},{4,6},{5,7},{6,4},{7,5},{8,10},{9,11},{10,... | collective-permute-start | bytes 983048 | tf_op jit(solution)/shard_map/ppermute | solution.py:68
  337.3 23.9 %collective-permute-start.31 = (bf16[64,2560]{1,0:T(8,128)(2,1)}, bf16[64,2560]{1,0:T(8,128)(2,1)S(1)}, u32[]{:S(2)}, u32[]{:S(2)}) collective-permute-start(bf16[64,2560]{1,0:T(8,128)(2,1)} %add_near.15), channel_id=1, source_target_pairs={{0,8},{1,9},{2,10},{3,11},{4,12},{5,13},{6,14},{7,15},{8,0},{9,1},... | collective-permute-start | bytes 983048 | tf_op jit(solution)/shard_map/ppermute | solution.py:72
  344.5 23.4 %collective-permute-start.33 = (bf16[64,2560]{1,0:T(8,128)(2,1)}, bf16[64,2560]{1,0:T(8,128)(2,1)}, u32[]{:S(2)}, u32[]{:S(2)}) collective-permute-start(bf16[64,2560]{1,0:T(8,128)(2,1)} %add_near.16), channel_id=1, source_target_pairs={{0,12},{1,13},{2,14},{3,15},{4,0},{5,1},{6,2},{7,3},{8,4},{9,5},{1... | collective-permute-start | bytes 983048 | tf_op jit(solution)/shard_map/ppermute | solution.py:72
  351.4 16.9 %collective-permute-start.35 = (bf16[64,2560]{1,0:T(8,128)(2,1)}, bf16[64,2560]{1,0:T(8,128)(2,1)}, u32[]{:S(2)}, u32[]{:S(2)}) collective-permute-start(bf16[64,2560]{1,0:T(8,128)(2,1)} %add_near.17), channel_id=1, source_target_pairs={{0,4},{1,5},{2,6},{3,7},{4,8},{5,9},{6,10},{7,11},{8,12},{9,13},{1... | collective-permute-start | bytes 983048 | tf_op jit(solution)/shard_map/ppermute | solution.py:72
  373.8 23.1 %collective-permute-start.38 = (bf16[64,2560]{1,0:T(8,128)(2,1)S(1)}, bf16[64,2560]{1,0:T(8,128)(2,1)S(1)}, u32[]{:S(2)}, u32[]{:S(2)}) collective-permute-start(bf16[64,2560]{1,0:T(8,128)(2,1)S(1)} %get-tuple-element.155.refs_0_), channel_id=1, source_target_pairs={{0,8},{1,9},{2,10},{3,11},{4,12},{5,13},{6,14},{7,15},{8,0},{9,1},... | collective-permute-start | bytes 983048 | tf_op jit(solution)/shard_map/ppermute | solution.py:72
  376.1 27.9 %collective-permute-start.37 = (bf16[64,2560]{1,0:T(8,128)(2,1)S(1)}, bf16[64,2560]{1,0:T(8,128)(2,1)S(1)}, u32[]{:S(2)}, u32[]{:S(2)}) collective-permute-start(bf16[64,2560]{1,0:T(8,128)(2,1)S(1)} %get-tuple-element.155.refs_0_), channel_id=1, source_target_pairs={{0,4},{1,5},{2,6},{3,7},{4,8},{5,9},{6,10},{7,11},{8,12},{9,13},{1... | collective-permute-start | bytes 983048 | tf_op jit(solution)/shard_map/ppermute | solution.py:72
  382.3 24.5 %collective-permute-start.44 = (bf16[64,2560]{1,0:T(8,128)(2,1)S(1)}, bf16[64,2560]{1,0:T(8,128)(2,1)S(1)}, u32[]{:S(2)}, u32[]{:S(2)}) collective-permute-start(bf16[64,2560]{1,0:T(8,128)(2,1)S(1)} %collective-permute-done.39.refs_3_), channel_id=1, source_target_pairs={{0,2},{1,3},{2,0},{3,1},{4,6},{5,7},{6,4},{7,5},{8,10},{9,11},{10,... | collective-permute-start | bytes 983048 | tf_op jit(solution)/shard_map/ppermute | solution.py:68
  452.2 32.6 %collective-permute-start.48 = (bf16[64,2560]{1,0:T(8,128)(2,1)}, bf16[64,2560]{1,0:T(8,128)(2,1)S(1)}, u32[]{:S(2)}, u32[]{:S(2)}) collective-permute-start(bf16[64,2560]{1,0:T(8,128)(2,1)} %get-tuple-element.164), channel_id=1, source_target_pairs={{0,2},{1,3},{2,0},{3,1},{4,6},{5,7},{6,4},{7,5},{8,10},{9,11},{10,... | collective-permute-start | bytes 983048 | tf_op jit(solution)/shard_map/ppermute | solution.py:68
  453.6 21.8 %collective-permute-start.51 = (bf16[64,2560]{1,0:T(8,128)(2,1)}, bf16[64,2560]{1,0:T(8,128)(2,1)S(1)}, u32[]{:S(2)}, u32[]{:S(2)}) collective-permute-start(bf16[64,2560]{1,0:T(8,128)(2,1)} %get-tuple-element.168), channel_id=1, source_target_pairs={{0,2},{1,3},{2,0},{3,1},{4,6},{5,7},{6,4},{7,5},{8,10},{9,11},{10,... | collective-permute-start | bytes 983048 | tf_op jit(solution)/shard_map/ppermute | solution.py:68
  454.8 27.7 %collective-permute-start.53 = (bf16[64,2560]{1,0:T(8,128)(2,1)}, bf16[64,2560]{1,0:T(8,128)(2,1)S(1)}, u32[]{:S(2)}, u32[]{:S(2)}) collective-permute-start(bf16[64,2560]{1,0:T(8,128)(2,1)} %get-tuple-element.170), channel_id=1, source_target_pairs={{0,2},{1,3},{2,0},{3,1},{4,6},{5,7},{6,4},{7,5},{8,10},{9,11},{10,... | collective-permute-start | bytes 983048 | tf_op jit(solution)/shard_map/ppermute | solution.py:68
  468.6 19.5 %collective-permute-start.50 = (bf16[64,2560]{1,0:T(8,128)(2,1)S(1)}, bf16[64,2560]{1,0:T(8,128)(2,1)S(1)}, u32[]{:S(2)}, u32[]{:S(2)}) collective-permute-start(bf16[64,2560]{1,0:T(8,128)(2,1)S(1)} %add_near.18), channel_id=1, source_target_pairs={{0,8},{1,9},{2,10},{3,11},{4,12},{5,13},{6,14},{7,15},{8,0},{9,1},... | collective-permute-start | bytes 983048 | tf_op jit(solution)/shard_map/ppermute | solution.py:72
  475.6 24.8 %collective-permute-start.52 = (bf16[64,2560]{1,0:T(8,128)(2,1)S(1)}, bf16[64,2560]{1,0:T(8,128)(2,1)S(1)}, u32[]{:S(2)}, u32[]{:S(2)}) collective-permute-start(bf16[64,2560]{1,0:T(8,128)(2,1)S(1)} %add_near.19), channel_id=1, source_target_pairs={{0,12},{1,13},{2,14},{3,15},{4,0},{5,1},{6,2},{7,3},{8,4},{9,5},{1... | collective-permute-start | bytes 983048 | tf_op jit(solution)/shard_map/ppermute | solution.py:72
  482.6 17.8 %collective-permute-start.54 = (bf16[64,2560]{1,0:T(8,128)(2,1)S(1)}, bf16[64,2560]{1,0:T(8,128)(2,1)S(1)}, u32[]{:S(2)}, u32[]{:S(2)}) collective-permute-start(bf16[64,2560]{1,0:T(8,128)(2,1)S(1)} %add_near.20), channel_id=1, source_target_pairs={{0,4},{1,5},{2,6},{3,7},{4,8},{5,9},{6,10},{7,11},{8,12},{9,13},{1... | collective-permute-start | bytes 983048 | tf_op jit(solution)/shard_map/ppermute | solution.py:72
  502.5 23.3 %collective-permute-start.57 = (bf16[64,2560]{1,0:T(8,128)(2,1)}, bf16[64,2560]{1,0:T(8,128)(2,1)}, u32[]{:S(2)}, u32[]{:S(2)}) collective-permute-start(bf16[64,2560]{1,0:T(8,128)(2,1)} %get-tuple-element.172.refs_0_), channel_id=1, source_target_pairs={{0,12},{1,13},{2,14},{3,15},{4,0},{5,1},{6,2},{7,3},{8,4},{9,5},{1... | collective-permute-start | bytes 983048 | tf_op jit(solution)/shard_map/ppermute | solution.py:72
  503.7 22.1 %collective-permute-start.56 = (bf16[64,2560]{1,0:T(8,128)(2,1)}, bf16[64,2560]{1,0:T(8,128)(2,1)}, u32[]{:S(2)}, u32[]{:S(2)}) collective-permute-start(bf16[64,2560]{1,0:T(8,128)(2,1)} %get-tuple-element.172.refs_0_), channel_id=1, source_target_pairs={{0,8},{1,9},{2,10},{3,11},{4,12},{5,13},{6,14},{7,15},{8,0},{9,1},... | collective-permute-start | bytes 983048 | tf_op jit(solution)/shard_map/ppermute | solution.py:72
  503.7 28.6 %collective-permute-start.55 = (bf16[64,2560]{1,0:T(8,128)(2,1)}, bf16[64,2560]{1,0:T(8,128)(2,1)}, u32[]{:S(2)}, u32[]{:S(2)}) collective-permute-start(bf16[64,2560]{1,0:T(8,128)(2,1)} %get-tuple-element.172.refs_0_), channel_id=1, source_target_pairs={{0,4},{1,5},{2,6},{3,7},{4,8},{5,9},{6,10},{7,11},{8,12},{9,13},{1... | collective-permute-start | bytes 983048 | tf_op jit(solution)/shard_map/ppermute | solution.py:72
  532.5 106.2 %all-to-all-start.2 = ((bf16[16,160,640]{2,1,0:T(8,128)(2,1)}), bf16[16,160,640]{2,1,0:T(8,128)(2,1)S(1)}, u32[]{:S(2)}, u32[]{:S(2)}) async-start(bf16[16,160,640]{2,1,0:T(8,128)(2,1)} %bitcast.77), calls=%async_computation.3 | async-start | bytes 6553600 | tf_op jit(solution)/shard_map/all_to_all | solution.py:80
  539.6 157.5 %reduce-scatter.5.cloned.1.call-start = ((), (), s32[]{:S(2)}) async-start(), calls=%async_computation.7 | async-start | bytes 5898240 | tf_op jit(solution)/shard_map/reduce_scatter | solution.py:218
  540.1 25.4 %collective-permute-start.59 = (bf16[64,2560]{1,0:T(8,128)(2,1)}, bf16[64,2560]{1,0:T(8,128)(2,1)S(1)}, u32[]{:S(2)}, u32[]{:S(2)}) collective-permute-start(bf16[64,2560]{1,0:T(8,128)(2,1)} %get-tuple-element.172.refs_0_), channel_id=1, source_target_pairs={{0,2},{1,3},{2,0},{3,1},{4,6},{5,7},{6,4},{7,5},{8,10},{9,11},{10,... | collective-permute-start | bytes 983048 | tf_op jit(solution)/shard_map/ppermute | solution.py:68
  565.4 24.4 %collective-permute-start.61 = (bf16[64,2560]{1,0:T(8,128)(2,1)}, bf16[64,2560]{1,0:T(8,128)(2,1)S(1)}, u32[]{:S(2)}, u32[]{:S(2)}) collective-permute-start(bf16[64,2560]{1,0:T(8,128)(2,1)} %collective-permute-done.56.refs_2_), channel_id=1, source_target_pairs={{0,2},{1,3},{2,0},{3,1},{4,6},{5,7},{6,4},{7,5},{8,10},{9,11},{10,... | collective-permute-start | bytes 983048 | tf_op jit(solution)/shard_map/ppermute | solution.py:68
  566.9 34.3 %collective-permute-start.60 = (bf16[64,2560]{1,0:T(8,128)(2,1)}, bf16[64,2560]{1,0:T(8,128)(2,1)S(1)}, u32[]{:S(2)}, u32[]{:S(2)}) collective-permute-start(bf16[64,2560]{1,0:T(8,128)(2,1)} %collective-permute-done.55.refs_1_), channel_id=1, source_target_pairs={{0,2},{1,3},{2,0},{3,1},{4,6},{5,7},{6,4},{7,5},{8,10},{9,11},{10,... | collective-permute-start | bytes 983048 | tf_op jit(solution)/shard_map/ppermute | solution.py:68
  568.5 34.7 %collective-permute-start.58 = (bf16[4,64,2560]{2,1,0:T(8,128)(2,1)S(1)}, bf16[4,64,2560]{2,1,0:T(8,128)(2,1)S(1)}, u32[]{:S(2)}, u32[]{:S(2)}) collective-permute-start(bf16[4,64,2560]{2,1,0:T(8,128)(2,1)S(1)} %stack.78.refs_0_), channel_id=1, source_target_pairs={{0,1},{1,0},{2,3},{3,2},{4,5},{5,4},{6,7},{7,6},{8,9},{9,8},{10,11... | collective-permute-start | bytes 3932168 | tf_op jit(solution)/shard_map/ppermute | solution.py:64
  639.2 39.4 %collective-permute-start.66 = (bf16[64,2560]{1,0:T(8,128)(2,1)}, bf16[64,2560]{1,0:T(8,128)(2,1)S(1)}, u32[]{:S(2)}, u32[]{:S(2)}) collective-permute-start(bf16[64,2560]{1,0:T(8,128)(2,1)} %copy-done.110), channel_id=1, source_target_pairs={{0,2},{1,3},{2,0},{3,1},{4,6},{5,7},{6,4},{7,5},{8,10},{9,11},{10,... | collective-permute-start | bytes 983048 | tf_op jit(solution)/shard_map/ppermute | solution.py:68
  639.8 15.9 %collective-permute-start.69 = (bf16[64,2560]{1,0:T(8,128)(2,1)}, bf16[64,2560]{1,0:T(8,128)(2,1)S(1)}, u32[]{:S(2)}, u32[]{:S(2)}) collective-permute-start(bf16[64,2560]{1,0:T(8,128)(2,1)} %copy-done.113), channel_id=1, source_target_pairs={{0,2},{1,3},{2,0},{3,1},{4,6},{5,7},{6,4},{7,5},{8,10},{9,11},{10,... | collective-permute-start | bytes 983048 | tf_op jit(solution)/shard_map/ppermute | solution.py:68
  640.7 34.9 %collective-permute-start.67 = (bf16[64,2560]{1,0:T(8,128)(2,1)}, bf16[64,2560]{1,0:T(8,128)(2,1)S(1)}, u32[]{:S(2)}, u32[]{:S(2)}) collective-permute-start(bf16[64,2560]{1,0:T(8,128)(2,1)} %copy-done.111), channel_id=1, source_target_pairs={{0,2},{1,3},{2,0},{3,1},{4,6},{5,7},{6,4},{7,5},{8,10},{9,11},{10,... | collective-permute-start | bytes 983048 | tf_op jit(solution)/shard_map/ppermute | solution.py:68
  641.3 28.5 %collective-permute-start.71 = (bf16[64,2560]{1,0:T(8,128)(2,1)}, bf16[64,2560]{1,0:T(8,128)(2,1)S(1)}, u32[]{:S(2)}, u32[]{:S(2)}) collective-permute-start(bf16[64,2560]{1,0:T(8,128)(2,1)} %copy-done.112), channel_id=1, source_target_pairs={{0,2},{1,3},{2,0},{3,1},{4,6},{5,7},{6,4},{7,5},{8,10},{9,11},{10,... | collective-permute-start | bytes 983048 | tf_op jit(solution)/shard_map/ppermute | solution.py:68
  655.9 22.8 %collective-permute-start.70 = (bf16[64,2560]{1,0:T(8,128)(2,1)S(1)}, bf16[64,2560]{1,0:T(8,128)(2,1)S(1)}, u32[]{:S(2)}, u32[]{:S(2)}) collective-permute-start(bf16[64,2560]{1,0:T(8,128)(2,1)S(1)} %add_near.22), channel_id=1, source_target_pairs={{0,12},{1,13},{2,14},{3,15},{4,0},{5,1},{6,2},{7,3},{8,4},{9,5},{1... | collective-permute-start | bytes 983048 | tf_op jit(solution)/shard_map/ppermute | solution.py:72
  675.7 20.1 %collective-permute-start.68 = (bf16[64,2560]{1,0:T(8,128)(2,1)S(1)}, bf16[64,2560]{1,0:T(8,128)(2,1)S(1)}, u32[]{:S(2)}, u32[]{:S(2)}) collective-permute-start(bf16[64,2560]{1,0:T(8,128)(2,1)S(1)} %add_near.21), channel_id=1, source_target_pairs={{0,8},{1,9},{2,10},{3,11},{4,12},{5,13},{6,14},{7,15},{8,0},{9,1},... | collective-permute-start | bytes 983048 | tf_op jit(solution)/shard_map/ppermute | solution.py:72
  697.1 54.7 %all-to-all-start.3 = ((bf16[16,160,384]{2,1,0:T(8,128)(2,1)}), bf16[16,160,384]{2,1,0:T(8,128)(2,1)}, u32[]{:S(2)}, u32[]{:S(2)}) async-start(bf16[16,160,384]{2,1,0:T(8,128)(2,1)} %bitcast.78), calls=%async_computation.5 | async-start | bytes 3932160 | tf_op jit(solution)/shard_map/all_to_all | solution.py:80
  (158 other events, 1533.5 us)
Sparse Core Ops, SparseCore 0:
  69.1 53.4 all-gather.4
  202.1 81.9 all-gather.6
  452.1 80.4 reduce-scatter.2
  638.9 55.5 reduce-scatter.4

commit v3 on v2

--- a/solution.py
+++ b/solution.py
@@ -95,7 +95,8 @@
 def gather_rows(own, *late, early=()):
     near = [own] + [move_z(own, m) for m in (1, 2, 3)]
     far = [move_x(own)]
-    far += [move_x(after(p, far[0], *early)) for p in near[1:]]
+    far += [move_x(after(near[1], far[0], *early)), None, move_x(after(near[3], far[0], *early))]
+    far[2] = move_x(after(near[2], far[1], far[3]))
     near_all, far_all = stack(near), stack(far)
     last = after(far_all, *late) if late else far_all
     return (near_all, move_c(near_all), far_all, move_c(last)), near, far
@@ -728,18 +729,6 @@
     ones = jnp.ones_like(norm_attn)
     extra = jnp.stack([norm_attn, norm_mlp, ones * counts[0], ones * counts[1]], axis=1)
     hidden = w_gate.shape[1] // 16
-    firsts = pack_first(w_query, key_matrix, value_matrix, w_out.T, extra, w_down.T)
-    seconds = pack_second(w_gate, w_up, w_down.T)
-    first_in = share_blocks(firsts)
-    pieces, near, far = gather_rows(own)
-    first_both = of_other(first_in)
-    second_in = share_blocks(after(seconds, first_both, *near, *far))
-    w_qkv, w_o, info = prepare_attention(place, first_in, first_both)
-    lengths = jnp.sum(info[2:4], axis=1) / F32(width // 16)
-    count = lengths[0] + lengths[1]
-    length = jnp.full((8, LANES), jnp.where(first, lengths[0], lengths[1]), F32)
-    factor = jnp.full((8, LANES), F32(seqs * seq_len) / count, F32)
-
     bit = jnp.arange(2, dtype=jnp.int32)
     pos = (
         jnp.arange(4, dtype=jnp.int32)[:, None, None, None] * (4 * seg)
@@ -756,6 +745,18 @@
     sine = jnp.concatenate([-sin_half, sin_half, pad], axis=1)
     kpos = pos[None, :]
 
+    firsts = pack_first(w_query, key_matrix, value_matrix, w_out.T, extra, w_down.T)
+    seconds = pack_second(after(w_gate, cosine, sine), w_up, w_down.T)
+    first_in = share_blocks(firsts)
+    first_both = of_other(first_in)
+    pieces, near, far = gather_rows(after(own, first_in), first_both)
+    second_in = share_blocks(after(seconds, *near, *far))
+    w_qkv, w_o, info = prepare_attention(place, first_in, first_both)
+    lengths = jnp.sum(info[2:4], axis=1) / F32(width // 16)
+    count = lengths[0] + lengths[1]
+    length = jnp.full((8, LANES), jnp.where(first, lengths[0], lengths[1]), F32)
+    factor = jnp.full((8, LANES), F32(seqs * seq_len) / count, F32)
+
     (h1, q, keys, values, ctx, lse), part = attention(
         place, pieces, w_qkv, w_o, info, length, kpos, cosine, sine
     )
@@ -778,13 +779,13 @@
     summed = over_sequences(shares)
     dresid, da_own = rows_after_feed_back(terms, resid, dout, info)
     pieces, near, far = gather_rows(da_own)
-    seconds = share_blocks(after(summed, *near))
+    seconds = share_blocks(after(summed, *near, *far))
     da, dqkv, part = attention_back(
         place, pieces, w_qkv, w_o, length, kpos, cosine, sine, q, keys, values, lse
     )
-    terms, far, _ = scatter_rows(part)
+    terms, far, x_come = scatter_rows(part)
     shares = attention_grads(place, h1, after(dqkv, *far), da, ctx, w_qkv, rest, tail2, squares)
-    summed = over_sequences(after(shares, seconds))
+    summed = over_sequences(after(shares, seconds, x_come[2]))
     dx = rows_at_end(terms, own, dresid, info)
     firsts = share_blocks(after(summed, seconds, dx))
     grad_gate, grad_up = unpack_second(after(seconds, dx), hidden)

time: 778 us -> 743 us (0.955)
  blocking collectives: 51 us -> 0 us
  local copies, waits for them, and re-layouts: 74.7 us -> 89.5 us
  starting transfers between devices: 105 us -> 117 us
  waiting for transfers between devices: 407 us -> 398 us
    all_to_all x3 -> x4, waiting for transfers between devices: 32.6 us -> 99.3 us  [share_out(): return lax.all_to_all(a, 'context', split_axis=0, concat_axis=0, tiled=True)]
    ppermute x32, waiting for transfers between devices: 178 us -> 117 us  [move_x(): return lax.ppermute(a, 'context', [(k, k ^ 2) for k in range(16)])]
    all_to_all x1 -> x0, blocking collectives: 51 us -> none  [share_out(): return lax.all_to_all(a, 'context', split_axis=0, concat_axis=0, tiled=True)]
    unnamed x250 -> x290, local copies, waits for them, and re-layouts: 67.8 us -> 82.6 us
    all_to_all x3 -> x4, starting transfers between devices: 23.5 us -> 35.8 us  [share_out(): return lax.all_to_all(a, 'context', split_axis=0, concat_axis=0, tiled=True)]
    ppermute x24, waiting for transfers between devices: 144 us -> 134 us  [move_z(): lax.ppermute(a, 'context', [(k, (k + 4 * step) % 16) for k in range(16)])]
    all_gather x2, waiting for transfers between devices: 18.5 us -> 9.58 us  [of_other(): return lax.all_gather(a, 'tensor', axis=0, tiled=False)]
    ppermute x24, starting transfers between devices: 42.8 us -> 34.8 us  [move_z(): lax.ppermute(a, 'context', [(k, (k + 4 * step) % 16) for k in range(16)])]
  transfers between devices with their start and end apart: 81 -> 82, of which waited for: 55 -> 55; matrix products, arithmetic and copies ran while one was open for 1% -> 1% of each run, Pallas kernels for 9% -> 9%
where the time goes in v3:
time: 743 us; the launch traced here: 736 us
  waiting for transfers between devices  398 us (54%)
  starting transfers between devices  117 us (16%)
  Pallas kernels  103 us (14%)
  local copies, waits for them, and re-layouts  89.5 us (12%)
  between operations  19.4 us (3%)
  other arithmetic  8.96 us (1%)
    ppermute x24, waiting for transfers between devices, move_z(): lax.ppermute(a, 'context', [(k, (k + 4 * step) % 16) for k in range(16)])  134 us
    ppermute x32, waiting for transfers between devices, move_x(): return lax.ppermute(a, 'context', [(k, k ^ 2) for k in range(16)])  117 us
    pallas_call x41, Pallas kernels, kernel_call(): pl.pallas_call(body, out_shape=outs, in_specs=[spec(i) for i in range(len...  103 us
    all_to_all x4, waiting for transfers between devices, share_out(): return lax.all_to_all(a, 'context', split_axis=0, concat_axis=0, tiled=True)  99.3 us
    unnamed x290, local copies, waits for them, and re-layouts  82.6 us
    all_to_all x4, starting transfers between devices, share_out(): return lax.all_to_all(a, 'context', split_axis=0, concat_axis=0, tiled=True)  35.8 us
    ppermute x24, starting transfers between devices, move_z(): lax.ppermute(a, 'context', [(k, (k + 4 * step) % 16) for k in range(16)])  34.8 us
    ppermute x32, starting transfers between devices, move_x(): return lax.ppermute(a, 'context', [(k, k ^ 2) for k in range(16)])  24.5 us
  transfers between devices with their start and end apart: 82, of which 55 were waited for; matrix products, arithmetic and copies ran while one was open for 1% of the time, Pallas kernels for 9%

profile of v3, /device:TPU:11, one launch (start us, length us, event | category | flops | bytes accessed | tf_op | source)
XLA Modules:
  0.0 736.3 jit_solution(968191180553591186)
XLA Ops:
  19.3 6.6 all-to-all-start
  26.0 44.4 %all-to-all-done.mine_ref.fm_ref = bf16[16,160,384]{2,1,0:T(8,128)(2,1)S(1)} async-done(((bf16[16,160,384]{2,1,0:T(8,128)(2,1)}), bf16[16,160,384]{2,1,0:T(8,128)(2,1)S(1)}, u32[]{:S(2)}, u32[]{:S(2)}) %all-to-all-start) | async-done | bytes 1966112 | tf_op jit(solution)/shard_map/all_to_all | solution.py:80
  81.2 6.3 collective-permute-done.refs_1_
  88.9 10.9 %collective-permute-done.1.refs_2_ = bf16[64,2560]{1,0:T(8,128)(2,1)} collective-permute-done((bf16[64,2560]{1,0:T(8,128)(2,1)S(1)}, bf16[64,2560]{1,0:T(8,128)(2,1)}, u32[]{:S(2)}, u32[]{:S(2)}) %collective-permute-start.1) | collective-permute-done | bytes 327712 | tf_op jit(solution)/shard_map/ppermute | solution.py:72
  110.2 12.1 %all-to-all-start.1 = ((bf16[16,160,640]{2,1,0:T(8,128)(2,1)}), bf16[16,160,640]{2,1,0:T(8,128)(2,1)}, u32[]{:S(2)}, u32[]{:S(2)}) async-start(bf16[16,160,640]{2,1,0:T(8,128)(2,1)} %pack_second.1), calls=%async_computation.1 | async-start | bytes 6553600 | tf_op jit(solution)/shard_map/all_to_all | solution.py:80
  146.0 18.6 %attention.1 = (bf16[1024,2560]{1,0:T(8,128)(2,1)S(1)}, bf16[2,1024,128]{2,1,0:T(8,128)(2,1)S(1)}, bf16[2,1024,128]{2,1,0:T(8,128)(2,1)S(1)}, bf16[2,1024,128]{2...) custom-call(s32[4]{0:T(128)S(1)} %pad_add_fusion.place_ref, ...), custom_call_target="tpu_custom_call" | custom-call | tf_op jit(solution)/shard_map/attention/pallas_call | solution.py:39
  176.4 8.9 %collective-permute-done.12.c_ref = bf16[64,2560]{1,0:T(8,128)(2,1)S(1)} collective-permute-done((bf16[64,2560]{1,0:T(8,128)(2,1)S(1)}, bf16[64,2560]{1,0:T(8,128)(2,1)S(1)}, u32[]{:S(2)}, u32[]{:S(2)}) %collective-permute-start.12) | collective-permute-done | bytes 327712 | tf_op jit(solution)/shard_map/ppermute | solution.py:68
  185.2 9.9 %all-to-all-done.1.m_ref = bf16[16,160,640]{2,1,0:T(8,128)(2,1)} async-done(((bf16[16,160,640]{2,1,0:T(8,128)(2,1)}), bf16[16,160,640]{2,1,0:T(8,128)(2,1)}, u32[]{:S(2)}, u32[]{:S(2)}) %all-to-all-start.1) | async-done | bytes 3276832 | tf_op jit(solution)/shard_map/all_to_all | solution.py:80
  200.0 11.8 %collective-permute-done.14.c_ref = bf16[64,2560]{1,0:T(8,128)(2,1)S(1)} collective-permute-done((bf16[64,2560]{1,0:T(8,128)(2,1)}, bf16[64,2560]{1,0:T(8,128)(2,1)S(1)}, u32[]{:S(2)}, u32[]{:S(2)}) %collective-permute-start.14) | collective-permute-done | bytes 327712 | tf_op jit(solution)/shard_map/ppermute | solution.py:68
  212.0 6.8 collective-permute-done.16.c_ref
  219.9 9.0 %collective-permute-done.17.refs_5_ = bf16[64,2560]{1,0:T(8,128)(2,1)S(1)} collective-permute-done((bf16[64,2560]{1,0:T(8,128)(2,1)S(1)}, bf16[64,2560]{1,0:T(8,128)(2,1)S(1)}, u32[]{:S(2)}, u32[]{:S(2)}) %collective-permute-start.17) | collective-permute-done | bytes 327712 | tf_op jit(solution)/shard_map/ppermute | solution.py:72
  231.8 4.4 collective-permute-start.19
  239.3 8.7 %collective-permute-done.18.refs_1_ = bf16[64,2560]{1,0:T(8,128)(2,1)S(1)} collective-permute-done((bf16[64,2560]{1,0:T(8,128)(2,1)S(1)}, bf16[64,2560]{1,0:T(8,128)(2,1)S(1)}, u32[]{:S(2)}, u32[]{:S(2)}) %collective-permute-start.18) | collective-permute-done | bytes 327712 | tf_op jit(solution)/shard_map/ppermute | solution.py:72
  248.9 9.6 %collective-permute-done.19.refs_2_ = bf16[64,2560]{1,0:T(8,128)(2,1)S(1)} collective-permute-done((bf16[64,2560]{1,0:T(8,128)(2,1)S(1)}, bf16[64,2560]{1,0:T(8,128)(2,1)S(1)}, u32[]{:S(2)}, u32[]{:S(2)}) %collective-permute-start.19) | collective-permute-done | bytes 327712 | tf_op jit(solution)/shard_map/ppermute | solution.py:72
  260.1 11.5 %collective-permute-start.21 = (bf16[4,64,2560]{2,1,0:T(8,128)(2,1)S(1)}, bf16[4,64,2560]{2,1,0:T(8,128)(2,1)}, u32[]{:S(2)}, u32[]{:S(2)}) collective-permute-start(bf16[4,64,2560]{2,1,0:T(8,128)(2,1)S(1)} %stack.74.refs_0_), channel_id=1, source_target_pairs={{0,1},{1,0},{2,3},{3,2},{4,5},{5,4},{6,7},{7,6},{8,9},{9,8},{10,11... | collective-permute-start | bytes 3932168 | tf_op jit(solution)/shard_map/ppermute | solution.py:64
  272.7 5.5 all-gather.7.cloned.1.call-done
  283.1 4.8 prepare_feed.1
  291.4 10.2 %feed.1 = (bf16[1024,2560]{1,0:T(8,128)(2,1)S(1)}, f32[1024,864]{1,0:T(8,128)S(1)}, bf16[1024,432]{1,0:T(8,128)(2,1)S(1)}, bf16[4,64,2560]{2,1,0:T(8,128)(2,1)},...) custom-call(bf16[4,64,2560]{2,1,0:T(8,128)(2,1)S(1)} %stack.74.refs_, ...), custom_call_target="tpu_custom_call" | custom-call | tf_op jit(solution)/shard_map/feed/pallas_call | solution.py:39
  318.7 11.8 %collective-permute-done.30.c_ref = bf16[64,2560]{1,0:T(8,128)(2,1)S(1)} collective-permute-done((bf16[64,2560]{1,0:T(8,128)(2,1)S(1)}, bf16[64,2560]{1,0:T(8,128)(2,1)S(1)}, u32[]{:S(2)}, u32[]{:S(2)}) %collective-permute-start.30) | collective-permute-done | bytes 327712 | tf_op jit(solution)/shard_map/ppermute | solution.py:68
  338.8 5.8 collective-permute-done.34.c_ref
  348.8 6.5 collective-permute-done.31.refs_3_
  356.0 5.8 collective-permute-done.33.refs_4_
  378.1 7.8 %collective-permute-done.37.refs_1_ = bf16[64,2560]{1,0:T(8,128)(2,1)S(1)} collective-permute-done((bf16[64,2560]{1,0:T(8,128)(2,1)S(1)}, bf16[64,2560]{1,0:T(8,128)(2,1)S(1)}, u32[]{:S(2)}, u32[]{:S(2)}) %collective-permute-start.37) | collective-permute-done | bytes 327712 | tf_op jit(solution)/shard_map/ppermute | solution.py:72
  387.0 10.1 %collective-permute-done.38.refs_2_ = bf16[64,2560]{1,0:T(8,128)(2,1)S(1)} collective-permute-done((bf16[64,2560]{1,0:T(8,128)(2,1)S(1)}, bf16[64,2560]{1,0:T(8,128)(2,1)S(1)}, u32[]{:S(2)}, u32[]{:S(2)}) %collective-permute-start.38) | collective-permute-done | bytes 327712 | tf_op jit(solution)/shard_map/ppermute | solution.py:72
  400.2 4.4 collective-permute-done.44.refs_2_
  412.1 8.8 %feed_back.1 = (bf16[1024,2560]{1,0:T(8,128)(2,1)S(1)}, bf16[1024,864]{1,0:T(8,128)(2,1)S(1)}, bf16[4,64,2560]{2,1,0:T(8,128)(2,1)S(1)}, bf16[4,64,2560]{2,1,0:T...) custom-call(bf16[4,64,2560]{2,1,0:T(8,128)(2,1)S(1)} %stack.76.refs_, ...), custom_call_target="tpu_custom_call" | custom-call | tf_op jit(solution)/shard_map/feed_back/pallas_call | solution.py:39
  428.0 8.9 %feed_grads.1 = (bf16[2,16,160,640]{3,2,1,0:T(8,128)(2,1)S(1)}, bf16[2560,16]{1,0:T(8,128)(2,1)S(1)}, f32[2560,1]{1,0:T(8,128)S(1)}) custom-call(s32[4]{0:T(128)S(1)} %pad_add_fusion.place_ref, bf16[2560,432]{1,0:T(8,128)(2,1)S(1)} %down_grads.1.down_ref, bf16[1024,2560]{1,0:T(8,128)(2,1)S(1)} %bitcast.71, bf16[1024,864]{1,0:T(8,128)(2,1)S(1)} %get-tuple-element.201.dgu_ref, ...), custom_call_target="tpu_custom_call" | custom-call | tf_op jit(solution)/shard_map/feed_grads/pallas_call | solution.py:39
  444.9 13.1 %collective-permute-done.49.c_ref = bf16[64,2560]{1,0:T(8,128)(2,1)S(1)} collective-permute-done((bf16[64,2560]{1,0:T(8,128)(2,1)}, bf16[64,2560]{1,0:T(8,128)(2,1)S(1)}, u32[]{:S(2)}, u32[]{:S(2)}) %collective-permute-start.49) | collective-permute-done | bytes 327712 | tf_op jit(solution)/shard_map/ppermute | solution.py:68
  467.4 4.6 collective-permute-done.53.c_ref
  472.5 9.2 %collective-permute-done.50.refs_3_ = bf16[64,2560]{1,0:T(8,128)(2,1)S(1)} collective-permute-done((bf16[64,2560]{1,0:T(8,128)(2,1)S(1)}, bf16[64,2560]{1,0:T(8,128)(2,1)S(1)}, u32[]{:S(2)}, u32[]{:S(2)}) %collective-permute-start.50) | collective-permute-done | bytes 327712 | tf_op jit(solution)/shard_map/ppermute | solution.py:72
  481.6 9.0 %collective-permute-done.52.refs_4_ = bf16[64,2560]{1,0:T(8,128)(2,1)S(1)} collective-permute-done((bf16[64,2560]{1,0:T(8,128)(2,1)S(1)}, bf16[64,2560]{1,0:T(8,128)(2,1)S(1)}, u32[]{:S(2)}, u32[]{:S(2)}) %collective-permute-start.52) | collective-permute-done | bytes 327712 | tf_op jit(solution)/shard_map/ppermute | solution.py:72
  503.5 6.2 collective-permute-done.55.refs_1_
  511.0 11.3 %collective-permute-done.56.refs_2_ = bf16[64,2560]{1,0:T(8,128)(2,1)S(1)} collective-permute-done((bf16[64,2560]{1,0:T(8,128)(2,1)S(1)}, bf16[64,2560]{1,0:T(8,128)(2,1)S(1)}, u32[]{:S(2)}, u32[]{:S(2)}) %collective-permute-start.56) | collective-permute-done | bytes 327712 | tf_op jit(solution)/shard_map/ppermute | solution.py:72
  525.0 6.7 collective-permute-done.62.refs_2_
  532.5 10.8 %all-to-all-start.2 = ((bf16[16,160,640]{2,1,0:T(8,128)(2,1)}), bf16[16,160,640]{2,1,0:T(8,128)(2,1)S(1)}, u32[]{:S(2)}, u32[]{:S(2)}) async-start(bf16[16,160,640]{2,1,0:T(8,128)(2,1)} %bitcast.77), calls=%async_computation.3 | async-start | bytes 6553600 | tf_op jit(solution)/shard_map/all_to_all | solution.py:80
  560.2 11.6 %attention_back.1 = (bf16[1024,2560]{1,0:T(8,128)(2,1)S(1)}, bf16[1024,480]{1,0:T(8,128)(2,1)S(1)}, bf16[4,64,2560]{2,1,0:T(8,128)(2,1)S(1)}, bf16[4,64,2560]{2,...) custom-call(s32[4]{0:T(128)S(1)} %pad_add_fusion.place_ref, ...), custom_call_target="tpu_custom_call" | custom-call | tf_op jit(solution)/shard_map/attention_back/pallas_call | solution.py:39
  579.6 7.2 attention_grads.1
  588.7 4.4 collective-permute-done.65.c_ref
  593.1 23.0 %all-to-all-done.2.s_ref = bf16[16,160,640]{2,1,0:T(8,128)(2,1)S(1)} async-done(((bf16[16,160,640]{2,1,0:T(8,128)(2,1)}), bf16[16,160,640]{2,1,0:T(8,128)(2,1)S(1)}, u32[]{:S(2)}, u32[]{:S(2)}) %all-to-all-start.2) | async-done | bytes 3276832 | tf_op jit(solution)/shard_map/all_to_all | solution.py:80
  619.5 13.2 %collective-permute-done.69.c_ref = bf16[64,2560]{1,0:T(8,128)(2,1)S(1)} collective-permute-done((bf16[64,2560]{1,0:T(8,128)(2,1)}, bf16[64,2560]{1,0:T(8,128)(2,1)S(1)}, u32[]{:S(2)}, u32[]{:S(2)}) %collective-permute-start.69) | collective-permute-done | bytes 327712 | tf_op jit(solution)/shard_map/ppermute | solution.py:68
  632.9 6.8 collective-permute-done.71.c_ref
  642.3 7.5 %collective-permute-done.72.refs_5_ = bf16[64,2560]{1,0:T(8,128)(2,1)S(1)} collective-permute-done((bf16[64,2560]{1,0:T(8,128)(2,1)S(1)}, bf16[64,2560]{1,0:T(8,128)(2,1)S(1)}, u32[]{:S(2)}, u32[]{:S(2)}) %collective-permute-start.72) | collective-permute-done | bytes 327712 | tf_op jit(solution)/shard_map/ppermute | solution.py:72
  649.8 13.4 %collective-permute-done.68.refs_3_ = bf16[64,2560]{1,0:T(8,128)(2,1)S(1)} collective-permute-done((bf16[64,2560]{1,0:T(8,128)(2,1)S(1)}, bf16[64,2560]{1,0:T(8,128)(2,1)S(1)}, u32[]{:S(2)}, u32[]{:S(2)}) %collective-permute-start.68) | collective-permute-done | bytes 327712 | tf_op jit(solution)/shard_map/ppermute | solution.py:72
  666.8 6.4 all-to-all-start.3
  673.4 9.0 %collective-permute-done.36 = bf16[64,2560]{1,0:T(8,128)(2,1)} collective-permute-done((bf16[64,2560]{1,0:T(8,128)(2,1)}, bf16[64,2560]{1,0:T(8,128)(2,1)}, u32[]{:S(2)}, u32[]{:S(2)}) %collective-permute-start.36) | collective-permute-done | bytes 327712 | tf_op jit(solution)/shard_map/ppermute | solution.py:76
  684.8 7.0 collective-permute-done.73
  695.8 22.0 %all-to-all-done.3.f_ref = bf16[16,160,384]{2,1,0:T(8,128)(2,1)} async-done(((bf16[16,160,384]{2,1,0:T(8,128)(2,1)}), bf16[16,160,384]{2,1,0:T(8,128)(2,1)}, u32[]{:S(2)}, u32[]{:S(2)}) %all-to-all-start.3) | async-done | bytes 1966112 | tf_op jit(solution)/shard_map/all_to_all | solution.py:80
  719.8 6.1 unpack_first.1
  (497 shorter events, 238.8 us)
Async XLA Ops:
  19.3 51.2 %all-to-all-start = ((bf16[16,160,384]{2,1,0:T(8,128)(2,1)}), bf16[16,160,384]{2,1,0:T(8,128)(2,1)S(1)}, u32[]{:S(2)}, u32[]{:S(2)}) async-start(bf16[16,160,384]{2,1,0:T(8,128)(2,1)} %copy-done.15), calls=%async_computation | async-start | bytes 3932160 | tf_op jit(solution)/shard_map/all_to_all | solution.py:80
  25.8 103.8 %all-gather.5.cloned.1.call-start = ((), (), s32[]{:S(2)}) async-start(), calls=%async_computation.8 | async-start | bytes 5898240 | tf_op jit(solution)/shard_map/all_gather | solution.py:215
  70.5 17.0 %collective-permute-start = (bf16[64,2560]{1,0:T(8,128)(2,1)S(1)}, bf16[64,2560]{1,0:T(8,128)(2,1)S(1)}, u32[]{:S(2)}, u32[]{:S(2)}) collective-permute-start(bf16[64,2560]{1,0:T(8,128)(2,1)S(1)} %dynamic-slice_bitcast_fusion.2.refs_0_.refs_6_), channel_id=1, source_target_pairs={{0,4},{1,5},{2,6},{3,7},{4,8},{5,9},{6,10},{7,11},{8,12},{9,13},{1... | collective-permute-start | bytes 983048 | tf_op jit(solution)/shard_map/ppermute | solution.py:72
  72.0 27.8 %collective-permute-start.1 = (bf16[64,2560]{1,0:T(8,128)(2,1)S(1)}, bf16[64,2560]{1,0:T(8,128)(2,1)}, u32[]{:S(2)}, u32[]{:S(2)}) collective-permute-start(bf16[64,2560]{1,0:T(8,128)(2,1)S(1)} %dynamic-slice_bitcast_fusion.2.refs_0_.refs_6_), channel_id=1, source_target_pairs={{0,8},{1,9},{2,10},{3,11},{4,12},{5,13},{6,14},{7,15},{8,0},{9,1},... | collective-permute-start | bytes 983048 | tf_op jit(solution)/shard_map/ppermute | solution.py:72
  79.6 20.3 %collective-permute-start.6 = (bf16[64,2560]{1,0:T(8,128)(2,1)S(1)}, bf16[64,2560]{1,0:T(8,128)(2,1)S(1)}, u32[]{:S(2)}, u32[]{:S(2)}) collective-permute-start(bf16[64,2560]{1,0:T(8,128)(2,1)S(1)} %collective-permute-done.2.refs_3_), channel_id=1, source_target_pairs={{0,2},{1,3},{2,0},{3,1},{4,6},{5,7},{6,4},{7,5},{8,10},{9,11},{10,... | collective-permute-start | bytes 983048 | tf_op jit(solution)/shard_map/ppermute | solution.py:68
  87.5 12.4 %collective-permute-start.5 = (bf16[64,2560]{1,0:T(8,128)(2,1)S(1)}, bf16[64,2560]{1,0:T(8,128)(2,1)S(1)}, u32[]{:S(2)}, u32[]{:S(2)}) collective-permute-start(bf16[64,2560]{1,0:T(8,128)(2,1)S(1)} %collective-permute-done.refs_1_), channel_id=1, source_target_pairs={{0,2},{1,3},{2,0},{3,1},{4,6},{5,7},{6,4},{7,5},{8,10},{9,11},{10,... | collective-permute-start | bytes 983048 | tf_op jit(solution)/shard_map/ppermute | solution.py:68
  110.2 84.9 %all-to-all-start.1 = ((bf16[16,160,640]{2,1,0:T(8,128)(2,1)}), bf16[16,160,640]{2,1,0:T(8,128)(2,1)}, u32[]{:S(2)}, u32[]{:S(2)}) async-start(bf16[16,160,640]{2,1,0:T(8,128)(2,1)} %pack_second.1), calls=%async_computation.1 | async-start | bytes 6553600 | tf_op jit(solution)/shard_map/all_to_all | solution.py:80
  122.3 155.9 %all-gather.7.cloned.1.call-start = ((), (), s32[]{:S(2)}) async-start(), calls=%async_computation.9 | async-start | bytes 9830400 | tf_op jit(solution)/shard_map/all_gather | solution.py:215
  123.8 15.7 %collective-permute-start.3 = (bf16[4,64,2560]{2,1,0:T(8,128)(2,1)S(1)}, bf16[4,64,2560]{2,1,0:T(8,128)(2,1)}, u32[]{:S(2)}, u32[]{:S(2)}) collective-permute-start(bf16[4,64,2560]{2,1,0:T(8,128)(2,1)S(1)} %stack.72.refs_0_), channel_id=1, source_target_pairs={{0,1},{1,0},{2,3},{3,2},{4,5},{5,4},{6,7},{7,6},{8,9},{9,8},{10,11... | collective-permute-start | bytes 3932168 | tf_op jit(solution)/shard_map/ppermute | solution.py:64
  195.1 337.4 %reduce-scatter.3.cloned.1.call-start = ((), (), s32[]{:S(2)}) async-start(), calls=%async_computation.6 | async-start | bytes 9830400 | tf_op jit(solution)/shard_map/reduce_scatter | solution.py:219
  195.5 24.4 %collective-permute-start.11 = (bf16[64,2560]{1,0:T(8,128)(2,1)}, bf16[64,2560]{1,0:T(8,128)(2,1)S(1)}, u32[]{:S(2)}, u32[]{:S(2)}) collective-permute-start(bf16[64,2560]{1,0:T(8,128)(2,1)} %get-tuple-element.130), channel_id=1, source_target_pairs={{0,2},{1,3},{2,0},{3,1},{4,6},{5,7},{6,4},{7,5},{8,10},{9,11},{10,... | collective-permute-start | bytes 983048 | tf_op jit(solution)/shard_map/ppermute | solution.py:68
  195.5 16.3 %collective-permute-start.14 = (bf16[64,2560]{1,0:T(8,128)(2,1)}, bf16[64,2560]{1,0:T(8,128)(2,1)S(1)}, u32[]{:S(2)}, u32[]{:S(2)}) collective-permute-start(bf16[64,2560]{1,0:T(8,128)(2,1)} %get-tuple-element.134), channel_id=1, source_target_pairs={{0,2},{1,3},{2,0},{3,1},{4,6},{5,7},{6,4},{7,5},{8,10},{9,11},{10,... | collective-permute-start | bytes 983048 | tf_op jit(solution)/shard_map/ppermute | solution.py:68
  196.9 21.9 %collective-permute-start.16 = (bf16[64,2560]{1,0:T(8,128)(2,1)}, bf16[64,2560]{1,0:T(8,128)(2,1)S(1)}, u32[]{:S(2)}, u32[]{:S(2)}) collective-permute-start(bf16[64,2560]{1,0:T(8,128)(2,1)} %get-tuple-element.136), channel_id=1, source_target_pairs={{0,2},{1,3},{2,0},{3,1},{4,6},{5,7},{6,4},{7,5},{8,10},{9,11},{10,... | collective-permute-start | bytes 983048 | tf_op jit(solution)/shard_map/ppermute | solution.py:68
  198.8 21.1 %collective-permute-start.13 = (bf16[64,2560]{1,0:T(8,128)(2,1)S(1)}, bf16[64,2560]{1,0:T(8,128)(2,1)S(1)}, u32[]{:S(2)}, u32[]{:S(2)}) collective-permute-start(bf16[64,2560]{1,0:T(8,128)(2,1)S(1)} %add_near.12), channel_id=1, source_target_pairs={{0,8},{1,9},{2,10},{3,11},{4,12},{5,13},{6,14},{7,15},{8,0},{9,1},... | collective-permute-start | bytes 983048 | tf_op jit(solution)/shard_map/ppermute | solution.py:72
  230.6 17.4 %collective-permute-start.18 = (bf16[64,2560]{1,0:T(8,128)(2,1)S(1)}, bf16[64,2560]{1,0:T(8,128)(2,1)S(1)}, u32[]{:S(2)}, u32[]{:S(2)}) collective-permute-start(bf16[64,2560]{1,0:T(8,128)(2,1)S(1)} %get-tuple-element.137.refs_0_), channel_id=1, source_target_pairs={{0,4},{1,5},{2,6},{3,7},{4,8},{5,9},{6,10},{7,11},{8,12},{9,13},{1... | collective-permute-start | bytes 983048 | tf_op jit(solution)/shard_map/ppermute | solution.py:72
  231.8 26.8 %collective-permute-start.19 = (bf16[64,2560]{1,0:T(8,128)(2,1)S(1)}, bf16[64,2560]{1,0:T(8,128)(2,1)S(1)}, u32[]{:S(2)}, u32[]{:S(2)}) collective-permute-start(bf16[64,2560]{1,0:T(8,128)(2,1)S(1)} %get-tuple-element.137.refs_0_), channel_id=1, source_target_pairs={{0,8},{1,9},{2,10},{3,11},{4,12},{5,13},{6,14},{7,15},{8,0},{9,1},... | collective-permute-start | bytes 983048 | tf_op jit(solution)/shard_map/ppermute | solution.py:72
  238.0 20.6 %collective-permute-start.24 = (bf16[64,2560]{1,0:T(8,128)(2,1)S(1)}, bf16[64,2560]{1,0:T(8,128)(2,1)S(1)}, u32[]{:S(2)}, u32[]{:S(2)}) collective-permute-start(bf16[64,2560]{1,0:T(8,128)(2,1)S(1)} %collective-permute-done.20.refs_3_), channel_id=1, source_target_pairs={{0,2},{1,3},{2,0},{3,1},{4,6},{5,7},{6,4},{7,5},{8,10},{9,11},{10,... | collective-permute-start | bytes 983048 | tf_op jit(solution)/shard_map/ppermute | solution.py:68
  258.5 13.0 %collective-permute-start.25 = (bf16[64,2560]{1,0:T(8,128)(2,1)S(1)}, bf16[64,2560]{1,0:T(8,128)(2,1)S(1)}, u32[]{:S(2)}, u32[]{:S(2)}) collective-permute-start(bf16[64,2560]{1,0:T(8,128)(2,1)S(1)} %collective-permute-done.19.refs_2_), channel_id=1, source_target_pairs={{0,2},{1,3},{2,0},{3,1},{4,6},{5,7},{6,4},{7,5},{8,10},{9,11},{10,... | collective-permute-start | bytes 983048 | tf_op jit(solution)/shard_map/ppermute | solution.py:68
  260.1 28.7 %collective-permute-start.21 = (bf16[4,64,2560]{2,1,0:T(8,128)(2,1)S(1)}, bf16[4,64,2560]{2,1,0:T(8,128)(2,1)}, u32[]{:S(2)}, u32[]{:S(2)}) collective-permute-start(bf16[4,64,2560]{2,1,0:T(8,128)(2,1)S(1)} %stack.74.refs_0_), channel_id=1, source_target_pairs={{0,1},{1,0},{2,3},{3,2},{4,5},{5,4},{6,7},{7,6},{8,9},{9,8},{10,11... | collective-permute-start | bytes 3932168 | tf_op jit(solution)/shard_map/ppermute | solution.py:64
  314.4 33.7 %collective-permute-start.29 = (bf16[64,2560]{1,0:T(8,128)(2,1)}, bf16[64,2560]{1,0:T(8,128)(2,1)S(1)}, u32[]{:S(2)}, u32[]{:S(2)}) collective-permute-start(bf16[64,2560]{1,0:T(8,128)(2,1)} %get-tuple-element.151), channel_id=1, source_target_pairs={{0,2},{1,3},{2,0},{3,1},{4,6},{5,7},{6,4},{7,5},{8,10},{9,11},{10,... | collective-permute-start | bytes 983048 | tf_op jit(solution)/shard_map/ppermute | solution.py:68
  314.8 15.7 %collective-permute-start.30 = (bf16[64,2560]{1,0:T(8,128)(2,1)S(1)}, bf16[64,2560]{1,0:T(8,128)(2,1)S(1)}, u32[]{:S(2)}, u32[]{:S(2)}) collective-permute-start(bf16[64,2560]{1,0:T(8,128)(2,1)S(1)} %get-tuple-element.153), channel_id=1, source_target_pairs={{0,2},{1,3},{2,0},{3,1},{4,6},{5,7},{6,4},{7,5},{8,10},{9,11},{10,... | collective-permute-start | bytes 983048 | tf_op jit(solution)/shard_map/ppermute | solution.py:68
  315.8 21.7 %collective-permute-start.32 = (bf16[64,2560]{1,0:T(8,128)(2,1)S(1)}, bf16[64,2560]{1,0:T(8,128)(2,1)S(1)}, u32[]{:S(2)}, u32[]{:S(2)}) collective-permute-start(bf16[64,2560]{1,0:T(8,128)(2,1)S(1)} %get-tuple-element.155), channel_id=1, source_target_pairs={{0,2},{1,3},{2,0},{3,1},{4,6},{5,7},{6,4},{7,5},{8,10},{9,11},{10,... | collective-permute-start | bytes 983048 | tf_op jit(solution)/shard_map/ppermute | solution.py:68
  316.3 28.3 %collective-permute-start.34 = (bf16[64,2560]{1,0:T(8,128)(2,1)S(1)}, bf16[64,2560]{1,0:T(8,128)(2,1)S(1)}, u32[]{:S(2)}, u32[]{:S(2)}) collective-permute-start(bf16[64,2560]{1,0:T(8,128)(2,1)S(1)} %get-tuple-element.157), channel_id=1, source_target_pairs={{0,2},{1,3},{2,0},{3,1},{4,6},{5,7},{6,4},{7,5},{8,10},{9,11},{10,... | collective-permute-start | bytes 983048 | tf_op jit(solution)/shard_map/ppermute | solution.py:68
  331.4 24.0 %collective-permute-start.31 = (bf16[64,2560]{1,0:T(8,128)(2,1)}, bf16[64,2560]{1,0:T(8,128)(2,1)S(1)}, u32[]{:S(2)}, u32[]{:S(2)}) collective-permute-start(bf16[64,2560]{1,0:T(8,128)(2,1)} %add_near.15), channel_id=1, source_target_pairs={{0,8},{1,9},{2,10},{3,11},{4,12},{5,13},{6,14},{7,15},{8,0},{9,1},... | collective-permute-start | bytes 983048 | tf_op jit(solution)/shard_map/ppermute | solution.py:72
  338.4 23.5 %collective-permute-start.33 = (bf16[64,2560]{1,0:T(8,128)(2,1)}, bf16[64,2560]{1,0:T(8,128)(2,1)}, u32[]{:S(2)}, u32[]{:S(2)}) collective-permute-start(bf16[64,2560]{1,0:T(8,128)(2,1)} %add_near.16), channel_id=1, source_target_pairs={{0,12},{1,13},{2,14},{3,15},{4,0},{5,1},{6,2},{7,3},{8,4},{9,5},{1... | collective-permute-start | bytes 983048 | tf_op jit(solution)/shard_map/ppermute | solution.py:72
  345.4 16.9 %collective-permute-start.35 = (bf16[64,2560]{1,0:T(8,128)(2,1)}, bf16[64,2560]{1,0:T(8,128)(2,1)}, u32[]{:S(2)}, u32[]{:S(2)}) collective-permute-start(bf16[64,2560]{1,0:T(8,128)(2,1)} %add_near.17), channel_id=1, source_target_pairs={{0,4},{1,5},{2,6},{3,7},{4,8},{5,9},{6,10},{7,11},{8,12},{9,13},{1... | collective-permute-start | bytes 983048 | tf_op jit(solution)/shard_map/ppermute | solution.py:72
  367.5 18.3 %collective-permute-start.37 = (bf16[64,2560]{1,0:T(8,128)(2,1)S(1)}, bf16[64,2560]{1,0:T(8,128)(2,1)S(1)}, u32[]{:S(2)}, u32[]{:S(2)}) collective-permute-start(bf16[64,2560]{1,0:T(8,128)(2,1)S(1)} %get-tuple-element.161.refs_0_), channel_id=1, source_target_pairs={{0,4},{1,5},{2,6},{3,7},{4,8},{5,9},{6,10},{7,11},{8,12},{9,13},{1... | collective-permute-start | bytes 983048 | tf_op jit(solution)/shard_map/ppermute | solution.py:72
  369.7 27.3 %collective-permute-start.38 = (bf16[64,2560]{1,0:T(8,128)(2,1)S(1)}, bf16[64,2560]{1,0:T(8,128)(2,1)S(1)}, u32[]{:S(2)}, u32[]{:S(2)}) collective-permute-start(bf16[64,2560]{1,0:T(8,128)(2,1)S(1)} %get-tuple-element.161.refs_0_), channel_id=1, source_target_pairs={{0,8},{1,9},{2,10},{3,11},{4,12},{5,13},{6,14},{7,15},{8,0},{9,1},... | collective-permute-start | bytes 983048 | tf_op jit(solution)/shard_map/ppermute | solution.py:72
  377.1 20.0 %collective-permute-start.43 = (bf16[64,2560]{1,0:T(8,128)(2,1)S(1)}, bf16[64,2560]{1,0:T(8,128)(2,1)S(1)}, u32[]{:S(2)}, u32[]{:S(2)}) collective-permute-start(bf16[64,2560]{1,0:T(8,128)(2,1)S(1)} %collective-permute-done.39.refs_3_), channel_id=1, source_target_pairs={{0,2},{1,3},{2,0},{3,1},{4,6},{5,7},{6,4},{7,5},{8,10},{9,11},{10,... | collective-permute-start | bytes 983048 | tf_op jit(solution)/shard_map/ppermute | solution.py:68
  441.7 30.8 %collective-permute-start.48 = (bf16[64,2560]{1,0:T(8,128)(2,1)}, bf16[64,2560]{1,0:T(8,128)(2,1)S(1)}, u32[]{:S(2)}, u32[]{:S(2)}) collective-permute-start(bf16[64,2560]{1,0:T(8,128)(2,1)} %get-tuple-element.170), channel_id=1, source_target_pairs={{0,2},{1,3},{2,0},{3,1},{4,6},{5,7},{6,4},{7,5},{8,10},{9,11},{10,... | collective-permute-start | bytes 983048 | tf_op jit(solution)/shard_map/ppermute | solution.py:68
  442.7 15.3 %collective-permute-start.49 = (bf16[64,2560]{1,0:T(8,128)(2,1)}, bf16[64,2560]{1,0:T(8,128)(2,1)S(1)}, u32[]{:S(2)}, u32[]{:S(2)}) collective-permute-start(bf16[64,2560]{1,0:T(8,128)(2,1)} %get-tuple-element.172), channel_id=1, source_target_pairs={{0,2},{1,3},{2,0},{3,1},{4,6},{5,7},{6,4},{7,5},{8,10},{9,11},{10,... | collective-permute-start | bytes 983048 | tf_op jit(solution)/shard_map/ppermute | solution.py:68
  443.2 21.8 %collective-permute-start.51 = (bf16[64,2560]{1,0:T(8,128)(2,1)}, bf16[64,2560]{1,0:T(8,128)(2,1)S(1)}, u32[]{:S(2)}, u32[]{:S(2)}) collective-permute-start(bf16[64,2560]{1,0:T(8,128)(2,1)} %get-tuple-element.174), channel_id=1, source_target_pairs={{0,2},{1,3},{2,0},{3,1},{4,6},{5,7},{6,4},{7,5},{8,10},{9,11},{10,... | collective-permute-start | bytes 983048 | tf_op jit(solution)/shard_map/ppermute | solution.py:68
  444.1 27.9 %collective-permute-start.53 = (bf16[64,2560]{1,0:T(8,128)(2,1)}, bf16[64,2560]{1,0:T(8,128)(2,1)S(1)}, u32[]{:S(2)}, u32[]{:S(2)}) collective-permute-start(bf16[64,2560]{1,0:T(8,128)(2,1)} %get-tuple-element.176), channel_id=1, source_target_pairs={{0,2},{1,3},{2,0},{3,1},{4,6},{5,7},{6,4},{7,5},{8,10},{9,11},{10,... | collective-permute-start | bytes 983048 | tf_op jit(solution)/shard_map/ppermute | solution.py:68
  458.1 23.5 %collective-permute-start.50 = (bf16[64,2560]{1,0:T(8,128)(2,1)S(1)}, bf16[64,2560]{1,0:T(8,128)(2,1)S(1)}, u32[]{:S(2)}, u32[]{:S(2)}) collective-permute-start(bf16[64,2560]{1,0:T(8,128)(2,1)S(1)} %add_near.18), channel_id=1, source_target_pairs={{0,8},{1,9},{2,10},{3,11},{4,12},{5,13},{6,14},{7,15},{8,0},{9,1},... | collective-permute-start | bytes 983048 | tf_op jit(solution)/shard_map/ppermute | solution.py:72
  465.1 25.5 %collective-permute-start.52 = (bf16[64,2560]{1,0:T(8,128)(2,1)S(1)}, bf16[64,2560]{1,0:T(8,128)(2,1)S(1)}, u32[]{:S(2)}, u32[]{:S(2)}) collective-permute-start(bf16[64,2560]{1,0:T(8,128)(2,1)S(1)} %add_near.19), channel_id=1, source_target_pairs={{0,12},{1,13},{2,14},{3,15},{4,0},{5,1},{6,2},{7,3},{8,4},{9,5},{1... | collective-permute-start | bytes 983048 | tf_op jit(solution)/shard_map/ppermute | solution.py:72
  472.1 18.5 %collective-permute-start.54 = (bf16[64,2560]{1,0:T(8,128)(2,1)S(1)}, bf16[64,2560]{1,0:T(8,128)(2,1)S(1)}, u32[]{:S(2)}, u32[]{:S(2)}) collective-permute-start(bf16[64,2560]{1,0:T(8,128)(2,1)S(1)} %add_near.20), channel_id=1, source_target_pairs={{0,4},{1,5},{2,6},{3,7},{4,8},{5,9},{6,10},{7,11},{8,12},{9,13},{1... | collective-permute-start | bytes 983048 | tf_op jit(solution)/shard_map/ppermute | solution.py:72
  493.1 16.7 %collective-permute-start.55 = (bf16[64,2560]{1,0:T(8,128)(2,1)S(1)}, bf16[64,2560]{1,0:T(8,128)(2,1)S(1)}, u32[]{:S(2)}, u32[]{:S(2)}) collective-permute-start(bf16[64,2560]{1,0:T(8,128)(2,1)S(1)} %get-tuple-element.178.refs_0_), channel_id=1, source_target_pairs={{0,4},{1,5},{2,6},{3,7},{4,8},{5,9},{6,10},{7,11},{8,12},{9,13},{1... | collective-permute-start | bytes 983048 | tf_op jit(solution)/shard_map/ppermute | solution.py:72
  494.5 27.8 %collective-permute-start.56 = (bf16[64,2560]{1,0:T(8,128)(2,1)S(1)}, bf16[64,2560]{1,0:T(8,128)(2,1)S(1)}, u32[]{:S(2)}, u32[]{:S(2)}) collective-permute-start(bf16[64,2560]{1,0:T(8,128)(2,1)S(1)} %get-tuple-element.178.refs_0_), channel_id=1, source_target_pairs={{0,8},{1,9},{2,10},{3,11},{4,12},{5,13},{6,14},{7,15},{8,0},{9,1},... | collective-permute-start | bytes 983048 | tf_op jit(solution)/shard_map/ppermute | solution.py:72
  501.8 20.5 %collective-permute-start.61 = (bf16[64,2560]{1,0:T(8,128)(2,1)S(1)}, bf16[64,2560]{1,0:T(8,128)(2,1)S(1)}, u32[]{:S(2)}, u32[]{:S(2)}) collective-permute-start(bf16[64,2560]{1,0:T(8,128)(2,1)S(1)} %collective-permute-done.57.refs_3_), channel_id=1, source_target_pairs={{0,2},{1,3},{2,0},{3,1},{4,6},{5,7},{6,4},{7,5},{8,10},{9,11},{10,... | collective-permute-start | bytes 983048 | tf_op jit(solution)/shard_map/ppermute | solution.py:68
  509.8 13.3 %collective-permute-start.60 = (bf16[64,2560]{1,0:T(8,128)(2,1)S(1)}, bf16[64,2560]{1,0:T(8,128)(2,1)S(1)}, u32[]{:S(2)}, u32[]{:S(2)}) collective-permute-start(bf16[64,2560]{1,0:T(8,128)(2,1)S(1)} %collective-permute-done.55.refs_1_), channel_id=1, source_target_pairs={{0,2},{1,3},{2,0},{3,1},{4,6},{5,7},{6,4},{7,5},{8,10},{9,11},{10,... | collective-permute-start | bytes 983048 | tf_op jit(solution)/shard_map/ppermute | solution.py:68
  532.5 83.5 %all-to-all-start.2 = ((bf16[16,160,640]{2,1,0:T(8,128)(2,1)}), bf16[16,160,640]{2,1,0:T(8,128)(2,1)S(1)}, u32[]{:S(2)}, u32[]{:S(2)}) async-start(bf16[16,160,640]{2,1,0:T(8,128)(2,1)} %bitcast.77), calls=%async_computation.3 | async-start | bytes 6553600 | tf_op jit(solution)/shard_map/all_to_all | solution.py:80
  543.3 123.5 %reduce-scatter.5.cloned.1.call-start = ((), (), s32[]{:S(2)}) async-start(), calls=%async_computation.7 | async-start | bytes 5898240 | tf_op jit(solution)/shard_map/reduce_scatter | solution.py:219
  579.2 13.8 %collective-permute-start.65 = (bf16[64,2560]{1,0:T(8,128)(2,1)}, bf16[64,2560]{1,0:T(8,128)(2,1)}, u32[]{:S(2)}, u32[]{:S(2)}) collective-permute-start(bf16[64,2560]{1,0:T(8,128)(2,1)} %get-tuple-element.191), channel_id=1, source_target_pairs={{0,2},{1,3},{2,0},{3,1},{4,6},{5,7},{6,4},{7,5},{8,10},{9,11},{10,... | collective-permute-start | bytes 983048 | tf_op jit(solution)/shard_map/ppermute | solution.py:68
  616.4 25.9 %collective-permute-start.67 = (bf16[64,2560]{1,0:T(8,128)(2,1)}, bf16[64,2560]{1,0:T(8,128)(2,1)S(1)}, u32[]{:S(2)}, u32[]{:S(2)}) collective-permute-start(bf16[64,2560]{1,0:T(8,128)(2,1)} %copy-done.131), channel_id=1, source_target_pairs={{0,2},{1,3},{2,0},{3,1},{4,6},{5,7},{6,4},{7,5},{8,10},{9,11},{10,... | collective-permute-start | bytes 983048 | tf_op jit(solution)/shard_map/ppermute | solution.py:68
  616.4 16.3 %collective-permute-start.69 = (bf16[64,2560]{1,0:T(8,128)(2,1)}, bf16[64,2560]{1,0:T(8,128)(2,1)S(1)}, u32[]{:S(2)}, u32[]{:S(2)}) collective-permute-start(bf16[64,2560]{1,0:T(8,128)(2,1)} %copy-done.133), channel_id=1, source_target_pairs={{0,2},{1,3},{2,0},{3,1},{4,6},{5,7},{6,4},{7,5},{8,10},{9,11},{10,... | collective-permute-start | bytes 983048 | tf_op jit(solution)/shard_map/ppermute | solution.py:68
  617.8 21.9 %collective-permute-start.71 = (bf16[64,2560]{1,0:T(8,128)(2,1)}, bf16[64,2560]{1,0:T(8,128)(2,1)S(1)}, u32[]{:S(2)}, u32[]{:S(2)}) collective-permute-start(bf16[64,2560]{1,0:T(8,128)(2,1)} %copy-done.132), channel_id=1, source_target_pairs={{0,2},{1,3},{2,0},{3,1},{4,6},{5,7},{6,4},{7,5},{8,10},{9,11},{10,... | collective-permute-start | bytes 983048 | tf_op jit(solution)/shard_map/ppermute | solution.py:68
  641.8 21.4 %collective-permute-start.68 = (bf16[64,2560]{1,0:T(8,128)(2,1)S(1)}, bf16[64,2560]{1,0:T(8,128)(2,1)S(1)}, u32[]{:S(2)}, u32[]{:S(2)}) collective-permute-start(bf16[64,2560]{1,0:T(8,128)(2,1)S(1)} %add_near.21), channel_id=1, source_target_pairs={{0,8},{1,9},{2,10},{3,11},{4,12},{5,13},{6,14},{7,15},{8,0},{9,1},... | collective-permute-start | bytes 983048 | tf_op jit(solution)/shard_map/ppermute | solution.py:72
  666.8 51.1 %all-to-all-start.3 = ((bf16[16,160,384]{2,1,0:T(8,128)(2,1)}), bf16[16,160,384]{2,1,0:T(8,128)(2,1)}, u32[]{:S(2)}, u32[]{:S(2)}) async-start(bf16[16,160,384]{2,1,0:T(8,128)(2,1)} %bitcast.78), calls=%async_computation.5 | async-start | bytes 3932160 | tf_op jit(solution)/shard_map/all_to_all | solution.py:80
  (179 other events, 1247.4 us)
Sparse Core Ops, SparseCore 0:
  75.8 53.8 all-gather.4
  195.3 82.8 all-gather.6
  441.6 80.4 reduce-scatter.2
  616.2 50.5 reduce-scatter.4

commit v4 on v3

--- a/solution.py
+++ b/solution.py
@@ -1,3 +1,4 @@
+import functools
 import functools
 import math
 
@@ -103,24 +104,25 @@
 
 
 def scatter_rows(part, *late):
-    far1, far0, near1, *near0 = part
+    far1, far0, near1, near0 = part
     shape = far1.shape[1:]
 
     def add_far(a_ref, b_ref, *outs):
         for m in range(4):
             outs[m][...] = (a_ref[m].astype(F32) + b_ref[m].astype(F32)).astype(BF)
 
-    def add_near(a_ref, b_ref, c_ref, out_ref):
-        out_ref[...] = (a_ref[...].astype(F32) + b_ref[...].astype(F32) + c_ref[...].astype(F32)).astype(BF)
+    def add_near(m, a_ref, b_ref, c_ref, out_ref):
+        out_ref[...] = (a_ref[m].astype(F32) + b_ref[m].astype(F32) + c_ref[...].astype(F32)).astype(BF)
 
     far = kernel_call(add_far, [whole(shape, BF)] * 4, (far0, move_c(far1)), limit=16, name="add_far")
     near1 = move_c(near1)
     come = {m: move_x(far[m]) for m in (2, 1, 3, 0)}
     if late:
         come[2] = after(come[2], *late)
-    terms = [near0[0], near1[0], come[0]]
+    terms = [near0, near1, come[0]]
     for m in (2, 1, 3):
-        s = kernel_call(add_near, whole(shape, BF), (near0[m], near1[m], come[m]), limit=8, name="add_near")
+        body = functools.partial(add_near, m)
+        s = kernel_call(body, whole(shape, BF), (near0, near1, come[m]), limit=8, name="add_near")
         terms.append(move_z(s, 4 - m))
     return terms, far, come
 
@@ -130,27 +132,21 @@
         whole((4, seg, width), BF),
         whole((4, seg, width), BF),
         whole((4, seg, width), BF),
-    ] + [whole((seg, width), BF)] * 4
+        whole((4, seg, width), BF),
+    ]
 
 
 def write_part(outs, group, value):
-    far1, far0, near1, *near0 = outs
+    far1, far0, near1, near0 = outs
     seg = far1.shape[1]
+    to = (near0, near1, far0, far1)[group]
     for m in range(4):
-        rows = value[m * seg : (m + 1) * seg]
-        if group == 3:
-            far1[m] = rows.astype(BF)
-        elif group == 2:
-            far0[m] = rows.astype(BF)
-        elif group == 1:
-            near1[m] = rows.astype(BF)
-        else:
-            near0[m][...] = rows.astype(BF)
+        to[m] = value[m * seg : (m + 1) * seg].astype(BF)
 
 
 def total(refs):
-    out = refs[0][...].astype(F32)
-    for r in refs[1:]:
+    out = refs[0][0].astype(F32) + refs[1][0].astype(F32)
+    for r in refs[2:]:
         out = out + r[...].astype(F32)
     return out
 
@@ -257,64 +253,37 @@
     return kernel_call(body, outs, (first, second), limit=16, name="unpack_first")
 
 
-def prepare_attention(place, mine, both):
-    size, d = mine.shape[1], HEAD_SIZE
-    depth = 16 * size
-
-    def body(place_ref, mine_ref, both_ref, w_ref, out_ref, row_ref, info_ref):
-        other_ref = both_ref.at[1 - place_ref[3]]
-        info_ref[...] = jnp.zeros_like(info_ref)
-        for k in range(16):
-            rs = slice(k * size, (k + 1) * size)
-            parts = [mine_ref[k], other_ref[k]]
-            w_ref[rs, :] = jnp.concatenate([p[:, : 3 * d] for p in parts], axis=1)
-            out_ref[rs, :] = jnp.concatenate([p[:, 3 * d : 4 * d] for p in parts], axis=1)
-            info_ref[rs, :EXTRA] = parts[0][:, 4 * d : 4 * d + EXTRA].astype(F32)
-        for b in range(depth // LANES):
-            rs = slice(b * LANES, (b + 1) * LANES)
-            row_ref[:, rs] = info_ref[rs, :].T[0:8, :]
-
-    return kernel_call(
-        body,
-        [whole((depth, 6 * d), BF), whole((depth, 2 * d), BF), whole((8, depth), F32)],
-        (place, mine, both),
-        scalars=1,
-        scratch=[pltpu.VMEM((depth, LANES), F32)],
-        limit=16,
-        name="prepare_attention",
-    )
-
-
-def prepare_feed(place, first_mine, first_both, mine, both, hidden):
-    size = mine.shape[1]
-    depth = 16 * size
+def order_attention(mine_ref, other_ref, w_ref, out_ref, row_ref, info_ref):
+    size, d = mine_ref.shape[1], HEAD_SIZE
+    info_ref[...] = jnp.zeros_like(info_ref)
+    for k in range(16):
+        rs = slice(k * size, (k + 1) * size)
+        parts = [mine_ref[k], other_ref[k]]
+        w_ref[rs, :] = jnp.concatenate([p[:, : 3 * d] for p in parts], axis=1)
+        out_ref[rs, :] = jnp.concatenate([p[:, 3 * d : 4 * d] for p in parts], axis=1)
+        info_ref[rs, :EXTRA] = parts[0][:, 4 * d : 4 * d + EXTRA].astype(F32)
+    for b in range(16 * size // LANES):
+        rs = slice(b * LANES, (b + 1) * LANES)
+        row_ref[:, rs] = info_ref[rs, :].T[0:8, :]
+
+
+def order_feed(fm_ref, fo_ref, m_ref, o_ref, gu_ref, d_ref, hidden):
+    size = m_ref.shape[1]
     at = 4 * HEAD_SIZE + EXTRA
     rest = hidden - (FIRST - at)
-
-    def body(place_ref, fm_ref, fboth_ref, m_ref, both_ref, gu_ref, d_ref):
-        fo_ref, o_ref = fboth_ref.at[1 - place_ref[3]], both_ref.at[1 - place_ref[3]]
-        for k in range(16):
-            rs = slice(k * size, (k + 1) * size)
-            fm, fo, m, o = fm_ref[k], fo_ref[k], m_ref[k], o_ref[k]
-            gu_ref[rs, :] = jnp.concatenate(
-                [
-                    m[:, rest : rest + hidden],
-                    o[:, rest : rest + hidden],
-                    m[:, rest + hidden : rest + 2 * hidden],
-                    o[:, rest + hidden : rest + 2 * hidden],
-                ],
-                axis=1,
-            )
-            d_ref[rs, :] = jnp.concatenate([fm[:, at:], m[:, :rest], fo[:, at:], o[:, :rest]], axis=1)
-
-    return kernel_call(
-        body,
-        [whole((depth, 4 * hidden), BF), whole((depth, 2 * hidden), BF)],
-        (place, first_mine, first_both, mine, both),
-        scalars=1,
-        limit=16,
-        name="prepare_feed",
-    )
+    for k in range(16):
+        rs = slice(k * size, (k + 1) * size)
+        fm, fo, m, o = fm_ref[k], fo_ref[k], m_ref[k], o_ref[k]
+        gu_ref[rs, :] = jnp.concatenate(
+            [
+                m[:, rest : rest + hidden],
+                o[:, rest : rest + hidden],
+                m[:, rest + hidden : rest + 2 * hidden],
+                o[:, rest + hidden : rest + 2 * hidden],
+            ],
+            axis=1,
+        )
+        d_ref[rs, :] = jnp.concatenate([fm[:, at:], m[:, :rest], fo[:, at:], o[:, :rest]], axis=1)
 
 
 def turn(a, cosine, sine):
@@ -329,7 +298,7 @@
     return jnp.concatenate([part, jnp.zeros((value.shape[0], LANES - HEAD_SIZE), value.dtype)], axis=1)
 
 
-def attention(place, pieces, weights, w_o, rows_info, length, kpos, cosine, sine):
+def attention(place, pieces, mine, both, kpos, cosine, sine):
     seg, width = pieces[0].shape[1:]
     rows = 16 * seg
     blocks = rows // BLOCK
@@ -337,11 +306,17 @@
 
     def body(place_ref, *refs):
         x_refs = [refs[i // 4].at[i % 4] for i in range(16)]
-        w_ref, wo_ref, info_ref, len_ref, kpos_ref, cos_ref, sin_ref = refs[4:11]
-        h_ref, q_ref, k_ref, v_ref, ctx_ref, lse_ref, *part = refs[11:]
+        mine_ref, both_ref, kpos_ref, cos_ref, sin_ref = refs[4:9]
+        h_ref, q_ref, k_ref, v_ref, ctx_ref, lse_ref, w_ref, wo_ref, row_ref, *part = refs[9:22]
+        other_ref, info_ref, sem = refs[22:]
+        other = pltpu.make_async_copy(both_ref.at[1 - place_ref[3]], other_ref, sem)
+        other.start()
+        other.wait()
+        order_attention(mine_ref, other_ref, w_ref, wo_ref, row_ref, info_ref)
         z = place_ref[0]
-        gain = info_ref[0:1, :]
-        length = len_ref[0:1, 0:1]
+        gain = row_ref[0:1, :]
+        counts = jnp.where(place_ref[3] == 0, row_ref[2:3, :], row_ref[3:4, :])
+        length = jnp.sum(counts, axis=1, keepdims=True) / F32(width // 16)
         for i in range(16):
 
             @pl.loop(0, seg // 16)
@@ -387,17 +362,23 @@
         whole((2, rows, LANES), BF),
         whole((rows, 2 * HEAD_SIZE), BF),
         whole((2, rows, 1), F32),
+        whole((width, 6 * HEAD_SIZE), BF),
+        whole((width, 2 * HEAD_SIZE), BF),
+        whole((8, width), F32),
     ] + part_shapes(seg, width)
     flops = 2 * rows * width * 6 * LANES + 2 * rows * rows * LANES * 2 * 2
     out = kernel_call(
         body,
         outs,
-        (place, *pieces, weights, w_o, rows_info, length, kpos, cosine, sine),
+        (place, *pieces, mine, both, kpos, cosine, sine),
         scalars=1,
+        far=(6,),
+        scratch=[pltpu.VMEM(mine.shape, BF), pltpu.VMEM((width, LANES), F32), pltpu.SemaphoreType.DMA],
+        limit=24,
         flops=flops,
         name="attention",
     )
-    return out[:6], out[6:]
+    return out[:9], out[9:]
 
 
 def attention_back(place, pieces, weights, w_o, length, kpos, cosine, sine, q, k, v, lse):
@@ -409,8 +390,8 @@
     def body(place_ref, *refs):
         d_refs = [refs[i // 4].at[i % 4] for i in range(16)]
         w_ref, wo_ref, len_ref, kpos_ref, cos_ref, sin_ref, q_ref, k_ref, v_ref, lse_ref = refs[4:14]
-        da_ref, dqkv_ref, *part = refs[14:23]
-        dctx_ref, dk_ref, dv_ref = refs[23:]
+        da_ref, dqkv_ref, *part = refs[14:20]
+        dctx_ref, dk_ref, dv_ref = refs[20:]
         z = place_ref[0]
         length = len_ref[0:1, 0:1]
         for i in range(16):
@@ -509,36 +490,51 @@
     )
 
 
-def feed(pieces, w_gu, w_d):
+def feed(place, pieces, first_mine, first_both, mine, both, hidden):
     seg, width = pieces[0].shape[1:]
     rows = 16 * seg
-    hidden = w_d.shape[1]
-
-    def body(*refs):
+    columns = 2 * hidden
+
+    def body(place_ref, *refs):
         h_refs = [refs[i // 4].at[i % 4] for i in range(16)]
-        wg_ref, wd_ref, h_ref, gate_ref, act_ref, *part = refs[4:]
+        fm_ref, fboth_ref, m_ref, both_ref, h_ref, gate_ref, act_ref, wg_ref, wd_ref, *part = refs[4:17]
+        fo_ref, o_ref, sem = refs[17:]
+        first = pltpu.make_async_copy(fboth_ref.at[1 - place_ref[3]], fo_ref, sem.at[0])
+        second = pltpu.make_async_copy(both_ref.at[1 - place_ref[3]], o_ref, sem.at[1])
+        first.start()
+        second.start()
         for i in range(16):
             h_ref[i * seg : (i + 1) * seg, :] = h_refs[i][...]
+        first.wait()
+        second.wait()
+        order_feed(fm_ref, fo_ref, m_ref, o_ref, wg_ref, wd_ref, hidden)
         for g in range(4):
             rs = slice(g * 4 * seg, (g + 1) * 4 * seg)
-            both = dot_nn(h_ref[rs, :], wg_ref[...])
-            gate_ref[rs, :] = both
-            gate, up = both[:, :hidden], both[:, hidden:]
+            gu = dot_nn(h_ref[rs, :], wg_ref[...])
+            gate_ref[rs, :] = gu
+            gate, up = gu[:, :columns], gu[:, columns:]
             act_ref[rs, :] = (gate * jax.nn.sigmoid(gate) * up).astype(BF)
         for g in (3, 2, 1, 0):
             rs = slice(g * 4 * seg, (g + 1) * 4 * seg)
             write_part(part, g, dot_nt(act_ref[rs, :], wd_ref[...]))
 
-    outs = [whole((rows, width), BF), whole((rows, 2 * hidden), F32), whole((rows, hidden), BF)]
+    outs = [whole((rows, width), BF), whole((rows, 2 * columns), F32), whole((rows, columns), BF)]
+    outs += [whole((width, 2 * columns), BF), whole((width, columns), BF)]
     out = kernel_call(
         body,
         outs + part_shapes(seg, width),
-        (*pieces, w_gu, w_d),
-        flops=2 * rows * width * hidden * 3,
-        limit=16,
+        (place, *pieces, first_mine, first_both, mine, both),
+        scalars=1,
+        far=(6, 8),
+        scratch=[
+            pltpu.VMEM(first_mine.shape, BF),
+            pltpu.VMEM(mine.shape, BF),
+            pltpu.SemaphoreType.DMA((2,)),
+        ],
+        limit=26,
         name="feed",
     )
-    return out[:3], out[3:]
+    return out[:5], out[5:]
 
 
 def feed_back(pieces, w_gu, w_d, gate_up):
@@ -751,21 +747,20 @@
     first_both = of_other(first_in)
     pieces, near, far = gather_rows(after(own, first_in), first_both)
     second_in = share_blocks(after(seconds, *near, *far))
-    w_qkv, w_o, info = prepare_attention(place, first_in, first_both)
+    (h1, q, keys, values, ctx, lse, w_qkv, w_o, info), part = attention(
+        place, pieces, first_in, first_both, kpos, cosine, sine
+    )
     lengths = jnp.sum(info[2:4], axis=1) / F32(width // 16)
     count = lengths[0] + lengths[1]
     length = jnp.full((8, LANES), jnp.where(first, lengths[0], lengths[1]), F32)
     factor = jnp.full((8, LANES), F32(seqs * seq_len) / count, F32)
-
-    (h1, q, keys, values, ctx, lse), part = attention(
-        place, pieces, w_qkv, w_o, info, length, kpos, cosine, sine
-    )
     terms, far, come = scatter_rows(part)
     second_both = of_other(after(second_in, come[2]))
     resid, h2_own = rows_after_attention(terms, own, info)
-    w_gu, w_d = prepare_feed(place, first_in, first_both, second_in, second_both, hidden)
-    pieces, _, _ = gather_rows(h2_own, w_gu)
-    (h2, gate_up, act), part = feed(pieces, w_gu, w_d)
+    pieces, _, _ = gather_rows(h2_own)
+    (h2, gate_up, act, w_gu, w_d), part = feed(
+        place, pieces, first_in, first_both, second_in, second_both, hidden
+    )
     okf = mine(valid).astype(F32)[:, None]
     terms, _, _ = scatter_rows(part)
     out_own, dout, dm_own, squares = rows_after_feed(

time: 743 us -> 735 us (0.989)
  waiting for transfers between devices: 398 us -> 377 us
  Pallas kernels: 103 us -> 112 us
    ppermute x32, waiting for transfers between devices: 117 us -> 106 us  [move_x(): return lax.ppermute(a, 'context', [(k, k ^ 2) for k in range(16)])]
    pallas_call x41 -> x39, Pallas kernels: 103 us -> 112 us  [kernel_call(): pl.pallas_call(body, out_shape=outs, in_specs=[spec(i) for i in range(len...]
    all_to_all x4, waiting for transfers between devices: 99.3 us -> 90.3 us  [share_out(): return lax.all_to_all(a, 'context', split_axis=0, concat_axis=0, tiled=True)]
    all_gather x2, waiting for transfers between devices: 9.58 us -> 0.99 us  [of_other(): return lax.all_gather(a, 'tensor', axis=0, tiled=False)]
    reduce_scatter x2, waiting for transfers between devices: 2.24 us -> 10.7 us  [over_sequences(): return lax.psum_scatter(parts, 'tensor', scatter_dimension=0, tiled=False)]
    unnamed x290 -> x246, local copies, waits for them, and re-layouts: 82.6 us -> 83.7 us
  transfers between devices with their start and end apart: 82 -> 82, of which waited for: 55 -> 56; matrix products, arithmetic and copies ran while one was open for 1% -> 1% of each run, Pallas kernels for 9% -> 9%
where the time goes in v4:
time: 735 us; the launch traced here: 728 us
  waiting for transfers between devices  377 us (51%)
  starting transfers between devices  121 us (16%)
  Pallas kernels  112 us (15%)
  local copies, waits for them, and re-layouts  89.8 us (12%)
  between operations  19.2 us (3%)
  other arithmetic  8.96 us (1%)
    ppermute x24, waiting for transfers between devices, move_z(): lax.ppermute(a, 'context', [(k, (k + 4 * step) % 16) for k in range(16)])  135 us
    pallas_call x39, Pallas kernels, kernel_call(): pl.pallas_call(body, out_shape=outs, in_specs=[spec(i) for i in range(len...  112 us
    ppermute x32, waiting for transfers between devices, move_x(): return lax.ppermute(a, 'context', [(k, k ^ 2) for k in range(16)])  106 us
    all_to_all x4, waiting for transfers between devices, share_out(): return lax.all_to_all(a, 'context', split_axis=0, concat_axis=0, tiled=True)  90.3 us
    unnamed x246, local copies, waits for them, and re-layouts  83.7 us
    ppermute x24, starting transfers between devices, move_z(): lax.ppermute(a, 'context', [(k, (k + 4 * step) % 16) for k in range(16)])  40.3 us
    all_to_all x4, starting transfers between devices, share_out(): return lax.all_to_all(a, 'context', split_axis=0, concat_axis=0, tiled=True)  36.7 us
    ppermute x16, starting transfers between devices, move_c(): return lax.ppermute(a, 'context', [(k, k ^ 1) for k in range(16)])  21.2 us
  transfers between devices with their start and end apart: 82, of which 56 were waited for; matrix products, arithmetic and copies ran while one was open for 1% of the time, Pallas kernels for 9%

profile of v4, /device:TPU:11, one launch (start us, length us, event | category | flops | bytes accessed | tf_op | source)
XLA Modules:
  0.0 728.2 jit_solution(2724065927569012533)
XLA Ops:
  19.3 6.6 all-to-all-start
  26.0 44.4 %all-to-all-done.refs_4_ = bf16[16,160,384]{2,1,0:T(8,128)(2,1)S(1)} async-done(((bf16[16,160,384]{2,1,0:T(8,128)(2,1)}), bf16[16,160,384]{2,1,0:T(8,128)(2,1)S(1)}, u32[]{:S(2)}, u32[]{:S(2)}) %all-to-all-start) | async-done | bytes 1966112 | tf_op jit(solution)/shard_map/all_to_all | solution.py:81
  73.2 6.4 collective-permute-done.4.refs_0_
  80.7 6.3 collective-permute-done.2.refs_3_
  89.0 9.6 %collective-permute-done.1.refs_2_ = bf16[64,2560]{1,0:T(8,128)(2,1)} collective-permute-done((bf16[64,2560]{1,0:T(8,128)(2,1)S(1)}, bf16[64,2560]{1,0:T(8,128)(2,1)}, u32[]{:S(2)}, u32[]{:S(2)}) %collective-permute-start.1) | collective-permute-done | bytes 327712 | tf_op jit(solution)/shard_map/ppermute | solution.py:73
  109.5 14.0 %all-to-all-start.1 = ((bf16[16,160,640]{2,1,0:T(8,128)(2,1)}), bf16[16,160,640]{2,1,0:T(8,128)(2,1)}, u32[]{:S(2)}, u32[]{:S(2)}) async-start(bf16[16,160,640]{2,1,0:T(8,128)(2,1)} %pack_second.1), calls=%async_computation.1 | async-start | bytes 6553600 | tf_op jit(solution)/shard_map/all_to_all | solution.py:81
  137.2 20.9 %attention.1 = (bf16[1024,2560]{1,0:T(8,128)(2,1)S(1)}, bf16[2,1024,128]{2,1,0:T(8,128)(2,1)S(1)}, bf16[2,1024,128]{2,1,0:T(8,128)(2,1)S(1)}, bf16[2,1024,128]{2...) custom-call(s32[4]{0:T(128)S(1)} %pad_add_fusion.place_ref, ...), custom_call_target="tpu_custom_call" | custom-call | tf_op jit(solution)/shard_map/attention/pallas_call | solution.py:40
  172.7 13.2 %collective-permute-done.12.c_ref = bf16[64,2560]{1,0:T(8,128)(2,1)S(1)} collective-permute-done((bf16[64,2560]{1,0:T(8,128)(2,1)S(1)}, bf16[64,2560]{1,0:T(8,128)(2,1)S(1)}, u32[]{:S(2)}, u32[]{:S(2)}) %collective-permute-start.12) | collective-permute-done | bytes 327712 | tf_op jit(solution)/shard_map/ppermute | solution.py:69
  186.5 9.7 %all-to-all-done.1.refs_6_ = bf16[16,160,640]{2,1,0:T(8,128)(2,1)} async-done(((bf16[16,160,640]{2,1,0:T(8,128)(2,1)}), bf16[16,160,640]{2,1,0:T(8,128)(2,1)}, u32[]{:S(2)}, u32[]{:S(2)}) %all-to-all-start.1) | async-done | bytes 3276832 | tf_op jit(solution)/shard_map/all_to_all | solution.py:81
  199.7 6.1 collective-permute-done.16.c_ref
  206.9 6.0 collective-permute-done.14.c_ref
  221.0 16.1 %collective-permute-done.13.refs_3_ = bf16[64,2560]{1,0:T(8,128)(2,1)S(1)} collective-permute-done((bf16[64,2560]{1,0:T(8,128)(2,1)S(1)}, bf16[64,2560]{1,0:T(8,128)(2,1)S(1)}, u32[]{:S(2)}, u32[]{:S(2)}) %collective-permute-start.13) | collective-permute-done | bytes 327712 | tf_op jit(solution)/shard_map/ppermute | solution.py:73
  239.4 4.9 collective-permute-start.19
  246.8 9.6 %collective-permute-done.18.refs_1_ = bf16[64,2560]{1,0:T(8,128)(2,1)S(1)} collective-permute-done((bf16[64,2560]{1,0:T(8,128)(2,1)S(1)}, bf16[64,2560]{1,0:T(8,128)(2,1)S(1)}, u32[]{:S(2)}, u32[]{:S(2)}) %collective-permute-start.18) | collective-permute-done | bytes 327712 | tf_op jit(solution)/shard_map/ppermute | solution.py:73
  256.7 9.7 %collective-permute-done.19.refs_2_ = bf16[64,2560]{1,0:T(8,128)(2,1)S(1)} collective-permute-done((bf16[64,2560]{1,0:T(8,128)(2,1)S(1)}, bf16[64,2560]{1,0:T(8,128)(2,1)S(1)}, u32[]{:S(2)}, u32[]{:S(2)}) %collective-permute-start.19) | collective-permute-done | bytes 327712 | tf_op jit(solution)/shard_map/ppermute | solution.py:73
  287.8 17.7 %feed.1 = (bf16[1024,2560]{1,0:T(8,128)(2,1)}, f32[1024,864]{1,0:T(8,128)S(1)}, bf16[1024,432]{1,0:T(8,128)(2,1)S(1)}, bf16[2560,864]{1,0:T(8,128)(2,1)}, bf16[2...) custom-call(s32[4]{0:T(128)S(1)} %pad_add_fusion.place_ref, ...), custom_call_target="tpu_custom_call" | custom-call | tf_op jit(solution)/shard_map/feed/pallas_call | solution.py:40
  322.3 4.9 collective-permute-done.34.c_ref
  328.0 6.0 collective-permute-start.35
  348.4 13.0 %collective-permute-done.31.refs_3_ = bf16[64,2560]{1,0:T(8,128)(2,1)} collective-permute-done((bf16[64,2560]{1,0:T(8,128)(2,1)}, bf16[64,2560]{1,0:T(8,128)(2,1)}, u32[]{:S(2)}, u32[]{:S(2)}) %collective-permute-start.31) | collective-permute-done | bytes 327712 | tf_op jit(solution)/shard_map/ppermute | solution.py:73
  373.2 9.2 %collective-permute-done.39.refs_3_ = bf16[64,2560]{1,0:T(8,128)(2,1)S(1)} collective-permute-done((bf16[64,2560]{1,0:T(8,128)(2,1)S(1)}, bf16[64,2560]{1,0:T(8,128)(2,1)S(1)}, u32[]{:S(2)}, u32[]{:S(2)}) %collective-permute-start.39) | collective-permute-done | bytes 327712 | tf_op jit(solution)/shard_map/ppermute | solution.py:73
  386.0 12.2 %collective-permute-done.38.refs_2_ = bf16[64,2560]{1,0:T(8,128)(2,1)S(1)} collective-permute-done((bf16[64,2560]{1,0:T(8,128)(2,1)S(1)}, bf16[64,2560]{1,0:T(8,128)(2,1)S(1)}, u32[]{:S(2)}, u32[]{:S(2)}) %collective-permute-start.38) | collective-permute-done | bytes 327712 | tf_op jit(solution)/shard_map/ppermute | solution.py:73
  398.9 6.9 collective-permute-start.40
  405.9 4.9 collective-permute-start.45
  415.8 8.9 %feed_back.1 = (bf16[1024,2560]{1,0:T(8,128)(2,1)S(1)}, bf16[1024,864]{1,0:T(8,128)(2,1)S(1)}, bf16[4,64,2560]{2,1,0:T(8,128)(2,1)S(1)}, bf16[4,64,2560]{2,1,0:T...) custom-call(bf16[4,64,2560]{2,1,0:T(8,128)(2,1)S(1)} %stack.76.refs_0_, ...), custom_call_target="tpu_custom_call" | custom-call | tf_op jit(solution)/shard_map/feed_back/pallas_call | solution.py:40
  429.3 9.1 %feed_grads.1 = (bf16[2,16,160,640]{3,2,1,0:T(8,128)(2,1)S(1)}, bf16[2560,16]{1,0:T(8,128)(2,1)S(1)}, f32[2560,1]{1,0:T(8,128)S(1)}) custom-call(s32[4]{0:T(128)S(1)} %pad_add_fusion.place_ref, bf16[2560,432]{1,0:T(8,128)(2,1)S(1)} %down_grads.1.down_ref, bf16[1024,2560]{1,0:T(8,128)(2,1)S(1)} %bitcast.38, bf16[1024,864]{1,0:T(8,128)(2,1)S(1)} %get-tuple-element.178.dgu_ref, ...), custom_call_target="tpu_custom_call" | custom-call | tf_op jit(solution)/shard_map/feed_grads/pallas_call | solution.py:40
  446.5 6.4 collective-permute-done.53.c_ref
  453.0 6.8 collective-permute-done.51.c_ref
  460.1 6.8 collective-permute-done.49.c_ref
  467.3 6.6 collective-permute-done.48.refs_2_
  473.9 8.8 %collective-permute-done.50.refs_3_ = bf16[64,2560]{1,0:T(8,128)(2,1)S(1)} collective-permute-done((bf16[64,2560]{1,0:T(8,128)(2,1)S(1)}, bf16[64,2560]{1,0:T(8,128)(2,1)S(1)}, u32[]{:S(2)}, u32[]{:S(2)}) %collective-permute-start.50) | collective-permute-done | bytes 327712 | tf_op jit(solution)/shard_map/ppermute | solution.py:73
  486.8 4.9 collective-permute-start.56
  495.7 7.3 collective-permute-done.55.refs_1_
  504.8 9.0 %collective-permute-done.56.refs_2_ = bf16[64,2560]{1,0:T(8,128)(2,1)S(1)} collective-permute-done((bf16[64,2560]{1,0:T(8,128)(2,1)S(1)}, bf16[64,2560]{1,0:T(8,128)(2,1)S(1)}, u32[]{:S(2)}, u32[]{:S(2)}) %collective-permute-start.56) | collective-permute-done | bytes 327712 | tf_op jit(solution)/shard_map/ppermute | solution.py:73
  516.0 6.5 collective-permute-done.62.refs_2_
  523.4 9.9 %all-to-all-start.2 = ((bf16[16,160,640]{2,1,0:T(8,128)(2,1)}), bf16[16,160,640]{2,1,0:T(8,128)(2,1)S(1)}, u32[]{:S(2)}, u32[]{:S(2)}) async-start(bf16[16,160,640]{2,1,0:T(8,128)(2,1)} %bitcast.43), calls=%async_computation.3 | async-start | bytes 6553600 | tf_op jit(solution)/shard_map/all_to_all | solution.py:81
  553.6 13.8 %attention_back.1 = (bf16[1024,2560]{1,0:T(8,128)(2,1)S(1)}, bf16[1024,480]{1,0:T(8,128)(2,1)S(1)}, bf16[4,64,2560]{2,1,0:T(8,128)(2,1)S(1)}, bf16[4,64,2560]{2,...) custom-call(s32[4]{0:T(128)S(1)} %pad_add_fusion.place_ref, ...), custom_call_target="tpu_custom_call" | custom-call | tf_op jit(solution)/shard_map/attention_back/pallas_call | solution.py:40
  576.5 7.3 %attention_grads.1 = bf16[2,16,160,384]{3,2,1,0:T(8,128)(2,1)S(1)} custom-call(s32[4]{0:T(128)S(1)} %pad_add_fusion.place_ref, bf16[1024,2560]{1,0:T(8,128)(2,1)S(1)} %copy-done.26, bf16[1024,480]{1,0:T(8,128)(2,1)S(1)} %get-tuple-element.170.dqkv_ref, bf16[1024,2560]{1,0:T(8,128)(2,1)S(1)} %get-tuple-element.171.da_ref, bf16[1024,160]{1,0:T(8,128)(2,1)S(1)} %copy-done.68, ...), custom_call_target="tpu_custom_call" | custom-call | tf_op jit(solution)/shard_map/attention_grads/pallas_call | solution.py:40
  585.7 6.2 collective-permute-done.65.c_ref
  591.9 14.1 %all-to-all-done.2.s_ref = bf16[16,160,640]{2,1,0:T(8,128)(2,1)S(1)} async-done(((bf16[16,160,640]{2,1,0:T(8,128)(2,1)}), bf16[16,160,640]{2,1,0:T(8,128)(2,1)S(1)}, u32[]{:S(2)}, u32[]{:S(2)}) %all-to-all-start.2) | async-done | bytes 3276832 | tf_op jit(solution)/shard_map/all_to_all | solution.py:81
  609.4 6.3 collective-permute-done.71.c_ref
  617.9 4.8 collective-permute-done.69.c_ref
  632.7 14.1 %collective-permute-done.68.refs_3_ = bf16[64,2560]{1,0:T(8,128)(2,1)S(1)} collective-permute-done((bf16[64,2560]{1,0:T(8,128)(2,1)S(1)}, bf16[64,2560]{1,0:T(8,128)(2,1)S(1)}, u32[]{:S(2)}, u32[]{:S(2)}) %collective-permute-start.68) | collective-permute-done | bytes 327712 | tf_op jit(solution)/shard_map/ppermute | solution.py:73
  648.2 10.5 %reduce-scatter.5.cloned.1.call-done = bf16[1,16,160,384]{3,2,1,0:T(8,128)(2,1)} async-done(((bf16[2,16,160,384]{3,2,1,0:T(8,128)(2,1)}), bf16[1,16,160,384]{3,2,1,0:T(8,128)(2,1)}) %reduce-scatter.5.cloned.1.call-update) | async-done | bytes 1966096 | tf_op jit(solution)/shard_map/reduce_scatter | solution.py:215
  658.7 6.3 all-to-all-start.3
  665.3 9.0 %collective-permute-done.36 = bf16[64,2560]{1,0:T(8,128)(2,1)} collective-permute-done((bf16[64,2560]{1,0:T(8,128)(2,1)}, bf16[64,2560]{1,0:T(8,128)(2,1)}, u32[]{:S(2)}, u32[]{:S(2)}) %collective-permute-start.36) | collective-permute-done | bytes 327712 | tf_op jit(solution)/shard_map/ppermute | solution.py:77
  676.7 6.9 collective-permute-done.73
  687.7 22.0 %all-to-all-done.3.f_ref = bf16[16,160,384]{2,1,0:T(8,128)(2,1)} async-done(((bf16[16,160,384]{2,1,0:T(8,128)(2,1)}), bf16[16,160,384]{2,1,0:T(8,128)(2,1)}, u32[]{:S(2)}, u32[]{:S(2)}) %all-to-all-start.3) | async-done | bytes 1966112 | tf_op jit(solution)/shard_map/all_to_all | solution.py:81
  711.7 6.1 unpack_first.1
  (446 shorter events, 232.3 us)
Async XLA Ops:
  19.3 51.2 %all-to-all-start = ((bf16[16,160,384]{2,1,0:T(8,128)(2,1)}), bf16[16,160,384]{2,1,0:T(8,128)(2,1)S(1)}, u32[]{:S(2)}, u32[]{:S(2)}) async-start(bf16[16,160,384]{2,1,0:T(8,128)(2,1)} %copy-done.16), calls=%async_computation | async-start | bytes 3932160 | tf_op jit(solution)/shard_map/all_to_all | solution.py:81
  25.8 102.3 %all-gather.5.cloned.1.call-start = ((), (), s32[]{:S(2)}) async-start(), calls=%async_computation.8 | async-start | bytes 5898240 | tf_op jit(solution)/shard_map/all_gather | solution.py:211
  71.6 15.4 %collective-permute-start.2 = (bf16[64,2560]{1,0:T(8,128)(2,1)S(1)}, bf16[64,2560]{1,0:T(8,128)(2,1)S(1)}, u32[]{:S(2)}, u32[]{:S(2)}) collective-permute-start(bf16[64,2560]{1,0:T(8,128)(2,1)S(1)} %dynamic-slice_bitcast_fusion.2.refs_0_.refs_6_), channel_id=1, source_target_pairs={{0,12},{1,13},{2,14},{3,15},{4,0},{5,1},{6,2},{7,3},{8,4},{9,5},{1... | collective-permute-start | bytes 983048 | tf_op jit(solution)/shard_map/ppermute | solution.py:73
  72.0 26.6 %collective-permute-start.1 = (bf16[64,2560]{1,0:T(8,128)(2,1)S(1)}, bf16[64,2560]{1,0:T(8,128)(2,1)}, u32[]{:S(2)}, u32[]{:S(2)}) collective-permute-start(bf16[64,2560]{1,0:T(8,128)(2,1)S(1)} %dynamic-slice_bitcast_fusion.2.refs_0_.refs_6_), channel_id=1, source_target_pairs={{0,8},{1,9},{2,10},{3,11},{4,12},{5,13},{6,14},{7,15},{8,0},{9,1},... | collective-permute-start | bytes 983048 | tf_op jit(solution)/shard_map/ppermute | solution.py:73
  79.6 19.0 %collective-permute-start.5 = (bf16[64,2560]{1,0:T(8,128)(2,1)S(1)}, bf16[64,2560]{1,0:T(8,128)(2,1)S(1)}, u32[]{:S(2)}, u32[]{:S(2)}) collective-permute-start(bf16[64,2560]{1,0:T(8,128)(2,1)S(1)} %collective-permute-done.refs_1_), channel_id=1, source_target_pairs={{0,2},{1,3},{2,0},{3,1},{4,6},{5,7},{6,4},{7,5},{8,10},{9,11},{10,... | collective-permute-start | bytes 983048 | tf_op jit(solution)/shard_map/ppermute | solution.py:69
  87.0 11.5 %collective-permute-start.6 = (bf16[64,2560]{1,0:T(8,128)(2,1)S(1)}, bf16[64,2560]{1,0:T(8,128)(2,1)S(1)}, u32[]{:S(2)}, u32[]{:S(2)}) collective-permute-start(bf16[64,2560]{1,0:T(8,128)(2,1)S(1)} %collective-permute-done.2.refs_3_), channel_id=1, source_target_pairs={{0,2},{1,3},{2,0},{3,1},{4,6},{5,7},{6,4},{7,5},{8,10},{9,11},{10,... | collective-permute-start | bytes 983048 | tf_op jit(solution)/shard_map/ppermute | solution.py:69
  109.5 86.8 %all-to-all-start.1 = ((bf16[16,160,640]{2,1,0:T(8,128)(2,1)}), bf16[16,160,640]{2,1,0:T(8,128)(2,1)}, u32[]{:S(2)}, u32[]{:S(2)}) async-start(bf16[16,160,640]{2,1,0:T(8,128)(2,1)} %pack_second.1), calls=%async_computation.1 | async-start | bytes 6553600 | tf_op jit(solution)/shard_map/all_to_all | solution.py:81
  123.4 157.0 %all-gather.7.cloned.1.call-start = ((), (), s32[]{:S(2)}) async-start(), calls=%async_computation.9 | async-start | bytes 9830400 | tf_op jit(solution)/shard_map/all_gather | solution.py:211
  172.4 13.4 %collective-permute-start.12 = (bf16[64,2560]{1,0:T(8,128)(2,1)S(1)}, bf16[64,2560]{1,0:T(8,128)(2,1)S(1)}, u32[]{:S(2)}, u32[]{:S(2)}) collective-permute-start(bf16[64,2560]{1,0:T(8,128)(2,1)S(1)} %get-tuple-element.115), channel_id=1, source_target_pairs={{0,2},{1,3},{2,0},{3,1},{4,6},{5,7},{6,4},{7,5},{8,10},{9,11},{10,... | collective-permute-start | bytes 983048 | tf_op jit(solution)/shard_map/ppermute | solution.py:69
  196.3 327.1 %reduce-scatter.3.cloned.1.call-start = ((), (), s32[]{:S(2)}) async-start(), calls=%async_computation.6 | async-start | bytes 9830400 | tf_op jit(solution)/shard_map/reduce_scatter | solution.py:215
  196.6 16.3 %collective-permute-start.14 = (bf16[64,2560]{1,0:T(8,128)(2,1)}, bf16[64,2560]{1,0:T(8,128)(2,1)S(1)}, u32[]{:S(2)}, u32[]{:S(2)}) collective-permute-start(bf16[64,2560]{1,0:T(8,128)(2,1)} %copy-done.112), channel_id=1, source_target_pairs={{0,2},{1,3},{2,0},{3,1},{4,6},{5,7},{6,4},{7,5},{8,10},{9,11},{10,... | collective-permute-start | bytes 983048 | tf_op jit(solution)/shard_map/ppermute | solution.py:69
  198.1 21.9 %collective-permute-start.11 = (bf16[64,2560]{1,0:T(8,128)(2,1)}, bf16[64,2560]{1,0:T(8,128)(2,1)S(1)}, u32[]{:S(2)}, u32[]{:S(2)}) collective-permute-start(bf16[64,2560]{1,0:T(8,128)(2,1)} %copy-done.109), channel_id=1, source_target_pairs={{0,2},{1,3},{2,0},{3,1},{4,6},{5,7},{6,4},{7,5},{8,10},{9,11},{10,... | collective-permute-start | bytes 983048 | tf_op jit(solution)/shard_map/ppermute | solution.py:69
  205.9 14.0 %collective-permute-start.17 = (bf16[64,2560]{1,0:T(8,128)(2,1)S(1)}, bf16[64,2560]{1,0:T(8,128)(2,1)S(1)}, u32[]{:S(2)}, u32[]{:S(2)}) collective-permute-start(bf16[64,2560]{1,0:T(8,128)(2,1)S(1)} %add_near.14), channel_id=1, source_target_pairs={{0,4},{1,5},{2,6},{3,7},{4,8},{5,9},{6,10},{7,11},{8,12},{9,13},{1... | collective-permute-start | bytes 983048 | tf_op jit(solution)/shard_map/ppermute | solution.py:73
  213.6 23.4 %collective-permute-start.13 = (bf16[64,2560]{1,0:T(8,128)(2,1)S(1)}, bf16[64,2560]{1,0:T(8,128)(2,1)S(1)}, u32[]{:S(2)}, u32[]{:S(2)}) collective-permute-start(bf16[64,2560]{1,0:T(8,128)(2,1)S(1)} %add_near.12), channel_id=1, source_target_pairs={{0,8},{1,9},{2,10},{3,11},{4,12},{5,13},{6,14},{7,15},{8,0},{9,1},... | collective-permute-start | bytes 983048 | tf_op jit(solution)/shard_map/ppermute | solution.py:73
  238.3 18.1 %collective-permute-start.18 = (bf16[64,2560]{1,0:T(8,128)(2,1)S(1)}, bf16[64,2560]{1,0:T(8,128)(2,1)S(1)}, u32[]{:S(2)}, u32[]{:S(2)}) collective-permute-start(bf16[64,2560]{1,0:T(8,128)(2,1)S(1)} %get-tuple-element.119.refs_0_), channel_id=1, source_target_pairs={{0,4},{1,5},{2,6},{3,7},{4,8},{5,9},{6,10},{7,11},{8,12},{9,13},{1... | collective-permute-start | bytes 983048 | tf_op jit(solution)/shard_map/ppermute | solution.py:73
  239.4 27.0 %collective-permute-start.19 = (bf16[64,2560]{1,0:T(8,128)(2,1)S(1)}, bf16[64,2560]{1,0:T(8,128)(2,1)S(1)}, u32[]{:S(2)}, u32[]{:S(2)}) collective-permute-start(bf16[64,2560]{1,0:T(8,128)(2,1)S(1)} %get-tuple-element.119.refs_0_), channel_id=1, source_target_pairs={{0,8},{1,9},{2,10},{3,11},{4,12},{5,13},{6,14},{7,15},{8,0},{9,1},... | collective-permute-start | bytes 983048 | tf_op jit(solution)/shard_map/ppermute | solution.py:73
  246.5 19.9 %collective-permute-start.24 = (bf16[64,2560]{1,0:T(8,128)(2,1)S(1)}, bf16[64,2560]{1,0:T(8,128)(2,1)S(1)}, u32[]{:S(2)}, u32[]{:S(2)}) collective-permute-start(bf16[64,2560]{1,0:T(8,128)(2,1)S(1)} %collective-permute-done.20.refs_3_), channel_id=1, source_target_pairs={{0,2},{1,3},{2,0},{3,1},{4,6},{5,7},{6,4},{7,5},{8,10},{9,11},{10,... | collective-permute-start | bytes 983048 | tf_op jit(solution)/shard_map/ppermute | solution.py:69
  319.4 14.9 %collective-permute-start.32 = (bf16[64,2560]{1,0:T(8,128)(2,1)S(1)}, bf16[64,2560]{1,0:T(8,128)(2,1)S(1)}, u32[]{:S(2)}, u32[]{:S(2)}) collective-permute-start(bf16[64,2560]{1,0:T(8,128)(2,1)S(1)} %get-tuple-element.132), channel_id=1, source_target_pairs={{0,2},{1,3},{2,0},{3,1},{4,6},{5,7},{6,4},{7,5},{8,10},{9,11},{10,... | collective-permute-start | bytes 983048 | tf_op jit(solution)/shard_map/ppermute | solution.py:69
  319.7 21.5 %collective-permute-start.30 = (bf16[64,2560]{1,0:T(8,128)(2,1)S(1)}, bf16[64,2560]{1,0:T(8,128)(2,1)S(1)}, u32[]{:S(2)}, u32[]{:S(2)}) collective-permute-start(bf16[64,2560]{1,0:T(8,128)(2,1)S(1)} %get-tuple-element.131), channel_id=1, source_target_pairs={{0,2},{1,3},{2,0},{3,1},{4,6},{5,7},{6,4},{7,5},{8,10},{9,11},{10,... | collective-permute-start | bytes 983048 | tf_op jit(solution)/shard_map/ppermute | solution.py:69
  321.9 26.4 %collective-permute-start.29 = (bf16[64,2560]{1,0:T(8,128)(2,1)}, bf16[64,2560]{1,0:T(8,128)(2,1)}, u32[]{:S(2)}, u32[]{:S(2)}) collective-permute-start(bf16[64,2560]{1,0:T(8,128)(2,1)} %get-tuple-element.130), channel_id=1, source_target_pairs={{0,2},{1,3},{2,0},{3,1},{4,6},{5,7},{6,4},{7,5},{8,10},{9,11},{10,... | collective-permute-start | bytes 983048 | tf_op jit(solution)/shard_map/ppermute | solution.py:69
  328.0 20.3 %collective-permute-start.35 = (bf16[64,2560]{1,0:T(8,128)(2,1)}, bf16[64,2560]{1,0:T(8,128)(2,1)}, u32[]{:S(2)}, u32[]{:S(2)}) collective-permute-start(bf16[64,2560]{1,0:T(8,128)(2,1)} %add_near.17), channel_id=1, source_target_pairs={{0,4},{1,5},{2,6},{3,7},{4,8},{5,9},{6,10},{7,11},{8,12},{9,13},{1... | collective-permute-start | bytes 983048 | tf_op jit(solution)/shard_map/ppermute | solution.py:73
  335.2 13.3 %collective-permute-start.33 = (bf16[64,2560]{1,0:T(8,128)(2,1)}, bf16[64,2560]{1,0:T(8,128)(2,1)}, u32[]{:S(2)}, u32[]{:S(2)}) collective-permute-start(bf16[64,2560]{1,0:T(8,128)(2,1)} %add_near.16), channel_id=1, source_target_pairs={{0,12},{1,13},{2,14},{3,15},{4,0},{5,1},{6,2},{7,3},{8,4},{9,5},{1... | collective-permute-start | bytes 983048 | tf_op jit(solution)/shard_map/ppermute | solution.py:73
  342.1 19.3 %collective-permute-start.31 = (bf16[64,2560]{1,0:T(8,128)(2,1)}, bf16[64,2560]{1,0:T(8,128)(2,1)}, u32[]{:S(2)}, u32[]{:S(2)}) collective-permute-start(bf16[64,2560]{1,0:T(8,128)(2,1)} %add_near.15), channel_id=1, source_target_pairs={{0,8},{1,9},{2,10},{3,11},{4,12},{5,13},{6,14},{7,15},{8,0},{9,1},... | collective-permute-start | bytes 983048 | tf_op jit(solution)/shard_map/ppermute | solution.py:73
  365.7 16.8 %collective-permute-start.39 = (bf16[64,2560]{1,0:T(8,128)(2,1)S(1)}, bf16[64,2560]{1,0:T(8,128)(2,1)S(1)}, u32[]{:S(2)}, u32[]{:S(2)}) collective-permute-start(bf16[64,2560]{1,0:T(8,128)(2,1)S(1)} %get-tuple-element.137.refs_0_), channel_id=1, source_target_pairs={{0,12},{1,13},{2,14},{3,15},{4,0},{5,1},{6,2},{7,3},{8,4},{9,5},{1... | collective-permute-start | bytes 983048 | tf_op jit(solution)/shard_map/ppermute | solution.py:73
  369.2 13.3 %collective-permute-start.41 = (bf16[64,2560]{1,0:T(8,128)(2,1)S(1)}, bf16[64,2560]{1,0:T(8,128)(2,1)S(1)}, u32[]{:S(2)}, u32[]{:S(2)}) collective-permute-start(bf16[64,2560]{1,0:T(8,128)(2,1)S(1)} %get-tuple-element.137.refs_0_), channel_id=1, source_target_pairs={{0,2},{1,3},{2,0},{3,1},{4,6},{5,7},{6,4},{7,5},{8,10},{9,11},{10,... | collective-permute-start | bytes 983048 | tf_op jit(solution)/shard_map/ppermute | solution.py:69
  370.0 16.0 %collective-permute-start.37 = (bf16[64,2560]{1,0:T(8,128)(2,1)S(1)}, bf16[64,2560]{1,0:T(8,128)(2,1)S(1)}, u32[]{:S(2)}, u32[]{:S(2)}) collective-permute-start(bf16[64,2560]{1,0:T(8,128)(2,1)S(1)} %get-tuple-element.137.refs_0_), channel_id=1, source_target_pairs={{0,4},{1,5},{2,6},{3,7},{4,8},{5,9},{6,10},{7,11},{8,12},{9,13},{1... | collective-permute-start | bytes 983048 | tf_op jit(solution)/shard_map/ppermute | solution.py:73
  370.0 28.2 %collective-permute-start.38 = (bf16[64,2560]{1,0:T(8,128)(2,1)S(1)}, bf16[64,2560]{1,0:T(8,128)(2,1)S(1)}, u32[]{:S(2)}, u32[]{:S(2)}) collective-permute-start(bf16[64,2560]{1,0:T(8,128)(2,1)S(1)} %get-tuple-element.137.refs_0_), channel_id=1, source_target_pairs={{0,8},{1,9},{2,10},{3,11},{4,12},{5,13},{6,14},{7,15},{8,0},{9,1},... | collective-permute-start | bytes 983048 | tf_op jit(solution)/shard_map/ppermute | solution.py:73
  382.4 15.8 %collective-permute-start.43 = (bf16[64,2560]{1,0:T(8,128)(2,1)S(1)}, bf16[64,2560]{1,0:T(8,128)(2,1)S(1)}, u32[]{:S(2)}, u32[]{:S(2)}) collective-permute-start(bf16[64,2560]{1,0:T(8,128)(2,1)S(1)} %collective-permute-done.39.refs_3_), channel_id=1, source_target_pairs={{0,2},{1,3},{2,0},{3,1},{4,6},{5,7},{6,4},{7,5},{8,10},{9,11},{10,... | collective-permute-start | bytes 983048 | tf_op jit(solution)/shard_map/ppermute | solution.py:69
  386.0 12.2 %collective-permute-start.42 = (bf16[64,2560]{1,0:T(8,128)(2,1)S(1)}, bf16[64,2560]{1,0:T(8,128)(2,1)S(1)}, u32[]{:S(2)}, u32[]{:S(2)}) collective-permute-start(bf16[64,2560]{1,0:T(8,128)(2,1)S(1)} %collective-permute-done.37.refs_1_), channel_id=1, source_target_pairs={{0,2},{1,3},{2,0},{3,1},{4,6},{5,7},{6,4},{7,5},{8,10},{9,11},{10,... | collective-permute-start | bytes 983048 | tf_op jit(solution)/shard_map/ppermute | solution.py:69
  398.9 11.9 %collective-permute-start.40 = (bf16[4,64,2560]{2,1,0:T(8,128)(2,1)S(1)}, bf16[4,64,2560]{2,1,0:T(8,128)(2,1)S(1)}, u32[]{:S(2)}, u32[]{:S(2)}) collective-permute-start(bf16[4,64,2560]{2,1,0:T(8,128)(2,1)S(1)} %stack.76.refs_0_), channel_id=1, source_target_pairs={{0,1},{1,0},{2,3},{3,2},{4,5},{5,4},{6,7},{7,6},{8,9},{9,8},{10,11... | collective-permute-start | bytes 3932168 | tf_op jit(solution)/shard_map/ppermute | solution.py:65
  445.0 14.9 %collective-permute-start.51 = (bf16[64,2560]{1,0:T(8,128)(2,1)}, bf16[64,2560]{1,0:T(8,128)(2,1)S(1)}, u32[]{:S(2)}, u32[]{:S(2)}) collective-permute-start(bf16[64,2560]{1,0:T(8,128)(2,1)} %get-tuple-element.150), channel_id=1, source_target_pairs={{0,2},{1,3},{2,0},{3,1},{4,6},{5,7},{6,4},{7,5},{8,10},{9,11},{10,... | collective-permute-start | bytes 983048 | tf_op jit(solution)/shard_map/ppermute | solution.py:69
  445.0 21.9 %collective-permute-start.49 = (bf16[64,2560]{1,0:T(8,128)(2,1)}, bf16[64,2560]{1,0:T(8,128)(2,1)S(1)}, u32[]{:S(2)}, u32[]{:S(2)}) collective-permute-start(bf16[64,2560]{1,0:T(8,128)(2,1)} %get-tuple-element.149), channel_id=1, source_target_pairs={{0,2},{1,3},{2,0},{3,1},{4,6},{5,7},{6,4},{7,5},{8,10},{9,11},{10,... | collective-permute-start | bytes 983048 | tf_op jit(solution)/shard_map/ppermute | solution.py:69
  446.4 27.5 %collective-permute-start.48 = (bf16[64,2560]{1,0:T(8,128)(2,1)}, bf16[64,2560]{1,0:T(8,128)(2,1)S(1)}, u32[]{:S(2)}, u32[]{:S(2)}) collective-permute-start(bf16[64,2560]{1,0:T(8,128)(2,1)} %get-tuple-element.148), channel_id=1, source_target_pairs={{0,2},{1,3},{2,0},{3,1},{4,6},{5,7},{6,4},{7,5},{8,10},{9,11},{10,... | collective-permute-start | bytes 983048 | tf_op jit(solution)/shard_map/ppermute | solution.py:69
  453.0 20.9 %collective-permute-start.54 = (bf16[64,2560]{1,0:T(8,128)(2,1)S(1)}, bf16[64,2560]{1,0:T(8,128)(2,1)S(1)}, u32[]{:S(2)}, u32[]{:S(2)}) collective-permute-start(bf16[64,2560]{1,0:T(8,128)(2,1)S(1)} %add_near.20), channel_id=1, source_target_pairs={{0,4},{1,5},{2,6},{3,7},{4,8},{5,9},{6,10},{7,11},{8,12},{9,13},{1... | collective-permute-start | bytes 983048 | tf_op jit(solution)/shard_map/ppermute | solution.py:73
  460.0 13.9 %collective-permute-start.52 = (bf16[64,2560]{1,0:T(8,128)(2,1)S(1)}, bf16[64,2560]{1,0:T(8,128)(2,1)S(1)}, u32[]{:S(2)}, u32[]{:S(2)}) collective-permute-start(bf16[64,2560]{1,0:T(8,128)(2,1)S(1)} %add_near.19), channel_id=1, source_target_pairs={{0,12},{1,13},{2,14},{3,15},{4,0},{5,1},{6,2},{7,3},{8,4},{9,5},{1... | collective-permute-start | bytes 983048 | tf_op jit(solution)/shard_map/ppermute | solution.py:73
  467.0 15.7 %collective-permute-start.50 = (bf16[64,2560]{1,0:T(8,128)(2,1)S(1)}, bf16[64,2560]{1,0:T(8,128)(2,1)S(1)}, u32[]{:S(2)}, u32[]{:S(2)}) collective-permute-start(bf16[64,2560]{1,0:T(8,128)(2,1)S(1)} %add_near.18), channel_id=1, source_target_pairs={{0,8},{1,9},{2,10},{3,11},{4,12},{5,13},{6,14},{7,15},{8,0},{9,1},... | collective-permute-start | bytes 983048 | tf_op jit(solution)/shard_map/ppermute | solution.py:73
  485.9 17.0 %collective-permute-start.55 = (bf16[64,2560]{1,0:T(8,128)(2,1)S(1)}, bf16[64,2560]{1,0:T(8,128)(2,1)S(1)}, u32[]{:S(2)}, u32[]{:S(2)}) collective-permute-start(bf16[64,2560]{1,0:T(8,128)(2,1)S(1)} %get-tuple-element.153.refs_0_), channel_id=1, source_target_pairs={{0,4},{1,5},{2,6},{3,7},{4,8},{5,9},{6,10},{7,11},{8,12},{9,13},{1... | collective-permute-start | bytes 983048 | tf_op jit(solution)/shard_map/ppermute | solution.py:73
  486.8 27.0 %collective-permute-start.56 = (bf16[64,2560]{1,0:T(8,128)(2,1)S(1)}, bf16[64,2560]{1,0:T(8,128)(2,1)S(1)}, u32[]{:S(2)}, u32[]{:S(2)}) collective-permute-start(bf16[64,2560]{1,0:T(8,128)(2,1)S(1)} %get-tuple-element.153.refs_0_), channel_id=1, source_target_pairs={{0,8},{1,9},{2,10},{3,11},{4,12},{5,13},{6,14},{7,15},{8,0},{9,1},... | collective-permute-start | bytes 983048 | tf_op jit(solution)/shard_map/ppermute | solution.py:73
  493.8 20.0 %collective-permute-start.61 = (bf16[64,2560]{1,0:T(8,128)(2,1)S(1)}, bf16[64,2560]{1,0:T(8,128)(2,1)S(1)}, u32[]{:S(2)}, u32[]{:S(2)}) collective-permute-start(bf16[64,2560]{1,0:T(8,128)(2,1)S(1)} %collective-permute-done.57.refs_3_), channel_id=1, source_target_pairs={{0,2},{1,3},{2,0},{3,1},{4,6},{5,7},{6,4},{7,5},{8,10},{9,11},{10,... | collective-permute-start | bytes 983048 | tf_op jit(solution)/shard_map/ppermute | solution.py:69
  502.9 11.6 %collective-permute-start.60 = (bf16[64,2560]{1,0:T(8,128)(2,1)S(1)}, bf16[64,2560]{1,0:T(8,128)(2,1)S(1)}, u32[]{:S(2)}, u32[]{:S(2)}) collective-permute-start(bf16[64,2560]{1,0:T(8,128)(2,1)S(1)} %collective-permute-done.55.refs_1_), channel_id=1, source_target_pairs={{0,2},{1,3},{2,0},{3,1},{4,6},{5,7},{6,4},{7,5},{8,10},{9,11},{10,... | collective-permute-start | bytes 983048 | tf_op jit(solution)/shard_map/ppermute | solution.py:69
  523.4 82.6 %all-to-all-start.2 = ((bf16[16,160,640]{2,1,0:T(8,128)(2,1)}), bf16[16,160,640]{2,1,0:T(8,128)(2,1)S(1)}, u32[]{:S(2)}, u32[]{:S(2)}) async-start(bf16[16,160,640]{2,1,0:T(8,128)(2,1)} %bitcast.43), calls=%async_computation.3 | async-start | bytes 6553600 | tf_op jit(solution)/shard_map/all_to_all | solution.py:81
  533.3 125.4 %reduce-scatter.5.cloned.1.call-start = ((), (), s32[]{:S(2)}) async-start(), calls=%async_computation.7 | async-start | bytes 5898240 | tf_op jit(solution)/shard_map/reduce_scatter | solution.py:215
  573.7 18.3 %collective-permute-start.65 = (bf16[64,2560]{1,0:T(8,128)(2,1)}, bf16[64,2560]{1,0:T(8,128)(2,1)}, u32[]{:S(2)}, u32[]{:S(2)}) collective-permute-start(bf16[64,2560]{1,0:T(8,128)(2,1)} %get-tuple-element.168), channel_id=1, source_target_pairs={{0,2},{1,3},{2,0},{3,1},{4,6},{5,7},{6,4},{7,5},{8,10},{9,11},{10,... | collective-permute-start | bytes 983048 | tf_op jit(solution)/shard_map/ppermute | solution.py:69
  606.4 16.3 %collective-permute-start.69 = (bf16[64,2560]{1,0:T(8,128)(2,1)}, bf16[64,2560]{1,0:T(8,128)(2,1)S(1)}, u32[]{:S(2)}, u32[]{:S(2)}) collective-permute-start(bf16[64,2560]{1,0:T(8,128)(2,1)} %copy-done.110), channel_id=1, source_target_pairs={{0,2},{1,3},{2,0},{3,1},{4,6},{5,7},{6,4},{7,5},{8,10},{9,11},{10,... | collective-permute-start | bytes 983048 | tf_op jit(solution)/shard_map/ppermute | solution.py:69
  607.8 21.9 %collective-permute-start.67 = (bf16[64,2560]{1,0:T(8,128)(2,1)}, bf16[64,2560]{1,0:T(8,128)(2,1)S(1)}, u32[]{:S(2)}, u32[]{:S(2)}) collective-permute-start(bf16[64,2560]{1,0:T(8,128)(2,1)} %copy-done.108), channel_id=1, source_target_pairs={{0,2},{1,3},{2,0},{3,1},{4,6},{5,7},{6,4},{7,5},{8,10},{9,11},{10,... | collective-permute-start | bytes 983048 | tf_op jit(solution)/shard_map/ppermute | solution.py:69
  617.1 12.6 %collective-permute-start.72 = (bf16[64,2560]{1,0:T(8,128)(2,1)S(1)}, bf16[64,2560]{1,0:T(8,128)(2,1)S(1)}, u32[]{:S(2)}, u32[]{:S(2)}) collective-permute-start(bf16[64,2560]{1,0:T(8,128)(2,1)S(1)} %add_near.23), channel_id=1, source_target_pairs={{0,4},{1,5},{2,6},{3,7},{4,8},{5,9},{6,10},{7,11},{8,12},{9,13},{1... | collective-permute-start | bytes 983048 | tf_op jit(solution)/shard_map/ppermute | solution.py:73
  624.2 22.7 %collective-permute-start.68 = (bf16[64,2560]{1,0:T(8,128)(2,1)S(1)}, bf16[64,2560]{1,0:T(8,128)(2,1)S(1)}, u32[]{:S(2)}, u32[]{:S(2)}) collective-permute-start(bf16[64,2560]{1,0:T(8,128)(2,1)S(1)} %add_near.21), channel_id=1, source_target_pairs={{0,8},{1,9},{2,10},{3,11},{4,12},{5,13},{6,14},{7,15},{8,0},{9,1},... | collective-permute-start | bytes 983048 | tf_op jit(solution)/shard_map/ppermute | solution.py:73
  658.7 51.1 %all-to-all-start.3 = ((bf16[16,160,384]{2,1,0:T(8,128)(2,1)}), bf16[16,160,384]{2,1,0:T(8,128)(2,1)}, u32[]{:S(2)}, u32[]{:S(2)}) async-start(bf16[16,160,384]{2,1,0:T(8,128)(2,1)} %bitcast.44), calls=%async_computation.5 | async-start | bytes 3932160 | tf_op jit(solution)/shard_map/all_to_all | solution.py:81
  (157 other events, 1060.1 us)
Sparse Core Ops, SparseCore 0:
  73.3 54.7 all-gather.4
  196.4 82.8 all-gather.6
  443.1 80.2 reduce-scatter.2
  606.2 52.4 reduce-scatter.4

commit v5 on v4

--- a/solution.py
+++ b/solution.py
@@ -93,11 +93,11 @@
     return kernel_call(body, whole((4, *pieces[0].shape), BF), tuple(pieces), limit=8, name="stack")
 
 
-def gather_rows(own, *late, early=()):
+def gather_rows(own, *late, early=(), mid=()):
     near = [own] + [move_z(own, m) for m in (1, 2, 3)]
     far = [move_x(own)]
     far += [move_x(after(near[1], far[0], *early)), None, move_x(after(near[3], far[0], *early))]
-    far[2] = move_x(after(near[2], far[1], far[3]))
+    far[2] = move_x(after(near[2], far[1], far[3], *mid))
     near_all, far_all = stack(near), stack(far)
     last = after(far_all, *late) if late else far_all
     return (near_all, move_c(near_all), far_all, move_c(last)), near, far
@@ -217,23 +217,32 @@
 
 def unpack_second(second, hidden):
     rows = second.shape[1]
-
-    def body(s_ref, g_ref, u_ref):
+    left = 3 * hidden - SECOND
+
+    def body(s_ref, g_ref, u_ref, d_ref):
         for k in range(16):
-            c = s_ref[k].astype(F32)
+            b = s_ref[k]
+            c = b[:, : 2 * hidden].astype(F32)
             g_ref[:, k * hidden : (k + 1) * hidden] = c[:, :hidden]
             u_ref[:, k * hidden : (k + 1) * hidden] = c[:, hidden : 2 * hidden]
-
-    return kernel_call(body, [whole((rows, 16 * hidden), F32)] * 2, (second,), limit=16, name="unpack_second")
-
-
-def unpack_first(first, second, hidden):
+            d_ref[:, k * hidden : (k + 1) * hidden] = jnp.concatenate(
+                [b[:, 2 * hidden :], jnp.zeros((rows, left), BF)], axis=1
+            )
+
+    wide = (rows, 16 * hidden)
+    return kernel_call(
+        body, [whole(wide, F32), whole(wide, F32), whole(wide, BF)], (second,), limit=16, name="unpack_second"
+    )
+
+
+def unpack_first(first, down, hidden):
     rows, d = first.shape[1], HEAD_SIZE
     cut = SECOND - 2 * hidden
     rest = 4 * d + hidden - cut
 
-    def body(f_ref, s_ref, q_ref, k_ref, v_ref, o_ref, d_ref, tail_ref):
+    def body(f_ref, down_ref, q_ref, k_ref, v_ref, o_ref, d_ref, tail_ref):
         tail = jnp.zeros((rows, 3), F32)
+        d_ref[...] = down_ref[...].astype(F32)
         for k in range(16):
             b = f_ref[k].astype(F32)
             q_ref[:, k * d : (k + 1) * d] = b[:, :d]
@@ -245,12 +254,11 @@
                 k_ref[:, k // 4 * d : (k // 4 + 1) * d] = keys[:, :d]
                 v_ref[:, k // 4 * d : (k // 4 + 1) * d] = keys[:, d:]
             tail = tail + b[:, rest : rest + 3]
-            d_ref[:, k * hidden : k * hidden + cut] = s_ref[k][:, 2 * hidden :].astype(F32)
             d_ref[:, k * hidden + cut : (k + 1) * hidden] = b[:, 4 * d : rest]
         tail_ref[...] = tail
 
     outs = [whole((rows, w), F32) for w in (16 * d, 4 * d, 4 * d, 16 * d, 16 * hidden, 3)]
-    return kernel_call(body, outs, (first, second), limit=16, name="unpack_first")
+    return kernel_call(body, outs, (first, down), limit=16, name="unpack_first")
 
 
 def order_attention(mine_ref, other_ref, w_ref, out_ref, row_ref, info_ref):
@@ -305,7 +313,7 @@
     scale = HEAD_SIZE ** (-0.5)
 
     def body(place_ref, *refs):
-        x_refs = [refs[i // 4].at[i % 4] for i in range(16)]
+        x_refs = refs[:4]
         mine_ref, both_ref, kpos_ref, cos_ref, sin_ref = refs[4:9]
         h_ref, q_ref, k_ref, v_ref, ctx_ref, lse_ref, w_ref, wo_ref, row_ref, *part = refs[9:22]
         other_ref, info_ref, sem = refs[22:]
@@ -317,14 +325,20 @@
         gain = row_ref[0:1, :]
         counts = jnp.where(place_ref[3] == 0, row_ref[2:3, :], row_ref[3:4, :])
         length = jnp.sum(counts, axis=1, keepdims=True) / F32(width // 16)
-        for i in range(16):
-
-            @pl.loop(0, seg // 16)
-            def _(r):
-                at = pl.multiple_of(r * 16, 16)
-                xs = x_refs[i][pl.ds(at, 16), :].astype(F32)
-                inv = lax.rsqrt(jnp.mean(xs * xs, axis=-1, keepdims=True) + eps)
-                h_ref[pl.ds(i * seg + at, 16), :] = (xs * inv * gain).astype(BF)
+        for g in range(4):
+
+            @pl.loop(0, 4)
+            def _(m):
+                squares = jnp.zeros((seg, LANES), F32)
+                for b in range(width // LANES):
+                    tile = x_refs[g][m, :, b * LANES : (b + 1) * LANES].astype(F32)
+                    squares = squares + tile * tile
+                inv = lax.rsqrt(jnp.sum(squares, axis=1, keepdims=True) / F32(width) + eps)
+                to = pl.ds(pl.multiple_of((g * 4 + m) * seg, seg), seg)
+                for b in range(width // LANES):
+                    at = slice(b * LANES, (b + 1) * LANES)
+                    tile = x_refs[g][m, :, at].astype(F32)
+                    h_ref[to, at] = (tile * inv * gain[:, at]).astype(BF)
 
         for g in range(4):
             qkv = dot_nn(h_ref[g * 4 * seg : (g + 1) * 4 * seg, :], w_ref[...])
@@ -347,7 +361,7 @@
                 top = jnp.max(s, axis=1, keepdims=True)
                 e = jnp.exp(s - top)
                 tot = jnp.sum(e, axis=1, keepdims=True)
-                ctx = dot_nn((e / tot).astype(BF), v_ref[h, :n, :]).astype(BF)
+                ctx = dot_nn((e * (1.0 / tot)).astype(BF), v_ref[h, :n, :]).astype(BF)
                 for g in range(4):
                     to = pl.ds(pl.multiple_of((g * 4 + m) * seg, seg), seg)
                     ctx_ref[to, h * HEAD_SIZE : (h + 1) * HEAD_SIZE] = ctx[g * seg : (g + 1) * seg, :HEAD_SIZE]
@@ -490,23 +504,20 @@
     )
 
 
-def feed(place, pieces, first_mine, first_both, mine, both, hidden):
+def feed(place, pieces, first_mine, first_both, mine, other, hidden):
     seg, width = pieces[0].shape[1:]
     rows = 16 * seg
     columns = 2 * hidden
 
     def body(place_ref, *refs):
         h_refs = [refs[i // 4].at[i % 4] for i in range(16)]
-        fm_ref, fboth_ref, m_ref, both_ref, h_ref, gate_ref, act_ref, wg_ref, wd_ref, *part = refs[4:17]
-        fo_ref, o_ref, sem = refs[17:]
-        first = pltpu.make_async_copy(fboth_ref.at[1 - place_ref[3]], fo_ref, sem.at[0])
-        second = pltpu.make_async_copy(both_ref.at[1 - place_ref[3]], o_ref, sem.at[1])
+        fm_ref, fboth_ref, m_ref, o_ref, h_ref, gate_ref, act_ref, wg_ref, wd_ref, *part = refs[4:17]
+        fo_ref, sem = refs[17:]
+        first = pltpu.make_async_copy(fboth_ref.at[1 - place_ref[3]], fo_ref, sem)
         first.start()
-        second.start()
         for i in range(16):
             h_ref[i * seg : (i + 1) * seg, :] = h_refs[i][...]
         first.wait()
-        second.wait()
         order_feed(fm_ref, fo_ref, m_ref, o_ref, wg_ref, wd_ref, hidden)
         for g in range(4):
             rs = slice(g * 4 * seg, (g + 1) * 4 * seg)
@@ -523,14 +534,10 @@
     out = kernel_call(
         body,
         outs + part_shapes(seg, width),
-        (place, *pieces, first_mine, first_both, mine, both),
+        (place, *pieces, first_mine, first_both, mine, other),
         scalars=1,
-        far=(6, 8),
-        scratch=[
-            pltpu.VMEM(first_mine.shape, BF),
-            pltpu.VMEM(mine.shape, BF),
-            pltpu.SemaphoreType.DMA((2,)),
-        ],
+        far=(6,),
+        scratch=[pltpu.VMEM(first_mine.shape, BF), pltpu.SemaphoreType.DMA],
         limit=26,
         name="feed",
     )
@@ -755,11 +762,11 @@
     length = jnp.full((8, LANES), jnp.where(first, lengths[0], lengths[1]), F32)
     factor = jnp.full((8, LANES), F32(seqs * seq_len) / count, F32)
     terms, far, come = scatter_rows(part)
-    second_both = of_other(after(second_in, come[2]))
+    second_other = move_y(after(second_in, come[2]))
     resid, h2_own = rows_after_attention(terms, own, info)
-    pieces, _, _ = gather_rows(h2_own)
+    pieces, _, _ = gather_rows(h2_own, mid=(second_other,))
     (h2, gate_up, act, w_gu, w_d), part = feed(
-        place, pieces, first_in, first_both, second_in, second_both, hidden
+        place, pieces, first_in, first_both, second_in, second_other, hidden
     )
     okf = mine(valid).astype(F32)[:, None]
     terms, _, _ = scatter_rows(part)
@@ -783,12 +790,12 @@
     summed = over_sequences(after(shares, seconds, x_come[2]))
     dx = rows_at_end(terms, own, dresid, info)
     firsts = share_blocks(after(summed, seconds, dx))
-    grad_gate, grad_up = unpack_second(after(seconds, dx), hidden)
+    grad_gate, grad_up, down = unpack_second(after(seconds, dx), hidden)
     both_out = move_y(out_own)
     both_dx = move_y(dx)
     output = jnp.stack([jnp.where(first, out_own, both_out), jnp.where(first, both_out, out_own)])
     input_grad = jnp.stack([jnp.where(first, dx, both_dx), jnp.where(first, both_dx, dx)]).astype(F32)
-    grad_query, grad_key, grad_value, grad_out, grad_down, tails = unpack_first(firsts, seconds, hidden)
+    grad_query, grad_key, grad_value, grad_out, grad_down, tails = unpack_first(firsts, down, hidden)
     return (
         output,
         tails[0, 2] / (count * width),

time: 735 us -> 723 us (0.984)
  local copies, waits for them, and re-layouts: 89.8 us -> 67.5 us
  waiting for transfers between devices: 377 us -> 397 us
  Pallas kernels: 112 us -> 104 us
    unnamed x246 -> x200, local copies, waits for them, and re-layouts: 83.7 us -> 61.4 us
    all_to_all x4, waiting for transfers between devices: 90.3 us -> 101 us  [share_out(): return lax.all_to_all(a, 'context', split_axis=0, concat_axis=0, tiled=True)]
    ppermute x32, waiting for transfers between devices: 106 us -> 115 us  [move_x(): return lax.ppermute(a, 'context', [(k, k ^ 2) for k in range(16)])]
    pallas_call x39, Pallas kernels: 112 us -> 104 us  [kernel_call(): pl.pallas_call(body, out_shape=outs, in_specs=[spec(i) for i in range(len...]
    ppermute x2 -> x3, waiting for transfers between devices: 15.9 us -> 16.5 us  [move_y(): return lax.ppermute(a, 'tensor', [(0, 1), (1, 0)])]
  transfers between devices with their start and end apart: 82 -> 82, of which waited for: 56 -> 57; matrix products, arithmetic and copies ran while one was open for 1% -> 1% of each run, Pallas kernels for 9% -> 8%
where the time goes in v5:
time: 723 us; the launch traced here: 717 us
  waiting for transfers between devices  397 us (55%)
  starting transfers between devices  122 us (17%)
  Pallas kernels  104 us (14%)
  local copies, waits for them, and re-layouts  67.5 us (9%)
  between operations  19.2 us (3%)
  other arithmetic  7.96 us (1%)
    ppermute x24, waiting for transfers between devices, move_z(): lax.ppermute(a, 'context', [(k, (k + 4 * step) % 16) for k in range(16)])  133 us
    ppermute x32, waiting for transfers between devices, move_x(): return lax.ppermute(a, 'context', [(k, k ^ 2) for k in range(16)])  115 us
    pallas_call x39, Pallas kernels, kernel_call(): pl.pallas_call(body, out_shape=outs, in_specs=[spec(i) for i in range(len...  104 us
    all_to_all x4, waiting for transfers between devices, share_out(): return lax.all_to_all(a, 'context', split_axis=0, concat_axis=0, tiled=True)  101 us
    unnamed x200, local copies, waits for them, and re-layouts  61.4 us
    all_to_all x4, starting transfers between devices, share_out(): return lax.all_to_all(a, 'context', split_axis=0, concat_axis=0, tiled=True)  39.2 us
    ppermute x24, starting transfers between devices, move_z(): lax.ppermute(a, 'context', [(k, (k + 4 * step) % 16) for k in range(16)])  35.9 us
    ppermute x16, starting transfers between devices, move_c(): return lax.ppermute(a, 'context', [(k, k ^ 1) for k in range(16)])  23.1 us
  transfers between devices with their start and end apart: 82, of which 57 were waited for; matrix products, arithmetic and copies ran while one was open for 1% of the time, Pallas kernels for 8%

profile of v5, /device:TPU:11, one launch (start us, length us, event | category | flops | bytes accessed | tf_op | source)
XLA Modules:
  0.0 716.6 jit_solution(2615276058657533169)
XLA Ops:
  19.3 6.6 all-to-all-start
  26.0 44.4 %all-to-all-done.refs_4_ = bf16[16,160,384]{2,1,0:T(8,128)(2,1)S(1)} async-done(((bf16[16,160,384]{2,1,0:T(8,128)(2,1)}), bf16[16,160,384]{2,1,0:T(8,128)(2,1)S(1)}, u32[]{:S(2)}, u32[]{:S(2)}) %all-to-all-start) | async-done | bytes 1966112 | tf_op jit(solution)/shard_map/all_to_all | solution.py:81
  73.2 6.4 collective-permute-done.4.refs_0_
  80.7 6.3 collective-permute-done.2.refs_3_
  89.0 9.6 %collective-permute-done.1.refs_2_ = bf16[64,2560]{1,0:T(8,128)(2,1)} collective-permute-done((bf16[64,2560]{1,0:T(8,128)(2,1)S(1)}, bf16[64,2560]{1,0:T(8,128)(2,1)}, u32[]{:S(2)}, u32[]{:S(2)}) %collective-permute-start.1) | collective-permute-done | bytes 327712 | tf_op jit(solution)/shard_map/ppermute | solution.py:73
  109.5 13.9 %all-to-all-start.1 = ((bf16[16,160,640]{2,1,0:T(8,128)(2,1)}), bf16[16,160,640]{2,1,0:T(8,128)(2,1)}, u32[]{:S(2)}, u32[]{:S(2)}) async-start(bf16[16,160,640]{2,1,0:T(8,128)(2,1)} %pack_second.1), calls=%async_computation.1 | async-start | bytes 6553600 | tf_op jit(solution)/shard_map/all_to_all | solution.py:81
  137.2 16.1 %attention.1 = (bf16[1024,2560]{1,0:T(8,128)(2,1)S(1)}, bf16[2,1024,128]{2,1,0:T(8,128)(2,1)S(1)}, bf16[2,1024,128]{2,1,0:T(8,128)(2,1)S(1)}, bf16[2,1024,128]{2...) custom-call(s32[4]{0:T(128)S(1)} %pad_add_fusion.place_ref, ...), custom_call_target="tpu_custom_call" | custom-call | tf_op jit(solution)/shard_map/attention/pallas_call | solution.py:40
  166.7 15.7 %collective-permute-done.12.c_ref = bf16[64,2560]{1,0:T(8,128)(2,1)S(1)} collective-permute-done((bf16[64,2560]{1,0:T(8,128)(2,1)S(1)}, bf16[64,2560]{1,0:T(8,128)(2,1)S(1)}, u32[]{:S(2)}, u32[]{:S(2)}) %collective-permute-start.12) | collective-permute-done | bytes 327712 | tf_op jit(solution)/shard_map/ppermute | solution.py:69
  183.1 13.1 %all-to-all-done.1.refs_6_ = bf16[16,160,640]{2,1,0:T(8,128)(2,1)} async-done(((bf16[16,160,640]{2,1,0:T(8,128)(2,1)}), bf16[16,160,640]{2,1,0:T(8,128)(2,1)}, u32[]{:S(2)}, u32[]{:S(2)}) %all-to-all-start.1) | async-done | bytes 3276832 | tf_op jit(solution)/shard_map/all_to_all | solution.py:81
  200.8 6.6 collective-permute-done.16.c_ref
  208.3 6.2 collective-permute-done.14.c_ref
  223.0 15.6 %collective-permute-done.13.refs_3_ = bf16[64,2560]{1,0:T(8,128)(2,1)S(1)} collective-permute-done((bf16[64,2560]{1,0:T(8,128)(2,1)S(1)}, bf16[64,2560]{1,0:T(8,128)(2,1)S(1)}, u32[]{:S(2)}, u32[]{:S(2)}) %collective-permute-start.13) | collective-permute-done | bytes 327712 | tf_op jit(solution)/shard_map/ppermute | solution.py:73
  240.8 4.9 collective-permute-start.19
  248.1 9.7 %collective-permute-done.18.refs_1_ = bf16[64,2560]{1,0:T(8,128)(2,1)S(1)} collective-permute-done((bf16[64,2560]{1,0:T(8,128)(2,1)S(1)}, bf16[64,2560]{1,0:T(8,128)(2,1)S(1)}, u32[]{:S(2)}, u32[]{:S(2)}) %collective-permute-start.18) | collective-permute-done | bytes 327712 | tf_op jit(solution)/shard_map/ppermute | solution.py:73
  258.0 9.8 %collective-permute-done.19.refs_2_ = bf16[64,2560]{1,0:T(8,128)(2,1)S(1)} collective-permute-done((bf16[64,2560]{1,0:T(8,128)(2,1)S(1)}, bf16[64,2560]{1,0:T(8,128)(2,1)S(1)}, u32[]{:S(2)}, u32[]{:S(2)}) %collective-permute-start.19) | collective-permute-done | bytes 327712 | tf_op jit(solution)/shard_map/ppermute | solution.py:73
  271.5 5.4 collective-permute-done.26.refs_2_
  281.8 17.0 %feed.1 = (bf16[1024,2560]{1,0:T(8,128)(2,1)}, f32[1024,864]{1,0:T(8,128)S(1)}, bf16[1024,432]{1,0:T(8,128)(2,1)S(1)}, bf16[2560,864]{1,0:T(8,128)(2,1)}, bf16[2...) custom-call(s32[4]{0:T(128)S(1)} %pad_add_fusion.place_ref, ...), custom_call_target="tpu_custom_call" | custom-call | tf_op jit(solution)/shard_map/feed/pallas_call | solution.py:40
  315.6 4.9 collective-permute-done.35.c_ref
  329.8 4.8 collective-permute-done.31.c_ref
  341.7 12.0 %collective-permute-done.32.refs_3_ = bf16[64,2560]{1,0:T(8,128)(2,1)} collective-permute-done((bf16[64,2560]{1,0:T(8,128)(2,1)}, bf16[64,2560]{1,0:T(8,128)(2,1)}, u32[]{:S(2)}, u32[]{:S(2)}) %collective-permute-start.32) | collective-permute-done | bytes 327712 | tf_op jit(solution)/shard_map/ppermute | solution.py:73
  369.3 6.8 collective-permute-done.38.refs_1_
  376.9 12.5 %collective-permute-done.39.refs_2_ = bf16[64,2560]{1,0:T(8,128)(2,1)S(1)} collective-permute-done((bf16[64,2560]{1,0:T(8,128)(2,1)S(1)}, bf16[64,2560]{1,0:T(8,128)(2,1)S(1)}, u32[]{:S(2)}, u32[]{:S(2)}) %collective-permute-start.39) | collective-permute-done | bytes 327712 | tf_op jit(solution)/shard_map/ppermute | solution.py:73
  389.6 9.5 %collective-permute-start.41 = (bf16[4,64,2560]{2,1,0:T(8,128)(2,1)S(1)}, bf16[4,64,2560]{2,1,0:T(8,128)(2,1)S(1)}, u32[]{:S(2)}, u32[]{:S(2)}) collective-permute-start(bf16[4,64,2560]{2,1,0:T(8,128)(2,1)S(1)} %stack.76.refs_0_), channel_id=1, source_target_pairs={{0,1},{1,0},{2,3},{3,2},{4,5},{5,4},{6,7},{7,6},{8,9},{9,8},{10,11... | collective-permute-start | bytes 3932168 | tf_op jit(solution)/shard_map/ppermute | solution.py:65
  399.1 4.9 collective-permute-start.46
  409.0 8.9 %feed_back.1 = (bf16[1024,2560]{1,0:T(8,128)(2,1)S(1)}, bf16[1024,864]{1,0:T(8,128)(2,1)S(1)}, bf16[4,64,2560]{2,1,0:T(8,128)(2,1)S(1)}, bf16[4,64,2560]{2,1,0:T...) custom-call(bf16[4,64,2560]{2,1,0:T(8,128)(2,1)S(1)} %stack.76.refs_0_, ...), custom_call_target="tpu_custom_call" | custom-call | tf_op jit(solution)/shard_map/feed_back/pallas_call | solution.py:40
  422.5 9.1 %feed_grads.1 = (bf16[2,16,160,640]{3,2,1,0:T(8,128)(2,1)S(1)}, bf16[2560,16]{1,0:T(8,128)(2,1)S(1)}, f32[2560,1]{1,0:T(8,128)S(1)}) custom-call(s32[4]{0:T(128)S(1)} %pad_add_fusion.place_ref, bf16[2560,432]{1,0:T(8,128)(2,1)S(1)} %down_grads.1.down_ref, bf16[1024,2560]{1,0:T(8,128)(2,1)S(1)} %bitcast.37, bf16[1024,864]{1,0:T(8,128)(2,1)S(1)} %get-tuple-element.179.dgu_ref, ...), custom_call_target="tpu_custom_call" | custom-call | tf_op jit(solution)/shard_map/feed_grads/pallas_call | solution.py:40
  439.6 6.4 collective-permute-done.54.c_ref
  446.2 6.8 collective-permute-done.52.c_ref
  453.2 6.8 collective-permute-done.50.c_ref
  460.2 6.8 collective-permute-done.49.refs_2_
  467.0 8.8 %collective-permute-done.51.refs_3_ = bf16[64,2560]{1,0:T(8,128)(2,1)S(1)} collective-permute-done((bf16[64,2560]{1,0:T(8,128)(2,1)S(1)}, bf16[64,2560]{1,0:T(8,128)(2,1)S(1)}, u32[]{:S(2)}, u32[]{:S(2)}) %collective-permute-start.51) | collective-permute-done | bytes 327712 | tf_op jit(solution)/shard_map/ppermute | solution.py:73
  479.9 4.9 collective-permute-start.57
  487.3 8.7 %collective-permute-done.56.refs_1_ = bf16[64,2560]{1,0:T(8,128)(2,1)S(1)} collective-permute-done((bf16[64,2560]{1,0:T(8,128)(2,1)S(1)}, bf16[64,2560]{1,0:T(8,128)(2,1)S(1)}, u32[]{:S(2)}, u32[]{:S(2)}) %collective-permute-start.56) | collective-permute-done | bytes 327712 | tf_op jit(solution)/shard_map/ppermute | solution.py:73
  497.2 9.7 %collective-permute-done.57.refs_2_ = bf16[64,2560]{1,0:T(8,128)(2,1)S(1)} collective-permute-done((bf16[64,2560]{1,0:T(8,128)(2,1)S(1)}, bf16[64,2560]{1,0:T(8,128)(2,1)S(1)}, u32[]{:S(2)}, u32[]{:S(2)}) %collective-permute-start.57) | collective-permute-done | bytes 327712 | tf_op jit(solution)/shard_map/ppermute | solution.py:73
  507.0 7.2 %collective-permute-done.63.refs_2_ = bf16[64,2560]{1,0:T(8,128)(2,1)S(1)} collective-permute-done((bf16[64,2560]{1,0:T(8,128)(2,1)S(1)}, bf16[64,2560]{1,0:T(8,128)(2,1)S(1)}, u32[]{:S(2)}, u32[]{:S(2)}) %collective-permute-start.63) | collective-permute-done | bytes 327712 | tf_op jit(solution)/shard_map/ppermute | solution.py:69
  515.0 12.2 %all-to-all-start.2 = ((bf16[16,160,640]{2,1,0:T(8,128)(2,1)}), bf16[16,160,640]{2,1,0:T(8,128)(2,1)}, u32[]{:S(2)}, u32[]{:S(2)}) async-start(bf16[16,160,640]{2,1,0:T(8,128)(2,1)} %bitcast.41), calls=%async_computation.3 | async-start | bytes 6553600 | tf_op jit(solution)/shard_map/all_to_all | solution.py:81
  542.8 13.9 %attention_back.1 = (bf16[1024,2560]{1,0:T(8,128)(2,1)S(1)}, bf16[1024,480]{1,0:T(8,128)(2,1)S(1)}, bf16[4,64,2560]{2,1,0:T(8,128)(2,1)S(1)}, bf16[4,64,2560]{2,...) custom-call(s32[4]{0:T(128)S(1)} %pad_add_fusion.place_ref, ...), custom_call_target="tpu_custom_call" | custom-call | tf_op jit(solution)/shard_map/attention_back/pallas_call | solution.py:40
  564.0 7.2 %attention_grads.1 = bf16[2,16,160,384]{3,2,1,0:T(8,128)(2,1)S(1)} custom-call(s32[4]{0:T(128)S(1)} %pad_add_fusion.place_ref, bf16[1024,2560]{1,0:T(8,128)(2,1)S(1)} %copy-done.16, bf16[1024,480]{1,0:T(8,128)(2,1)S(1)} %get-tuple-element.171.dqkv_ref, bf16[1024,2560]{1,0:T(8,128)(2,1)S(1)} %get-tuple-element.172.da_ref, bf16[1024,160]{1,0:T(8,128)(2,1)S(1)} %copy-done.56, ...), custom_call_target="tpu_custom_call" | custom-call | tf_op jit(solution)/shard_map/attention_grads/pallas_call | solution.py:40
  575.5 24.7 %all-to-all-done.2.s_ref = bf16[16,160,640]{2,1,0:T(8,128)(2,1)} async-done(((bf16[16,160,640]{2,1,0:T(8,128)(2,1)}), bf16[16,160,640]{2,1,0:T(8,128)(2,1)}, u32[]{:S(2)}, u32[]{:S(2)}) %all-to-all-start.2) | async-done | bytes 3276832 | tf_op jit(solution)/shard_map/all_to_all | solution.py:81
  603.5 6.1 collective-permute-done.72.c_ref
  610.6 6.0 collective-permute-done.70.c_ref
  624.4 15.8 %collective-permute-done.69.refs_3_ = bf16[64,2560]{1,0:T(8,128)(2,1)S(1)} collective-permute-done((bf16[64,2560]{1,0:T(8,128)(2,1)S(1)}, bf16[64,2560]{1,0:T(8,128)(2,1)S(1)}, u32[]{:S(2)}, u32[]{:S(2)}) %collective-permute-start.69) | collective-permute-done | bytes 327712 | tf_op jit(solution)/shard_map/ppermute | solution.py:73
  640.8 9.9 %reduce-scatter.5.cloned.1.call-done = bf16[1,16,160,384]{3,2,1,0:T(8,128)(2,1)} async-done(((bf16[2,16,160,384]{3,2,1,0:T(8,128)(2,1)}), bf16[1,16,160,384]{3,2,1,0:T(8,128)(2,1)}) %reduce-scatter.5.cloned.1.call-update) | async-done | bytes 1966096 | tf_op jit(solution)/shard_map/reduce_scatter | solution.py:215
  650.8 6.5 all-to-all-start.3
  657.6 8.6 %collective-permute-done.37 = bf16[64,2560]{1,0:T(8,128)(2,1)S(1)} collective-permute-done((bf16[64,2560]{1,0:T(8,128)(2,1)S(1)}, bf16[64,2560]{1,0:T(8,128)(2,1)S(1)}, u32[]{:S(2)}, u32[]{:S(2)}) %collective-permute-start.37) | collective-permute-done | bytes 327712 | tf_op jit(solution)/shard_map/ppermute | solution.py:77
  667.6 6.8 collective-permute-done.74
  675.6 6.2 unpack_second.1
  682.8 19.1 %all-to-all-done.3.f_ref = bf16[16,160,384]{2,1,0:T(8,128)(2,1)S(1)} async-done(((bf16[16,160,384]{2,1,0:T(8,128)(2,1)}), bf16[16,160,384]{2,1,0:T(8,128)(2,1)S(1)}, u32[]{:S(2)}, u32[]{:S(2)}) %all-to-all-start.3) | async-done | bytes 1966112 | tf_op jit(solution)/shard_map/all_to_all | solution.py:81
  (399 shorter events, 207.3 us)
Async XLA Ops:
  19.3 51.2 %all-to-all-start = ((bf16[16,160,384]{2,1,0:T(8,128)(2,1)}), bf16[16,160,384]{2,1,0:T(8,128)(2,1)S(1)}, u32[]{:S(2)}, u32[]{:S(2)}) async-start(bf16[16,160,384]{2,1,0:T(8,128)(2,1)} %copy-done.10), calls=%async_computation | async-start | bytes 3932160 | tf_op jit(solution)/shard_map/all_to_all | solution.py:81
  25.8 102.3 %all-gather.3.cloned.1.call-start = ((), (), s32[]{:S(2)}) async-start(), calls=%async_computation.8 | async-start | bytes 5898240 | tf_op jit(solution)/shard_map/all_gather | solution.py:211
  71.6 15.4 %collective-permute-start.2 = (bf16[64,2560]{1,0:T(8,128)(2,1)S(1)}, bf16[64,2560]{1,0:T(8,128)(2,1)S(1)}, u32[]{:S(2)}, u32[]{:S(2)}) collective-permute-start(bf16[64,2560]{1,0:T(8,128)(2,1)S(1)} %dynamic-slice_bitcast_fusion.2.refs_0_.refs_6_), channel_id=1, source_target_pairs={{0,12},{1,13},{2,14},{3,15},{4,0},{5,1},{6,2},{7,3},{8,4},{9,5},{1... | collective-permute-start | bytes 983048 | tf_op jit(solution)/shard_map/ppermute | solution.py:73
  72.0 26.6 %collective-permute-start.1 = (bf16[64,2560]{1,0:T(8,128)(2,1)S(1)}, bf16[64,2560]{1,0:T(8,128)(2,1)}, u32[]{:S(2)}, u32[]{:S(2)}) collective-permute-start(bf16[64,2560]{1,0:T(8,128)(2,1)S(1)} %dynamic-slice_bitcast_fusion.2.refs_0_.refs_6_), channel_id=1, source_target_pairs={{0,8},{1,9},{2,10},{3,11},{4,12},{5,13},{6,14},{7,15},{8,0},{9,1},... | collective-permute-start | bytes 983048 | tf_op jit(solution)/shard_map/ppermute | solution.py:73
  79.6 19.0 %collective-permute-start.5 = (bf16[64,2560]{1,0:T(8,128)(2,1)S(1)}, bf16[64,2560]{1,0:T(8,128)(2,1)S(1)}, u32[]{:S(2)}, u32[]{:S(2)}) collective-permute-start(bf16[64,2560]{1,0:T(8,128)(2,1)S(1)} %collective-permute-done.refs_1_), channel_id=1, source_target_pairs={{0,2},{1,3},{2,0},{3,1},{4,6},{5,7},{6,4},{7,5},{8,10},{9,11},{10,... | collective-permute-start | bytes 983048 | tf_op jit(solution)/shard_map/ppermute | solution.py:69
  87.0 11.5 %collective-permute-start.6 = (bf16[64,2560]{1,0:T(8,128)(2,1)S(1)}, bf16[64,2560]{1,0:T(8,128)(2,1)S(1)}, u32[]{:S(2)}, u32[]{:S(2)}) collective-permute-start(bf16[64,2560]{1,0:T(8,128)(2,1)S(1)} %collective-permute-done.2.refs_3_), channel_id=1, source_target_pairs={{0,2},{1,3},{2,0},{3,1},{4,6},{5,7},{6,4},{7,5},{8,10},{9,11},{10,... | collective-permute-start | bytes 983048 | tf_op jit(solution)/shard_map/ppermute | solution.py:69
  98.6 10.2 %collective-permute-start.7 = (bf16[64,2560]{1,0:T(8,128)(2,1)}, bf16[64,2560]{1,0:T(8,128)(2,1)S(1)}, u32[]{:S(2)}, u32[]{:S(2)}) collective-permute-start(bf16[64,2560]{1,0:T(8,128)(2,1)} %collective-permute-done.1.refs_2_), channel_id=1, source_target_pairs={{0,2},{1,3},{2,0},{3,1},{4,6},{5,7},{6,4},{7,5},{8,10},{9,11},{10,... | collective-permute-start | bytes 983048 | tf_op jit(solution)/shard_map/ppermute | solution.py:69
  109.5 86.8 %all-to-all-start.1 = ((bf16[16,160,640]{2,1,0:T(8,128)(2,1)}), bf16[16,160,640]{2,1,0:T(8,128)(2,1)}, u32[]{:S(2)}, u32[]{:S(2)}) async-start(bf16[16,160,640]{2,1,0:T(8,128)(2,1)} %pack_second.1), calls=%async_computation.1 | async-start | bytes 6553600 | tf_op jit(solution)/shard_map/all_to_all | solution.py:81
  123.4 391.0 %reduce-scatter.3.cloned.1.call-start = ((), (), s32[]{:S(2)}) async-start(), calls=%async_computation.6 | async-start | bytes 9830400 | tf_op jit(solution)/shard_map/reduce_scatter | solution.py:215
  166.4 16.0 %collective-permute-start.12 = (bf16[64,2560]{1,0:T(8,128)(2,1)S(1)}, bf16[64,2560]{1,0:T(8,128)(2,1)S(1)}, u32[]{:S(2)}, u32[]{:S(2)}) collective-permute-start(bf16[64,2560]{1,0:T(8,128)(2,1)S(1)} %get-tuple-element.116), channel_id=1, source_target_pairs={{0,2},{1,3},{2,0},{3,1},{4,6},{5,7},{6,4},{7,5},{8,10},{9,11},{10,... | collective-permute-start | bytes 983048 | tf_op jit(solution)/shard_map/ppermute | solution.py:69
  196.2 72.6 %collective-permute-start.25 = (bf16[16,160,640]{2,1,0:T(8,128)(2,1)}, bf16[16,160,640]{2,1,0:T(8,128)(2,1)S(1)}, u32[]{:S(2)}, u32[]{:S(2)}) collective-permute-start(bf16[16,160,640]{2,1,0:T(8,128)(2,1)} %all-to-all-done.1.refs_6_), channel_id=1, source_target_pairs={{0,16},{16,0},{1,17},{17,1},{2,18},{18,2},{3,19},{19,3},{4,20},{20... | collective-permute-start | bytes 9830408 | tf_op jit(solution)/shard_map/ppermute | solution.py:77
  197.9 16.5 %collective-permute-start.14 = (bf16[64,2560]{1,0:T(8,128)(2,1)}, bf16[64,2560]{1,0:T(8,128)(2,1)S(1)}, u32[]{:S(2)}, u32[]{:S(2)}) collective-permute-start(bf16[64,2560]{1,0:T(8,128)(2,1)} %copy-done.89), channel_id=1, source_target_pairs={{0,2},{1,3},{2,0},{3,1},{4,6},{5,7},{6,4},{7,5},{8,10},{9,11},{10,... | collective-permute-start | bytes 983048 | tf_op jit(solution)/shard_map/ppermute | solution.py:69
  199.4 22.1 %collective-permute-start.11 = (bf16[64,2560]{1,0:T(8,128)(2,1)}, bf16[64,2560]{1,0:T(8,128)(2,1)S(1)}, u32[]{:S(2)}, u32[]{:S(2)}) collective-permute-start(bf16[64,2560]{1,0:T(8,128)(2,1)} %copy-done.88), channel_id=1, source_target_pairs={{0,2},{1,3},{2,0},{3,1},{4,6},{5,7},{6,4},{7,5},{8,10},{9,11},{10,... | collective-permute-start | bytes 983048 | tf_op jit(solution)/shard_map/ppermute | solution.py:69
  207.6 13.9 %collective-permute-start.17 = (bf16[64,2560]{1,0:T(8,128)(2,1)S(1)}, bf16[64,2560]{1,0:T(8,128)(2,1)S(1)}, u32[]{:S(2)}, u32[]{:S(2)}) collective-permute-start(bf16[64,2560]{1,0:T(8,128)(2,1)S(1)} %add_near.14), channel_id=1, source_target_pairs={{0,4},{1,5},{2,6},{3,7},{4,8},{5,9},{6,10},{7,11},{8,12},{9,13},{1... | collective-permute-start | bytes 983048 | tf_op jit(solution)/shard_map/ppermute | solution.py:73
  215.2 23.3 %collective-permute-start.13 = (bf16[64,2560]{1,0:T(8,128)(2,1)S(1)}, bf16[64,2560]{1,0:T(8,128)(2,1)S(1)}, u32[]{:S(2)}, u32[]{:S(2)}) collective-permute-start(bf16[64,2560]{1,0:T(8,128)(2,1)S(1)} %add_near.12), channel_id=1, source_target_pairs={{0,8},{1,9},{2,10},{3,11},{4,12},{5,13},{6,14},{7,15},{8,0},{9,1},... | collective-permute-start | bytes 983048 | tf_op jit(solution)/shard_map/ppermute | solution.py:73
  239.6 18.1 %collective-permute-start.18 = (bf16[64,2560]{1,0:T(8,128)(2,1)S(1)}, bf16[64,2560]{1,0:T(8,128)(2,1)S(1)}, u32[]{:S(2)}, u32[]{:S(2)}) collective-permute-start(bf16[64,2560]{1,0:T(8,128)(2,1)S(1)} %get-tuple-element.120.refs_0_), channel_id=1, source_target_pairs={{0,4},{1,5},{2,6},{3,7},{4,8},{5,9},{6,10},{7,11},{8,12},{9,13},{1... | collective-permute-start | bytes 983048 | tf_op jit(solution)/shard_map/ppermute | solution.py:73
  240.8 27.0 %collective-permute-start.19 = (bf16[64,2560]{1,0:T(8,128)(2,1)S(1)}, bf16[64,2560]{1,0:T(8,128)(2,1)S(1)}, u32[]{:S(2)}, u32[]{:S(2)}) collective-permute-start(bf16[64,2560]{1,0:T(8,128)(2,1)S(1)} %get-tuple-element.120.refs_0_), channel_id=1, source_target_pairs={{0,8},{1,9},{2,10},{3,11},{4,12},{5,13},{6,14},{7,15},{8,0},{9,1},... | collective-permute-start | bytes 983048 | tf_op jit(solution)/shard_map/ppermute | solution.py:73
  247.9 19.9 %collective-permute-start.24 = (bf16[64,2560]{1,0:T(8,128)(2,1)S(1)}, bf16[64,2560]{1,0:T(8,128)(2,1)S(1)}, u32[]{:S(2)}, u32[]{:S(2)}) collective-permute-start(bf16[64,2560]{1,0:T(8,128)(2,1)S(1)} %collective-permute-done.20.refs_3_), channel_id=1, source_target_pairs={{0,2},{1,3},{2,0},{3,1},{4,6},{5,7},{6,4},{7,5},{8,10},{9,11},{10,... | collective-permute-start | bytes 983048 | tf_op jit(solution)/shard_map/ppermute | solution.py:69
  304.6 11.0 %collective-permute-start.28 = (bf16[4,64,2560]{2,1,0:T(8,128)(2,1)}, bf16[4,64,2560]{2,1,0:T(8,128)(2,1)S(1)}, u32[]{:S(2)}, u32[]{:S(2)}) collective-permute-start(bf16[4,64,2560]{2,1,0:T(8,128)(2,1)} %get-tuple-element.128), channel_id=1, source_target_pairs={{0,1},{1,0},{2,3},{3,2},{4,5},{5,4},{6,7},{7,6},{8,9},{9,8},{10,11... | collective-permute-start | bytes 3932168 | tf_op jit(solution)/shard_map/ppermute | solution.py:65
  312.2 15.5 %collective-permute-start.33 = (bf16[64,2560]{1,0:T(8,128)(2,1)S(1)}, bf16[64,2560]{1,0:T(8,128)(2,1)S(1)}, u32[]{:S(2)}, u32[]{:S(2)}) collective-permute-start(bf16[64,2560]{1,0:T(8,128)(2,1)S(1)} %get-tuple-element.133), channel_id=1, source_target_pairs={{0,2},{1,3},{2,0},{3,1},{4,6},{5,7},{6,4},{7,5},{8,10},{9,11},{10,... | collective-permute-start | bytes 983048 | tf_op jit(solution)/shard_map/ppermute | solution.py:69
  313.0 21.5 %collective-permute-start.31 = (bf16[64,2560]{1,0:T(8,128)(2,1)S(1)}, bf16[64,2560]{1,0:T(8,128)(2,1)S(1)}, u32[]{:S(2)}, u32[]{:S(2)}) collective-permute-start(bf16[64,2560]{1,0:T(8,128)(2,1)S(1)} %get-tuple-element.132), channel_id=1, source_target_pairs={{0,2},{1,3},{2,0},{3,1},{4,6},{5,7},{6,4},{7,5},{8,10},{9,11},{10,... | collective-permute-start | bytes 983048 | tf_op jit(solution)/shard_map/ppermute | solution.py:69
  314.7 27.0 %collective-permute-start.30 = (bf16[64,2560]{1,0:T(8,128)(2,1)}, bf16[64,2560]{1,0:T(8,128)(2,1)}, u32[]{:S(2)}, u32[]{:S(2)}) collective-permute-start(bf16[64,2560]{1,0:T(8,128)(2,1)} %get-tuple-element.131), channel_id=1, source_target_pairs={{0,2},{1,3},{2,0},{3,1},{4,6},{5,7},{6,4},{7,5},{8,10},{9,11},{10,... | collective-permute-start | bytes 983048 | tf_op jit(solution)/shard_map/ppermute | solution.py:69
  321.4 20.3 %collective-permute-start.36 = (bf16[64,2560]{1,0:T(8,128)(2,1)}, bf16[64,2560]{1,0:T(8,128)(2,1)}, u32[]{:S(2)}, u32[]{:S(2)}) collective-permute-start(bf16[64,2560]{1,0:T(8,128)(2,1)} %add_near.17), channel_id=1, source_target_pairs={{0,4},{1,5},{2,6},{3,7},{4,8},{5,9},{6,10},{7,11},{8,12},{9,13},{1... | collective-permute-start | bytes 983048 | tf_op jit(solution)/shard_map/ppermute | solution.py:73
  328.5 13.2 %collective-permute-start.34 = (bf16[64,2560]{1,0:T(8,128)(2,1)}, bf16[64,2560]{1,0:T(8,128)(2,1)}, u32[]{:S(2)}, u32[]{:S(2)}) collective-permute-start(bf16[64,2560]{1,0:T(8,128)(2,1)} %add_near.16), channel_id=1, source_target_pairs={{0,12},{1,13},{2,14},{3,15},{4,0},{5,1},{6,2},{7,3},{8,4},{9,5},{1... | collective-permute-start | bytes 983048 | tf_op jit(solution)/shard_map/ppermute | solution.py:73
  335.4 18.3 %collective-permute-start.32 = (bf16[64,2560]{1,0:T(8,128)(2,1)}, bf16[64,2560]{1,0:T(8,128)(2,1)}, u32[]{:S(2)}, u32[]{:S(2)}) collective-permute-start(bf16[64,2560]{1,0:T(8,128)(2,1)} %add_near.15), channel_id=1, source_target_pairs={{0,8},{1,9},{2,10},{3,11},{4,12},{5,13},{6,14},{7,15},{8,0},{9,1},... | collective-permute-start | bytes 983048 | tf_op jit(solution)/shard_map/ppermute | solution.py:73
  361.4 14.8 %collective-permute-start.38 = (bf16[64,2560]{1,0:T(8,128)(2,1)S(1)}, bf16[64,2560]{1,0:T(8,128)(2,1)S(1)}, u32[]{:S(2)}, u32[]{:S(2)}) collective-permute-start(bf16[64,2560]{1,0:T(8,128)(2,1)S(1)} %get-tuple-element.138.refs_0_), channel_id=1, source_target_pairs={{0,4},{1,5},{2,6},{3,7},{4,8},{5,9},{6,10},{7,11},{8,12},{9,13},{1... | collective-permute-start | bytes 983048 | tf_op jit(solution)/shard_map/ppermute | solution.py:73
  361.5 27.9 %collective-permute-start.39 = (bf16[64,2560]{1,0:T(8,128)(2,1)S(1)}, bf16[64,2560]{1,0:T(8,128)(2,1)S(1)}, u32[]{:S(2)}, u32[]{:S(2)}) collective-permute-start(bf16[64,2560]{1,0:T(8,128)(2,1)S(1)} %get-tuple-element.138.refs_0_), channel_id=1, source_target_pairs={{0,8},{1,9},{2,10},{3,11},{4,12},{5,13},{6,14},{7,15},{8,0},{9,1},... | collective-permute-start | bytes 983048 | tf_op jit(solution)/shard_map/ppermute | solution.py:73
  368.3 21.1 %collective-permute-start.44 = (bf16[64,2560]{1,0:T(8,128)(2,1)S(1)}, bf16[64,2560]{1,0:T(8,128)(2,1)S(1)}, u32[]{:S(2)}, u32[]{:S(2)}) collective-permute-start(bf16[64,2560]{1,0:T(8,128)(2,1)S(1)} %collective-permute-done.40.refs_3_), channel_id=1, source_target_pairs={{0,2},{1,3},{2,0},{3,1},{4,6},{5,7},{6,4},{7,5},{8,10},{9,11},{10,... | collective-permute-start | bytes 983048 | tf_op jit(solution)/shard_map/ppermute | solution.py:69
  376.1 13.3 %collective-permute-start.43 = (bf16[64,2560]{1,0:T(8,128)(2,1)S(1)}, bf16[64,2560]{1,0:T(8,128)(2,1)S(1)}, u32[]{:S(2)}, u32[]{:S(2)}) collective-permute-start(bf16[64,2560]{1,0:T(8,128)(2,1)S(1)} %collective-permute-done.38.refs_1_), channel_id=1, source_target_pairs={{0,2},{1,3},{2,0},{3,1},{4,6},{5,7},{6,4},{7,5},{8,10},{9,11},{10,... | collective-permute-start | bytes 983048 | tf_op jit(solution)/shard_map/ppermute | solution.py:69
  389.6 14.5 %collective-permute-start.41 = (bf16[4,64,2560]{2,1,0:T(8,128)(2,1)S(1)}, bf16[4,64,2560]{2,1,0:T(8,128)(2,1)S(1)}, u32[]{:S(2)}, u32[]{:S(2)}) collective-permute-start(bf16[4,64,2560]{2,1,0:T(8,128)(2,1)S(1)} %stack.76.refs_0_), channel_id=1, source_target_pairs={{0,1},{1,0},{2,3},{3,2},{4,5},{5,4},{6,7},{7,6},{8,9},{9,8},{10,11... | collective-permute-start | bytes 3932168 | tf_op jit(solution)/shard_map/ppermute | solution.py:65
  438.1 14.9 %collective-permute-start.52 = (bf16[64,2560]{1,0:T(8,128)(2,1)}, bf16[64,2560]{1,0:T(8,128)(2,1)S(1)}, u32[]{:S(2)}, u32[]{:S(2)}) collective-permute-start(bf16[64,2560]{1,0:T(8,128)(2,1)} %get-tuple-element.151), channel_id=1, source_target_pairs={{0,2},{1,3},{2,0},{3,1},{4,6},{5,7},{6,4},{7,5},{8,10},{9,11},{10,... | collective-permute-start | bytes 983048 | tf_op jit(solution)/shard_map/ppermute | solution.py:69
  438.1 21.9 %collective-permute-start.50 = (bf16[64,2560]{1,0:T(8,128)(2,1)}, bf16[64,2560]{1,0:T(8,128)(2,1)S(1)}, u32[]{:S(2)}, u32[]{:S(2)}) collective-permute-start(bf16[64,2560]{1,0:T(8,128)(2,1)} %get-tuple-element.150), channel_id=1, source_target_pairs={{0,2},{1,3},{2,0},{3,1},{4,6},{5,7},{6,4},{7,5},{8,10},{9,11},{10,... | collective-permute-start | bytes 983048 | tf_op jit(solution)/shard_map/ppermute | solution.py:69
  439.6 27.5 %collective-permute-start.49 = (bf16[64,2560]{1,0:T(8,128)(2,1)}, bf16[64,2560]{1,0:T(8,128)(2,1)S(1)}, u32[]{:S(2)}, u32[]{:S(2)}) collective-permute-start(bf16[64,2560]{1,0:T(8,128)(2,1)} %get-tuple-element.149), channel_id=1, source_target_pairs={{0,2},{1,3},{2,0},{3,1},{4,6},{5,7},{6,4},{7,5},{8,10},{9,11},{10,... | collective-permute-start | bytes 983048 | tf_op jit(solution)/shard_map/ppermute | solution.py:69
  446.1 20.9 %collective-permute-start.55 = (bf16[64,2560]{1,0:T(8,128)(2,1)S(1)}, bf16[64,2560]{1,0:T(8,128)(2,1)S(1)}, u32[]{:S(2)}, u32[]{:S(2)}) collective-permute-start(bf16[64,2560]{1,0:T(8,128)(2,1)S(1)} %add_near.20), channel_id=1, source_target_pairs={{0,4},{1,5},{2,6},{3,7},{4,8},{5,9},{6,10},{7,11},{8,12},{9,13},{1... | collective-permute-start | bytes 983048 | tf_op jit(solution)/shard_map/ppermute | solution.py:73
  453.1 13.9 %collective-permute-start.53 = (bf16[64,2560]{1,0:T(8,128)(2,1)S(1)}, bf16[64,2560]{1,0:T(8,128)(2,1)S(1)}, u32[]{:S(2)}, u32[]{:S(2)}) collective-permute-start(bf16[64,2560]{1,0:T(8,128)(2,1)S(1)} %add_near.19), channel_id=1, source_target_pairs={{0,12},{1,13},{2,14},{3,15},{4,0},{5,1},{6,2},{7,3},{8,4},{9,5},{1... | collective-permute-start | bytes 983048 | tf_op jit(solution)/shard_map/ppermute | solution.py:73
  460.1 15.7 %collective-permute-start.51 = (bf16[64,2560]{1,0:T(8,128)(2,1)S(1)}, bf16[64,2560]{1,0:T(8,128)(2,1)S(1)}, u32[]{:S(2)}, u32[]{:S(2)}) collective-permute-start(bf16[64,2560]{1,0:T(8,128)(2,1)S(1)} %add_near.18), channel_id=1, source_target_pairs={{0,8},{1,9},{2,10},{3,11},{4,12},{5,13},{6,14},{7,15},{8,0},{9,1},... | collective-permute-start | bytes 983048 | tf_op jit(solution)/shard_map/ppermute | solution.py:73
  478.4 17.6 %collective-permute-start.56 = (bf16[64,2560]{1,0:T(8,128)(2,1)S(1)}, bf16[64,2560]{1,0:T(8,128)(2,1)S(1)}, u32[]{:S(2)}, u32[]{:S(2)}) collective-permute-start(bf16[64,2560]{1,0:T(8,128)(2,1)S(1)} %get-tuple-element.154.refs_0_), channel_id=1, source_target_pairs={{0,4},{1,5},{2,6},{3,7},{4,8},{5,9},{6,10},{7,11},{8,12},{9,13},{1... | collective-permute-start | bytes 983048 | tf_op jit(solution)/shard_map/ppermute | solution.py:73
  479.9 27.0 %collective-permute-start.57 = (bf16[64,2560]{1,0:T(8,128)(2,1)S(1)}, bf16[64,2560]{1,0:T(8,128)(2,1)S(1)}, u32[]{:S(2)}, u32[]{:S(2)}) collective-permute-start(bf16[64,2560]{1,0:T(8,128)(2,1)S(1)} %get-tuple-element.154.refs_0_), channel_id=1, source_target_pairs={{0,8},{1,9},{2,10},{3,11},{4,12},{5,13},{6,14},{7,15},{8,0},{9,1},... | collective-permute-start | bytes 983048 | tf_op jit(solution)/shard_map/ppermute | solution.py:73
  486.2 20.8 %collective-permute-start.62 = (bf16[64,2560]{1,0:T(8,128)(2,1)S(1)}, bf16[64,2560]{1,0:T(8,128)(2,1)S(1)}, u32[]{:S(2)}, u32[]{:S(2)}) collective-permute-start(bf16[64,2560]{1,0:T(8,128)(2,1)S(1)} %collective-permute-done.58.refs_3_), channel_id=1, source_target_pairs={{0,2},{1,3},{2,0},{3,1},{4,6},{5,7},{6,4},{7,5},{8,10},{9,11},{10,... | collective-permute-start | bytes 983048 | tf_op jit(solution)/shard_map/ppermute | solution.py:69
  496.1 10.9 %collective-permute-start.61 = (bf16[64,2560]{1,0:T(8,128)(2,1)S(1)}, bf16[64,2560]{1,0:T(8,128)(2,1)S(1)}, u32[]{:S(2)}, u32[]{:S(2)}) collective-permute-start(bf16[64,2560]{1,0:T(8,128)(2,1)S(1)} %collective-permute-done.56.refs_1_), channel_id=1, source_target_pairs={{0,2},{1,3},{2,0},{3,1},{4,6},{5,7},{6,4},{7,5},{8,10},{9,11},{10,... | collective-permute-start | bytes 983048 | tf_op jit(solution)/shard_map/ppermute | solution.py:69
  515.0 85.1 %all-to-all-start.2 = ((bf16[16,160,640]{2,1,0:T(8,128)(2,1)}), bf16[16,160,640]{2,1,0:T(8,128)(2,1)}, u32[]{:S(2)}, u32[]{:S(2)}) async-start(bf16[16,160,640]{2,1,0:T(8,128)(2,1)} %bitcast.41), calls=%async_computation.3 | async-start | bytes 6553600 | tf_op jit(solution)/shard_map/all_to_all | solution.py:81
  527.3 123.5 %reduce-scatter.5.cloned.1.call-start = ((), (), s32[]{:S(2)}) async-start(), calls=%async_computation.7 | async-start | bytes 5898240 | tf_op jit(solution)/shard_map/reduce_scatter | solution.py:215
  560.6 14.9 %collective-permute-start.66 = (bf16[64,2560]{1,0:T(8,128)(2,1)S(1)}, bf16[64,2560]{1,0:T(8,128)(2,1)S(1)}, u32[]{:S(2)}, u32[]{:S(2)}) collective-permute-start(bf16[64,2560]{1,0:T(8,128)(2,1)S(1)} %get-tuple-element.169), channel_id=1, source_target_pairs={{0,2},{1,3},{2,0},{3,1},{4,6},{5,7},{6,4},{7,5},{8,10},{9,11},{10,... | collective-permute-start | bytes 983048 | tf_op jit(solution)/shard_map/ppermute | solution.py:69
  600.5 16.1 %collective-permute-start.70 = (bf16[64,2560]{1,0:T(8,128)(2,1)}, bf16[64,2560]{1,0:T(8,128)(2,1)S(1)}, u32[]{:S(2)}, u32[]{:S(2)}) collective-permute-start(bf16[64,2560]{1,0:T(8,128)(2,1)} %get-tuple-element.168), channel_id=1, source_target_pairs={{0,2},{1,3},{2,0},{3,1},{4,6},{5,7},{6,4},{7,5},{8,10},{9,11},{10,... | collective-permute-start | bytes 983048 | tf_op jit(solution)/shard_map/ppermute | solution.py:69
  601.9 21.7 %collective-permute-start.68 = (bf16[64,2560]{1,0:T(8,128)(2,1)S(1)}, bf16[64,2560]{1,0:T(8,128)(2,1)S(1)}, u32[]{:S(2)}, u32[]{:S(2)}) collective-permute-start(bf16[64,2560]{1,0:T(8,128)(2,1)S(1)} %get-tuple-element.167), channel_id=1, source_target_pairs={{0,2},{1,3},{2,0},{3,1},{4,6},{5,7},{6,4},{7,5},{8,10},{9,11},{10,... | collective-permute-start | bytes 983048 | tf_op jit(solution)/shard_map/ppermute | solution.py:69
  609.7 13.9 %collective-permute-start.73 = (bf16[64,2560]{1,0:T(8,128)(2,1)S(1)}, bf16[64,2560]{1,0:T(8,128)(2,1)S(1)}, u32[]{:S(2)}, u32[]{:S(2)}) collective-permute-start(bf16[64,2560]{1,0:T(8,128)(2,1)S(1)} %add_near.23), channel_id=1, source_target_pairs={{0,4},{1,5},{2,6},{3,7},{4,8},{5,9},{6,10},{7,11},{8,12},{9,13},{1... | collective-permute-start | bytes 983048 | tf_op jit(solution)/shard_map/ppermute | solution.py:73
  616.9 23.3 %collective-permute-start.69 = (bf16[64,2560]{1,0:T(8,128)(2,1)S(1)}, bf16[64,2560]{1,0:T(8,128)(2,1)S(1)}, u32[]{:S(2)}, u32[]{:S(2)}) collective-permute-start(bf16[64,2560]{1,0:T(8,128)(2,1)S(1)} %add_near.21), channel_id=1, source_target_pairs={{0,8},{1,9},{2,10},{3,11},{4,12},{5,13},{6,14},{7,15},{8,0},{9,1},... | collective-permute-start | bytes 983048 | tf_op jit(solution)/shard_map/ppermute | solution.py:73
  650.8 51.1 %all-to-all-start.3 = ((bf16[16,160,384]{2,1,0:T(8,128)(2,1)}), bf16[16,160,384]{2,1,0:T(8,128)(2,1)S(1)}, u32[]{:S(2)}, u32[]{:S(2)}) async-start(bf16[16,160,384]{2,1,0:T(8,128)(2,1)} %bitcast.42), calls=%async_computation.5 | async-start | bytes 3932160 | tf_op jit(solution)/shard_map/all_to_all | solution.py:81
  (134 other events, 935.7 us)
Sparse Core Ops, SparseCore 0:
  73.3 54.7 all-gather.2
  436.3 78.1 reduce-scatter.2
  600.3 50.4 reduce-scatter.4
